TPU v7x, 512 devices: a whole 4x8x8 slice. The times are simulated.
512 devices in a mesh: archive: 64 (over z, x, core), dp: 8 (over y).
Axes of the slice: x: 4, y: 8, z: 8, core: 2. Of those that a mesh axis runs over, the one named last changes fastest.
Arguments:
- query_frames: bfloat16 [4096, 32, 512], P(('archive', 'dp')), may hold values from -7 to 7
- line_frames: bfloat16 [512, 128, 512], P('archive'), may hold values from -7 to 7
- frame_count: int32 [512], replicated, may hold values from 1 to 128, 49152 in all
- line_home: int32 [512], replicated, may hold values from 0 to 511, as said below
- mined: int32 [4096, 6], P(('archive', 'dp')), may hold values from 0 to 511, as said below
- positive: int32 [4096], P(('archive', 'dp')), may hold values from 0 to 5
- w_in: bfloat16 [512, 384], replicated, may hold values from -0.25 to 0.25
- bias_in: float32 [384], replicated, may hold values from -0.5 to 0.5
- w_out: bfloat16 [384, 128], replicated, may hold values from -0.3125 to 0.3125
Outputs:
- query_loss: float32 [4096], P(('archive', 'dp'))
- grad_w_in: float32 [512, 384], replicated
- grad_bias: float32 [384], replicated
- grad_w_out: float32 [384, 128], replicated
Inputs may be any that keep to these rules, and one draw needn't show every extreme that they name: `line_home`: storage row of each line id: each row once. The 48 mined ids of the queries of one device are distinct lines; at most 2 of them lie on one archive shard (shard line_home[id] // 8), and in every draw one shard receives exactly 2 of them from every device. `frame_count`: frame slots at and beyond a row's count are padding.
All inputs are finite; a program needn't handle non-finite values.
Results may differ from a plain program's by a relative error of at most 0.0064.
Values may be sent and summed in bfloat16 or wider, within the bound.
No kernel may reach another device: no remote copies, remote signals or barrier semaphores. Data moves between devices by JAX's collectives and lax.ppermute only.
A program may use at most 64 MiB of HBM per device.

v0:
```python
import math

import jax
import jax.numpy as jnp
from jax import lax
from jax.sharding import PartitionSpec as P

LOSS_SCALE = 4096.0
SCORE_SCALE = 4.0


def head_forward(frames, w_in, bias_in, w_out):
    pre_act = jnp.dot(frames, w_in, preferred_element_type=jnp.float32) + bias_in
    hidden = jax.nn.gelu(pre_act).astype(jnp.bfloat16)
    vectors = jnp.dot(hidden, w_out, preferred_element_type=jnp.float32).astype(jnp.bfloat16)
    return (pre_act, hidden, vectors)


def head_backward(frames, pre_act, hidden, grad_vec, w_out):
    highest = lax.Precision.HIGHEST
    grad_w_out = jnp.dot(hidden.astype(jnp.float32).T, grad_vec, precision=highest)
    grad_hidden = jnp.dot(grad_vec, w_out.astype(jnp.float32).T, precision=highest)
    _, pullback = jax.vjp(jax.nn.gelu, pre_act)
    grad_pre = pullback(grad_hidden)[0]
    grad_bias = jnp.sum(grad_pre, axis=0)
    grad_w_in = jnp.dot(frames.astype(jnp.float32).T, grad_pre, precision=highest)
    return (grad_w_in, grad_bias, grad_w_out)


def match_forward(query_vec, line_vec, counts):
    vec_width = query_vec.shape[-1]
    slot_total = line_vec.shape[1]
    logits = jnp.einsum("nid,nfd->nif", query_vec, line_vec, preferred_element_type=jnp.float32)
    logits = logits * (SCORE_SCALE / math.sqrt(vec_width))
    usable = jnp.arange(slot_total, dtype=jnp.int32)[None, None, :] < counts[:, None, None]
    logits = jnp.where(usable, logits, -jnp.inf)
    peak = jnp.max(logits, axis=-1, keepdims=True)
    scaled = jnp.exp(logits - peak)
    totals = jnp.sum(scaled, axis=-1, keepdims=True)
    log_total = peak[..., 0] + jnp.log(totals[..., 0])
    return (jnp.mean(log_total, axis=-1), scaled / totals)


def match_backward(weights, grad_match, query_vec, line_vec):
    query_len = query_vec.shape[1]
    vec_width = query_vec.shape[2]
    factor = grad_match * (SCORE_SCALE / (math.sqrt(vec_width) * query_len))
    score_grad = (weights * factor[:, None, None]).astype(jnp.bfloat16)
    grad_query = jnp.einsum(
        "nif,nfd->nid", score_grad, line_vec, preferred_element_type=jnp.float32
    )
    grad_line = jnp.einsum(
        "nif,nid->nfd", score_grad, query_vec, preferred_element_type=jnp.float32
    )
    return (grad_query, grad_line)


def cross_entropy(matches, positives, scale):
    peak = jnp.max(matches, axis=1, keepdims=True)
    log_total = peak[:, 0] + jnp.log(jnp.sum(jnp.exp(matches - peak), axis=1))
    picked = jnp.arange(matches.shape[1], dtype=jnp.int32)[None, :] == positives[:, None]
    chosen = jnp.sum(jnp.where(picked, matches, 0.0), axis=1)
    grads = (jnp.exp(matches - log_total[:, None]) - picked.astype(jnp.float32)) * scale
    return (log_total - chosen, grads)


def local(query_frames, line_frames, frame_count, line_home, mined, positive, w_in, bias_in, w_out):
    query_count, query_len, feat_width = query_frames.shape
    line_count, line_len, _ = line_frames.shape
    vec_width = w_out.shape[1]
    mined_count = mined.shape[1]
    owner_count = lax.axis_size("archive")
    capacity = max(2, (query_count * mined_count + owner_count - 1) // owner_count + 1)
    slot_count = owner_count * capacity
    request_count = query_count * mined_count
    loss_factor = LOSS_SCALE / (query_count * owner_count * lax.axis_size("dp"))
    query_flat = query_frames.reshape(query_count * query_len, feat_width)
    query_pre, query_hidden, query_vec = head_forward(query_flat, w_in, bias_in, w_out)
    query_vec = query_vec.reshape(query_count, query_len, vec_width)
    line_flat = line_frames.reshape(line_count * line_len, feat_width)
    line_pre, line_hidden, line_vec = head_forward(line_flat, w_in, bias_in, w_out)
    line_vec = line_vec.reshape(line_count, line_len, vec_width)
    request_rows = line_home[mined.reshape(-1)]
    request_owner = request_rows // line_count
    request_local = request_rows % line_count
    request_frames = frame_count[request_rows]
    request_ids = jnp.arange(request_count, dtype=jnp.int32)
    same_owner = (request_owner[:, None] == request_owner[None, :]) & (
        request_ids[None, :] < request_ids[:, None]
    )
    request_rank = jnp.sum(same_owner.astype(jnp.int32), axis=1)
    request_slot = request_owner * capacity + request_rank
    slot_hits = request_slot[None, :] == jnp.arange(slot_count, dtype=jnp.int32)[:, None]
    slot_used = jnp.any(slot_hits, axis=1)
    slot_request = jnp.sum(jnp.where(slot_hits, request_ids[None, :], 0), axis=1)
    send_local = jnp.where(slot_used, request_local[slot_request], -1).reshape(
        owner_count, capacity
    )
    got_local = lax.all_to_all(
        send_local, "archive", split_axis=0, concat_axis=0, tiled=True
    ).reshape(-1)
    got_used = got_local >= 0
    got_row = jnp.maximum(got_local, 0)
    line_onehot = (
        (got_row[None, :] == jnp.arange(line_count, dtype=jnp.int32)[:, None]) & got_used[None, :]
    ).astype(jnp.float32)
    got_lines = line_vec[got_row]
    sent_lines = got_lines.reshape(owner_count, capacity, line_len, vec_width)
    fetched = lax.all_to_all(
        sent_lines, "archive", split_axis=0, concat_axis=0, tiled=True
    ).reshape(slot_count, line_len, vec_width)
    request_lines = fetched[request_slot]
    repeated = jnp.broadcast_to(
        query_vec[:, None], (query_count, mined_count, query_len, vec_width)
    ).reshape(request_count, query_len, vec_width)
    matches, weights = match_forward(repeated, request_lines, request_frames)
    query_loss, grad_match = cross_entropy(
        matches.reshape(query_count, mined_count), positive, loss_factor
    )
    grad_query, grad_line = match_backward(weights, grad_match.reshape(-1), repeated, request_lines)
    grad_query = jnp.sum(grad_query.reshape(query_count, mined_count, query_len, vec_width), axis=1)
    slot_grads = jnp.where(slot_used[:, None, None], grad_line[slot_request], 0.0).reshape(
        owner_count, capacity, line_len, vec_width
    )
    got_grads = lax.all_to_all(
        slot_grads, "archive", split_axis=0, concat_axis=0, tiled=True
    ).reshape(slot_count, line_len * vec_width)
    grad_lines = jnp.dot(
        line_onehot, got_grads, precision=lax.Precision.HIGHEST, preferred_element_type=jnp.float32
    )
    grad_lines = grad_lines.reshape(line_count * line_len, vec_width)
    query_terms = head_backward(
        query_flat,
        query_pre,
        query_hidden,
        grad_query.reshape(query_count * query_len, vec_width),
        w_out,
    )
    line_terms = head_backward(line_flat, line_pre, line_hidden, grad_lines, w_out)
    grad_w_in, grad_bias, grad_w_out = lax.psum(
        (
            query_terms[0] + line_terms[0],
            query_terms[1] + line_terms[1],
            query_terms[2] + line_terms[2],
        ),
        ("archive", "dp"),
    )
    return (query_loss, grad_w_in, grad_bias, grad_w_out)


def solution(mesh):
    placed = (
        P(("archive", "dp"), None, None),
        P("archive", None, None),
        P(),
        P(),
        P(("archive", "dp"), None),
        P(("archive", "dp")),
        P(),
        P(),
        P(),
    )
    return jax.shard_map(
        local,
        mesh=mesh,
        in_specs=placed,
        out_specs=(P(("archive", "dp")), P(), P(), P()),
        check_vma=False,
    )
```

profile of v0, /device:TPU:1, one launch (start us, length us, event | category | flops | bytes accessed | tf_op | source)
XLA Modules:
  0.0 654.7 jit_solution(12338602011563378123)
XLA Ops:
  8.1 1.5 gather_fusion
  9.9 1.2 gather_fusion.2
  11.9 14.8 %all-to-all-start = ((s32[64,1,2]{2,1,0:T(1,128)}), s32[64,1,2]{2,1,0:T(1,128)S(1)}, u32[]{:S(2)}, u32[]{:S(2)}) async-start(s32[64,1,2]{2,1,0:T(1,128)} %bitcast.10), calls=%async_computation | async-start | bytes 65536 | tf_op jit(solution)/shard_map/all_to_all | solution.py:99
  26.8 3.2 multiply_convert_fusion
  31.2 4.8 all-to-all-done
  36.3 3.1 gather_fusion.3
  39.4 5.8 all-to-all-start.1
  47.8 92.1 %all-to-all-done.1 = bf16[64,2,128,128]{3,2,1,0:T(8,128)(2,1)} async-done(((bf16[64,2,128,128]{3,2,1,0:T(8,128)(2,1)}), bf16[64,2,128,128]{3,2,1,0:T(8,128)(2,1)}, u32[]{:S(2)}, u32[]{:S(2)}) %all-to-all-start.1) | async-done | bytes 4194336 | tf_op jit(solution)/shard_map/all_to_all | solution.py:109
  139.9 3.0 gather_fusion.4
  145.8 4.2 fusion.29
  150.1 6.2 gather_fusion.5
  156.3 7.2 %broadcast_select_fusion = f32[64,2,128,128]{3,2,1,0:T(8,128)} fusion(f32[64,2,128,128]{3,2,1,0:T(8,128)} %bitcast.68, pred[64,2]{1,0:T(8,128)(4,1)S(1)} %broadcast_in_dim.54), kind=kLoop, calls=%fused_computation.9 | loop fusion | flops 2097152 | bytes 16777344 | tf_op jit(solution)/shard_map/jit(_where)/select_n | solution.py:122
  163.5 7.3 %all-to-all-start.2 = ((f32[64,2,128,128]{3,2,1,0:T(8,128)}), f32[64,2,128,128]{3,2,1,0:T(8,128)}, u32[]{:S(2)}, u32[]{:S(2)}) async-start(f32[64,2,128,128]{3,2,1,0:T(8,128)} %broadcast_select_fusion), calls=%async_computation.2 | async-start | bytes 16777216 | tf_op jit(solution)/shard_map/all_to_all | solution.py:125
  171.3 1.5 fusion.30
  172.8 1.2 reduce_sum.93
  174.0 2.3 fusion.33
  176.3 177.4 %all-to-all-done.2 = f32[64,2,128,128]{3,2,1,0:T(8,128)} async-done(((f32[64,2,128,128]{3,2,1,0:T(8,128)}), f32[64,2,128,128]{3,2,1,0:T(8,128)}, u32[]{:S(2)}, u32[]{:S(2)}) %all-to-all-start.2) | async-done | bytes 8388640 | tf_op jit(solution)/shard_map/all_to_all | solution.py:125
  353.7 10.6 %fusion = f32[8,16384]{1,0:T(8,128)S(1)} fusion(f32[16,8,128,128]{3,2,1,0:T(8,128)} %bitcast.20, s32[128]{0:T(128)S(1)} %reshape.347, pred[128]{0:T(512)(128)(4,1)S(1)} %ge.11), kind=kOutput, calls=%fused_computation.6 | convolution fusion | flops 201328640 | bytes 8913536 | tf_op jit(solution)/shard_map/dot_general | solution.py:128
  366.6 1.7 fusion.34
  368.3 1.4 fusion.35
  369.7 1.4 fusion.9
  371.2 101.0 %psum.22 = f32[384]{0:T(512)} all-reduce(f32[384]{0:T(512)S(1)} %add.168), channel_id=1, replica_groups=mesh['archive'=64,'dp'=8] {'archive','dp'}, use_global_device_ids=true, to_apply=%region_13.14 | all-reduce | flops 384 | bytes 3072 | tf_op jit(solution)/shard_map/psum | solution.py:140
  472.2 172.7 %all-reduce.3.cloned.1.call-done = (f32[512,384]{0,1:T(8,128)}, f32[384,128]{1,0:T(8,128)}) async-done(((f32[512,384]{0,1:T(8,128)}, f32[384,128]{1,0:T(8,128)}), (f32[512,384]{0,1:T(8,128)}, f32[384,128]{1,0:T(8,128)})) %all-reduce.3.cloned.1.call-update) | async-done | bytes 983056 | tf_op jit(solution)/shard_map/psum | solution.py:140
  644.9 2.3 copy.18
  (81 shorter events, 12.2 us)
Async XLA Ops:
  7.2 19.6 %copy-start = (bf16[8,128,512]{2,1,0:T(8,128)(2,1)S(1)}, bf16[8,128,512]{2,1,0:T(8,128)(2,1)}, u32[]{:S(2)}) copy-start(bf16[8,128,512]{2,1,0:T(8,128)(2,1)} %param.10) | copy-start | bytes 3145732
  11.9 24.1 %all-to-all-start = ((s32[64,1,2]{2,1,0:T(1,128)}), s32[64,1,2]{2,1,0:T(1,128)S(1)}, u32[]{:S(2)}, u32[]{:S(2)}) async-start(s32[64,1,2]{2,1,0:T(1,128)} %bitcast.10), calls=%async_computation | async-start | bytes 65536 | tf_op jit(solution)/shard_map/all_to_all | solution.py:99
  26.8 4.1 copy-start.12
  30.0 0.9 copy-start.3
  39.4 6.0 copy-start.15
  39.4 6.2 copy-start.1
  39.4 7.1 %copy-start.5 = (bf16[8,32,512]{2,1,0:T(8,128)(2,1)S(1)}, bf16[8,32,512]{2,1,0:T(8,128)(2,1)}, u32[]{:S(2)}) copy-start(bf16[8,32,512]{2,1,0:T(8,128)(2,1)} %param.9) | copy-start | bytes 786436
  39.4 7.1 %copy-start.7 = (bf16[512,384]{1,0:T(8,128)(2,1)S(1)}, bf16[512,384]{1,0:T(8,128)(2,1)}, u32[]{:S(2)}) copy-start(bf16[512,384]{1,0:T(8,128)(2,1)} %param.15) | copy-start | bytes 1179652
  39.4 7.1 %copy-start.14 = (f32[384]{0:T(512)S(1)}, f32[384]{0:T(512)}, u32[]{:S(2)}) copy-start(f32[384]{0:T(512)} %param.16) | copy-start | bytes 4612
  39.4 100.5 %all-to-all-start.1 = ((bf16[64,2,128,128]{3,2,1,0:T(8,128)(2,1)}), bf16[64,2,128,128]{3,2,1,0:T(8,128)(2,1)}, u32[]{:S(2)}, u32[]{:S(2)}) async-start(bf16[64,2,128,128]{3,2,1,0:T(8,128)(2,1)} %bitcast.69), calls=%async_computation.1 | async-start | bytes 8388608 | tf_op jit(solution)/shard_map/all_to_all | solution.py:109
  46.8 0.7 copy-start.8
  143.0 1.5 copy-start.2
  163.5 190.2 %all-to-all-start.2 = ((f32[64,2,128,128]{3,2,1,0:T(8,128)}), f32[64,2,128,128]{3,2,1,0:T(8,128)}, u32[]{:S(2)}, u32[]{:S(2)}) async-start(f32[64,2,128,128]{3,2,1,0:T(8,128)} %broadcast_select_fusion), calls=%async_computation.2 | async-start | bytes 16777216 | tf_op jit(solution)/shard_map/all_to_all | solution.py:125
  170.8 474.1 %all-reduce.3.cloned.1.call-start = ((), (), s32[]{:S(2)}) async-start(), calls=%async_computation.3 | async-start | bytes 1966080 | tf_op jit(solution)/shard_map/psum | solution.py:140
  353.7 10.7 %copy-start.4 = (bf16[1024,384]{1,0:T(8,128)(2,1)S(1)}, bf16[1024,384]{1,0:T(8,128)(2,1)}, u32[]{:S(2)}) copy-start(bf16[1024,384]{1,0:T(8,128)(2,1)} %copy-done.3) | copy-start | bytes 2359300
  364.3 1.1 copy-start.9
  364.4 2.1 copy-start.13
  364.4 2.1 copy-start.16
  368.3 1.5 copy-start.6
  368.3 1.5 copy-start.10
  644.9 2.3 copy-start.11
Sparse Core Ops, SparseCore 0:
  371.3 273.5 all-reduce.2
where the time goes:
time: 657 us; the launch traced here: 655 us
  waiting for transfers between devices  447 us (68%)
  blocking collectives  101 us (15%)
  matrix products  30.4 us (5%)
  starting transfers between devices  28.2 us (4%)
  local copies, waits for them, and re-layouts  23 us (4%)
  between operations  14.4 us (2%)
  other arithmetic  10.7 us (2%)
    all_to_all x1, waiting for transfers between devices, local(): lax.all_to_all(slot_grads, 'archive', split_axis=0, concat_axis=0, tiled=...  177 us
    psum x1, waiting for transfers between devices, local(): lax.psum((query_terms[0] + line_terms[0], query_terms[1] + line_terms[1],...  173 us
    psum x1, blocking collectives, local(): lax.psum((query_terms[0] + line_terms[0], query_terms[1] + line_terms[1],...  101 us
    all_to_all x1, waiting for transfers between devices, local(): lax.all_to_all(sent_lines, 'archive', split_axis=0, concat_axis=0, tiled=...  92.1 us
    all_to_all x1, starting transfers between devices, local(): lax.all_to_all(send_local, 'archive', split_axis=0, concat_axis=0, tiled=...  14.8 us
  transfers between devices with their start and end apart: 4, of which 4 were waited for; matrix products, arithmetic and copies ran while one was open for 2% of the time, Pallas kernels for 0%

commit v1 on v0

v1 whole, which is shorter than its diff:
```python
import math

import jax
import jax.numpy as jnp
from jax import lax
from jax.experimental import pallas as pl
from jax.experimental.pallas import tpu as pltpu
from jax.sharding import PartitionSpec as P

LOSS_SCALE = 4096.0
SCORE_SCALE = 4.0
LANES = 128
CAP = 2
HALF = LANES // CAP
META = 8
UNUSED = 100.0
FLOOR = -1e30
GELU_A = math.sqrt(2.0 / math.pi)
GELU_B = 0.044715
GROUP = 4

f32 = jnp.float32
bf16 = jnp.bfloat16


def dot(a, b, ca=1, cb=0):
    return lax.dot_general(a, b, (((ca,), (cb,)), ((), ())), preferred_element_type=f32)


def split2(x):
    hi = x.astype(bf16)
    return hi, (x - hi.astype(f32)).astype(bf16)


def call(body, outs, args, smem_count, scratch=(), flops=0, transcendentals=0):
    nbytes = sum(a.size * a.dtype.itemsize for a in list(args) + list(outs))
    vmem = pl.BlockSpec(memory_space=pltpu.VMEM)
    smem = pl.BlockSpec(memory_space=pltpu.SMEM)
    return pl.pallas_call(
        body,
        out_shape=tuple(outs),
        in_specs=[smem] * smem_count + [vmem] * (len(args) - smem_count),
        out_specs=tuple(vmem for _ in outs),
        scratch_shapes=list(scratch),
        compiler_params=pltpu.CompilerParams(vmem_limit_bytes=40 << 20),
        cost_estimate=pl.CostEstimate(
            flops=flops, bytes_accessed=nbytes, transcendentals=transcendentals
        ),
    )(*args)


def gelu_parts(pre):
    t = jnp.tanh(GELU_A * (pre + GELU_B * pre * pre * pre))
    return t, (0.5 * pre * (1.0 + t)).astype(bf16)


def ask_kernel(mined, home, positive, x, w_in, bias, w_out, send, vec, rid, code, count):
    query_count, mined_count = mined.shape
    owner_count = send.shape[0]
    query_len = x.shape[0] // query_count
    line_count = home.shape[0] // owner_count
    rows = CAP * query_len
    _, hidden = gelu_parts(dot(x[...], w_in[...]) + bias[...])
    vec[...] = dot(hidden, w_out[...]).astype(bf16)
    send[...] = jnp.zeros(send.shape, bf16)

    def clear(owner, carry):
        count[owner] = 0
        for c in range(CAP):
            rid[c, owner] = int(UNUSED)
            code[c, owner] = int(UNUSED)
        return carry

    lax.fori_loop(0, owner_count, clear, 0)

    def place(query, carry):
        block = vec[pl.ds(pl.multiple_of(query * query_len, query_len), query_len), :]
        for j in range(mined_count):
            row = home[mined[query, j]]
            owner = row // line_count
            rank = count[owner]
            count[owner] = rank + 1
            rid[rank, owner] = row - owner * line_count
            code[rank, owner] = query + jnp.where(positive[query] == j, 8, 0)
            send[owner, pl.ds(pl.multiple_of(rank * query_len, query_len), query_len), :] = block
        return carry

    lax.fori_loop(0, query_count, place, 0)
    sub = lax.broadcasted_iota(jnp.int32, (META, LANES), 0)

    def label(owner, carry):
        tile = jnp.where(
            sub == 0,
            rid[0, owner],
            jnp.where(sub == 1, rid[1, owner], jnp.where(sub == 2, code[0, owner], code[1, owner])),
        )
        send[owner, rows : rows + META, :] = tile.astype(f32).astype(bf16)
        return carry

    lax.fori_loop(0, owner_count, label, 0)


def head_kernel(xl, xq, w_in, bias, w_out, line_vec, hidden_all, slope_t):
    step = 256
    line_frames = xl.shape[0]
    for first in range(0, line_frames + xq.shape[0], step):
        if first < line_frames:
            x = xl[first : first + step, :]
        else:
            x = xq[first - line_frames : first - line_frames + step, :]
        size = x.shape[0]
        pre = dot(x, w_in[...]) + bias[...]
        t, hidden = gelu_parts(pre)
        slope = 0.5 * (1.0 + t) + 0.5 * pre * (1.0 - t * t) * GELU_A * (
            1.0 + 3.0 * GELU_B * pre * pre
        )
        hidden_all[first : first + size, :] = hidden
        slope_t[:, first : first + size] = slope.T
        if first < line_frames:
            line_vec[first : first + size, :] = dot(hidden, w_out[...]).astype(bf16)


def spread(meta, first, query_len):
    parts = []
    for b in range(meta.shape[0]):
        for c in range(CAP):
            parts.append(jnp.broadcast_to(meta[b, first + c : first + c + 1, :], (query_len, LANES)))
    return jnp.concatenate(parts, axis=0)


def match_kernel(place, counts, got, line_vec, send, weights, own):
    owner_count = got.shape[0]
    rows = got.shape[1] - META
    query_len = rows // CAP
    line_total = line_vec.shape[0]
    line_count = line_total // LANES
    scale = SCORE_SCALE / math.sqrt(line_vec.shape[1])
    lines = line_vec[...]
    lane1 = lax.broadcasted_iota(jnp.int32, (1, LANES), 1)
    pads = [
        jnp.where(lane1 < counts[place[0] * line_count + r], 0.0, FLOOR) for r in range(line_count)
    ]
    total = GROUP * rows
    lane = lax.broadcasted_iota(jnp.int32, (total, LANES), 1)
    row = lax.broadcasted_iota(jnp.int32, (total, LANES), 0)
    target = row // rows + HALF * ((row // query_len) % CAP)

    def step(g, carry):
        match_row, code_row = carry
        first = g * GROUP
        queries = got[pl.ds(first, GROUP), 0:rows, :].reshape(total, LANES)
        meta = got[pl.ds(first, GROUP), rows : rows + META, :].astype(f32)
        rid = spread(meta, 0, query_len)
        logits = dot(queries, lines, 1, 1) * scale
        chosen = jnp.zeros((total, LANES), f32)
        for r in range(line_count):
            part = logits[:, r * LANES : (r + 1) * LANES] + pads[r]
            chosen = jnp.where(rid == r, part, chosen)
        peak = jnp.max(chosen, axis=1, keepdims=True)
        scaled = jnp.exp(chosen - peak)
        totals = jnp.sum(scaled, axis=1, keepdims=True)
        log_total = peak + jnp.log(totals)
        weight = (scaled * (1.0 / totals)).astype(bf16)
        weights[pl.ds(first, GROUP)] = weight.reshape(GROUP, rows, LANES)
        rid_b = rid.astype(bf16)
        zero = jnp.zeros((total, LANES), bf16)
        wide = jnp.concatenate(
            [jnp.where(rid_b == r, weight, zero) for r in range(line_count)], axis=1
        )
        send[pl.ds(first, GROUP), 0:rows, :] = (
            dot(wide, lines).astype(bf16).reshape(GROUP, rows, LANES)
        )
        mine = (lane == target + first) & (rid < line_count)
        match_row += jnp.sum(
            jnp.where(mine, log_total * (1.0 / query_len), 0.0), axis=0, keepdims=True
        )
        for b in range(GROUP):
            for c in range(CAP):
                code_row = jnp.where(
                    lane1 == first + b + HALF * c, meta[b, 2 + c : 3 + c, :], code_row
                )
        return match_row, code_row

    match_row, code_row = lax.fori_loop(
        0,
        owner_count // GROUP,
        step,
        (jnp.zeros((1, LANES), f32), jnp.full((1, LANES), UNUSED, f32)),
    )
    sub = lax.broadcasted_iota(jnp.int32, (META, LANES), 0)
    own[...] = jnp.where(sub == 0, match_row, code_row)
    high = match_row.astype(bf16).astype(f32)
    middle = (match_row - high).astype(bf16).astype(f32)
    low = match_row - high - middle
    tile = jnp.where(
        sub == 0, high, jnp.where(sub == 1, middle, jnp.where(sub == 2, low, code_row))
    ).astype(bf16)

    def label(b, carry):
        send[b, rows : rows + META, :] = tile
        return carry

    lax.fori_loop(0, owner_count, label, 0)


def grad_kernel(
    place, back, got, weights, own, xl, xq, hidden_all, slope_t, w_out, loss, grads, own_scale, ask_scale, line_acc, query_acc, *, loss_factor
):
    owner_count = got.shape[0]
    rows = got.shape[1] - META
    query_len = rows // CAP
    line_total = xl.shape[0]
    line_count = line_total // LANES
    query_frames = xq.shape[0]
    vec_width = w_out.shape[1]
    hid = w_out.shape[0]
    me = place[0]

    shape3 = (owner_count, META, LANES)
    lane3 = lax.broadcasted_iota(jnp.int32, shape3, 2)
    sub3 = lax.broadcasted_iota(jnp.int32, shape3, 1)
    owner3 = lax.broadcasted_iota(jnp.int32, shape3, 0)
    subf = sub3.astype(f32)
    meta = back[:, rows : rows + META, :].astype(f32)
    match = jnp.sum(jnp.where(sub3 < 3, meta, 0.0), axis=1, keepdims=True)
    code = jnp.sum(jnp.where(sub3 == 3, meta, 0.0), axis=1, keepdims=True)
    match = jnp.broadcast_to(match, shape3)
    code = jnp.broadcast_to(code, shape3)
    is_pos = (code >= 8.0) & (code < 16.0)
    query_of = jnp.where(is_pos, code - 8.0, code)
    here = query_of == subf
    peak = jnp.max(jnp.where(here, match, FLOOR), axis=0)
    peak = jnp.maximum(peak, pltpu.roll(peak, HALF, 1))
    total = jnp.sum(jnp.where(here, jnp.exp(match - peak[None]), 0.0), axis=0)
    total = total + pltpu.roll(total, HALF, 1)
    chosen = jnp.sum(jnp.where(here & is_pos, match, 0.0), axis=0)
    chosen = chosen + pltpu.roll(chosen, HALF, 1)
    log_total = peak + jnp.log(jnp.where(total > 0.0, total, 1.0))
    lane2 = lax.broadcasted_iota(jnp.int32, (META, LANES), 1)
    sub2 = lax.broadcasted_iota(jnp.int32, (META, LANES), 0).astype(f32)
    picked = jnp.sum(jnp.where(lane2 == me, log_total - chosen, 0.0), axis=1, keepdims=True)
    loss[...] = jnp.broadcast_to(picked, (META, LANES))

    factor = loss_factor * SCORE_SCALE / (math.sqrt(vec_width) * query_len)

    own_match = own[0:1, :]
    own_code = own[1:2, :]
    own_pos = (own_code >= 8.0) & (own_code < 16.0)
    own_query = jnp.where(own_pos, own_code - 8.0, own_code)
    own_grad = jnp.exp(jnp.minimum(own_match - log_total, 0.0)) - jnp.where(own_pos, 1.0, 0.0)
    own_grad = factor * jnp.sum(jnp.where(own_query == sub2, own_grad, 0.0), axis=0, keepdims=True)
    aim = lane3 == owner3 + HALF * sub3
    own_scale[...] = jnp.broadcast_to(
        jnp.sum(
            jnp.where(aim, jnp.broadcast_to(own_grad[None], shape3), 0.0), axis=2, keepdims=True
        ),
        shape3,
    )

    ask_grad = jnp.exp(jnp.minimum(match - log_total[None], 0.0)) - jnp.where(is_pos, 1.0, 0.0)
    ask_grad = factor * jnp.sum(jnp.where(here, ask_grad, 0.0), axis=1, keepdims=True)
    both = jnp.where(sub3 < CAP, jnp.broadcast_to(ask_grad, shape3), query_of)
    aim = lane3 == me + HALF * (sub3 % CAP)
    ask_scale[...] = jnp.broadcast_to(
        jnp.sum(jnp.where(aim, both, 0.0), axis=2, keepdims=True), shape3
    )

    size = GROUP * rows
    line_acc[...] = jnp.zeros(line_acc.shape, f32)
    query_acc[...] = jnp.zeros(query_acc.shape, f32)
    frame = (lax.broadcasted_iota(jnp.int32, (size, LANES), 0) % query_len).astype(f32)
    lane = lax.broadcasted_iota(jnp.int32, (size, LANES), 1).astype(f32)
    zero = jnp.zeros((size, LANES), bf16)
    one = jnp.ones((size, LANES), bf16)

    def step(g, carry):
        first = g * GROUP
        queries = got[pl.ds(first, GROUP), 0:rows, :].reshape(size, LANES)
        rid = spread(got[pl.ds(first, GROUP), rows : rows + META, :].astype(f32), 0, query_len)
        rid = rid.astype(bf16)
        scale = spread(own_scale[pl.ds(first, GROUP)], 0, query_len)
        weight = weights[pl.ds(first, GROUP)].reshape(size, LANES).astype(f32)
        score = (weight * scale).astype(bf16)
        wide = jnp.concatenate(
            [jnp.where(rid == r, score, zero) for r in range(line_count)], axis=1
        )
        line_acc[...] += dot(queries, wide, 0, 0)

        labels = ask_scale[pl.ds(first, GROUP)]
        scale = spread(labels, 0, query_len)
        target = spread(labels, CAP, query_len) * float(query_len) + frame
        pulled = back[pl.ds(first, GROUP), 0:rows, :].reshape(size, LANES).astype(f32)
        pulled = (pulled * scale).astype(bf16)
        wide = jnp.concatenate(
            [
                jnp.where(target == lane + float(k), one, zero)
                for k in range(0, query_acc.shape[1], LANES)
            ],
            axis=1,
        )
        query_acc[...] += dot(pulled, wide, 0, 0)
        return carry

    lax.fori_loop(0, owner_count // GROUP, step, 0)

    grad_in = None
    grad_out = None
    grad_bias = None
    ones = jnp.ones((META, 1), bf16)
    spans = ((line_acc, xl, 0, line_total), (query_acc, xq, line_total, query_frames))
    for acc, x, first, span in spans:
        g_hi, g_lo = split2(acc[:, 0:span])
        grad_hidden = dot(w_out[...], g_hi) + dot(w_out[...], g_lo)
        p_hi, p_lo = split2(grad_hidden * slope_t[:, first : first + span])
        hidden = hidden_all[first : first + span, :]
        ones = jnp.ones((META, span), bf16)
        part_in = dot(p_hi, x[...]) + dot(p_lo, x[...])
        part_out = dot(g_hi, hidden) + dot(g_lo, hidden)
        part_bias = dot(ones, p_hi, 1, 1) + dot(ones, p_lo, 1, 1)
        grad_in = part_in if grad_in is None else grad_in + part_in
        grad_out = part_out if grad_out is None else grad_out + part_out
        grad_bias = part_bias if grad_bias is None else grad_bias + part_bias
    base = 0
    for k in range(0, x.shape[1], LANES):
        grads[base : base + hid, :] = grad_in[:, k : k + LANES].astype(bf16)
        base += hid
    for k in range(0, hid, LANES):
        grads[base : base + vec_width, :] = grad_out[:, k : k + LANES].astype(bf16)
        base += vec_width
    rest = grads.shape[0] - base
    sub = lax.broadcasted_iota(jnp.int32, (rest, LANES), 0)
    tile = jnp.zeros((rest, LANES), f32)
    for i, k in enumerate(range(0, hid, LANES)):
        tile = jnp.where(sub == i, grad_bias[0:1, k : k + LANES], tile)
    grads[base:, :] = tile.astype(bf16)


def sum_archive_kernel(got, send):
    part = got[0].astype(f32)
    for k in range(1, got.shape[0]):
        part = part + got[k].astype(f32)
    for k in range(send.shape[0]):
        send[k] = part


def sum_dp_kernel(got, send):
    part = got[0]
    for k in range(1, got.shape[0]):
        part = part + got[k]
    part = part.astype(bf16)
    for k in range(send.shape[0]):
        send[k] = part


def unpack_kernel(got, grad_in, grad_bias, grad_out):
    feat, hid = grad_in.shape
    vec_width = grad_out.shape[1]
    base = 0
    for k in range(0, feat, LANES):
        grad_in[k : k + LANES, :] = got[base : base + hid, :].astype(f32).T
        base += hid
    for k in range(0, hid, LANES):
        grad_out[k : k + LANES, :] = got[base : base + vec_width, :].astype(f32).T
        base += vec_width
    tail = got[base : base + 16, :].astype(f32)
    for i, k in enumerate(range(0, hid, LANES)):
        grad_bias[0:1, k : k + LANES] = tail[i : i + 1, :]


def exchange(x, axis):
    return lax.all_to_all(x, axis, split_axis=0, concat_axis=0, tiled=True)


def shape_of(shape, dtype):
    return jax.ShapeDtypeStruct(shape, dtype)


def local(query_frames, line_frames, frame_count, line_home, mined, positive, w_in, bias_in, w_out):
    query_count, query_len, feat = query_frames.shape
    line_count, line_len, _ = line_frames.shape
    hid, vec_width = w_out.shape
    owner_count = lax.axis_size("archive")
    dp_count = lax.axis_size("dp")
    loss_factor = LOSS_SCALE / (query_count * owner_count * dp_count)
    frames_q = query_count * query_len
    frames_l = line_count * line_len
    frames = frames_q + frames_l
    rows = CAP * query_len
    xq = query_frames.reshape(frames_q, feat)
    xl = line_frames.reshape(frames_l, feat)
    bias = bias_in.reshape(1, hid)
    place = lax.axis_index("archive").astype(jnp.int32).reshape(1)
    wire = shape_of((owner_count, rows + META, vec_width), bf16)
    head_flops = 2 * hid * (feat + vec_width)

    (asked,) = call(
        ask_kernel,
        [wire],
        [mined, line_home, positive, xq, w_in, bias, w_out],
        3,
        [
            pltpu.VMEM((frames_q, vec_width), bf16),
            pltpu.SMEM((CAP, owner_count), jnp.int32),
            pltpu.SMEM((CAP, owner_count), jnp.int32),
            pltpu.SMEM((owner_count,), jnp.int32),
        ],
        flops=frames_q * head_flops,
    )
    got = exchange(asked, "archive")
    line_vec, hidden_all, slope_t = call(
        head_kernel,
        [
            shape_of((frames_l, vec_width), bf16),
            shape_of((frames, hid), bf16),
            shape_of((hid, frames), f32),
        ],
        [xl, xq, w_in, bias, w_out],
        0,
        flops=frames * head_flops,
        transcendentals=frames * hid,
    )
    match_flops = 2 * owner_count * rows * frames_l * vec_width
    answer, weights, own = call(
        match_kernel,
        [
            wire,
            shape_of((owner_count, rows, line_len), bf16),
            shape_of((META, LANES), f32),
        ],
        [place, frame_count, got, line_vec],
        2,
        flops=2 * match_flops,
    )
    back = exchange(answer, "archive")
    flat_rows = owner_count * 16 * -(-(feat * hid + hid * vec_width + hid) // (LANES * 16 * owner_count))

    def grads_body(*refs):
        grad_kernel(*refs, loss_factor=loss_factor)

    loss, partial = call(
        grads_body,
        [shape_of((META, LANES), f32), shape_of((flat_rows, LANES), bf16)],
        [place, back, got, weights, own, xl, xq, hidden_all, slope_t, w_out],
        1,
        [
            pltpu.VMEM((owner_count, META, LANES), f32),
            pltpu.VMEM((owner_count, META, LANES), f32),
            pltpu.VMEM((vec_width, frames_l), f32),
            pltpu.VMEM((vec_width, frames_q), f32),
        ],
        flops=match_flops + 4 * frames * head_flops,
    )
    share = flat_rows // owner_count
    parts = exchange(partial.reshape(owner_count, share, LANES), "archive")
    (sums,) = call(sum_archive_kernel, [shape_of((dp_count, share, LANES), f32)], [parts], 0)
    sums = exchange(sums, "dp")
    (whole,) = call(sum_dp_kernel, [shape_of((owner_count, share, LANES), bf16)], [sums], 0)
    whole = exchange(whole, "archive")
    grad_in, grad_bias, grad_out = call(
        unpack_kernel,
        [shape_of((feat, hid), f32), shape_of((1, hid), f32), shape_of((hid, vec_width), f32)],
        [whole.reshape(flat_rows, LANES)],
        0,
    )
    return (loss[:query_count, 0], grad_in, grad_bias.reshape(hid), grad_out)


def solution(mesh):
    placed = (
        P(("archive", "dp"), None, None),
        P("archive", None, None),
        P(),
        P(),
        P(("archive", "dp"), None),
        P(("archive", "dp")),
        P(),
        P(),
        P(),
    )
    return jax.shard_map(
        local,
        mesh=mesh,
        in_specs=placed,
        out_specs=(P(("archive", "dp")), P(), P(), P()),
        check_vma=False,
    )
```

time: 657 us -> 180 us (0.27)
  waiting for transfers between devices: 447 us -> 43 us
  matrix products: 30.4 us -> 0 us
  Pallas kernels: 0 us -> 29.1 us
  blocking collectives: 101 us -> 75.8 us
  local copies, waits for them, and re-layouts: 23 us -> 8.47 us
  between operations: 14.4 us -> 0.74 us
  other arithmetic: 10.7 us -> 0.6 us
    all_to_all x3 -> x2, waiting for transfers between devices: 274 us -> 43 us  [exchange(): return lax.all_to_all(x, axis, split_axis=0, concat_axis=0, tiled=True)]
    psum x1 -> x0, waiting for transfers between devices: 173 us -> none  [local(): lax.psum((query_terms[0] + line_terms[0], query_terms[1] + line_terms[1],...]
    psum x1 -> x0, blocking collectives: 101 us -> none  [local(): lax.psum((query_terms[0] + line_terms[0], query_terms[1] + line_terms[1],...]
    all_to_all x0 -> x3, blocking collectives: none -> 75.8 us  [exchange(): return lax.all_to_all(x, axis, split_axis=0, concat_axis=0, tiled=True)]
    dot_general x14 -> x0, matrix products: 30.4 us -> none  [the longest x1 10.6 us: local(): jnp.dot(line_onehot, got_grads, precision=lax.Precision.HIGHEST, preferre...]
    pallas_call x0 -> x7, Pallas kernels: none -> 29.1 us  [call(): pl.pallas_call(body, out_shape=tuple(outs), in_specs=[smem] * smem_count...]
    gather x6 -> x0, local copies, waits for them, and re-layouts: 15.8 us -> none  [the longest x1 6.19 us: local(): grad_line[slot_request]]
    select_n x6 -> x0, other arithmetic: 7.26 us -> none  [the longest x1 7.22 us: local(): jnp.where(slot_used[:, None, None], grad_line[slot_request], 0.0)]
  transfers between devices with their start and end apart: 4 -> 2, of which waited for: 4 -> 2; matrix products, arithmetic and copies ran while one was open for 2% -> 0% of each run, Pallas kernels for 0% -> 1%
where the time goes in v1:
time: 180 us
  blocking collectives  75.8 us (42%)
  waiting for transfers between devices  43 us (24%)
  Pallas kernels  29.1 us (16%)
  starting transfers between devices  22.2 us (12%)
  local copies, waits for them, and re-layouts  8.47 us (5%)
    all_to_all x3, blocking collectives, exchange(): return lax.all_to_all(x, axis, split_axis=0, concat_axis=0, tiled=True)  75.8 us
    all_to_all x2, waiting for transfers between devices, exchange(): return lax.all_to_all(x, axis, split_axis=0, concat_axis=0, tiled=True)  43 us
    pallas_call x7, Pallas kernels, call(): pl.pallas_call(body, out_shape=tuple(outs), in_specs=[smem] * smem_count...  29.1 us
    all_to_all x2, starting transfers between devices, exchange(): return lax.all_to_all(x, axis, split_axis=0, concat_axis=0, tiled=True)  22.2 us
    unnamed x30, local copies, waits for them, and re-layouts  7.16 us
  transfers between devices with their start and end apart: 2, of which 2 were waited for; matrix products, arithmetic and copies ran while one was open for 0% of the time, Pallas kernels for 1%

profile of v1, /device:TPU:1, one launch (start us, length us, event | category | flops | bytes accessed | tf_op | source)
XLA Modules:
  0.0 179.9 jit_solution(16082772118125675201)
XLA Ops:
  0.6 0.7 reshape.31.bias
  1.3 1.0 copy-done
  2.3 0.9 copy-done.2
  3.3 0.9 copy-done.4
  4.2 0.7 copy-done.6
  4.8 0.7 copy-done.7
  5.5 0.7 copy-done.8
  6.2 4.0 %shard_map.120 = bf16[64,72,128]{2,1,0:T(8,128)(2,1)} custom-call(s32[8,6]{1,0:T(8,128)S(1)} %copy-done.6, s32[512]{0:T(512)S(1)} %copy-done.7, s32[8]{0:T(128)S(1)} %copy-done.8, bf16[256,512]{1,0:T(8,128)(2,1)S(1)} %bitcast.7, bf16[512,384]{1,0:T(8,128)(2,1)S(1)} %copy-done, f32[1,384]{1,0:T(1,128)S(1)} %reshape.31.bias, bf16[384,128]{1,0:T(8,128)(2,1)S(1)} %copy-done.4), custom_call_target="tpu_custom_call" | custom-call | flops 125829120 | bytes 1937120 | tf_op jit(solution)/shard_map/pallas_call | solution.py:39
  10.2 15.0 %all-to-all-start = ((bf16[64,72,128]{2,1,0:T(8,128)(2,1)}), bf16[64,72,128]{2,1,0:T(8,128)(2,1)S(1)}, u32[]{:S(2)}, u32[]{:S(2)}) async-start(bf16[64,72,128]{2,1,0:T(8,128)(2,1)} %shard_map.120), calls=%async_computation | async-start | bytes 2359296 | tf_op jit(solution)/shard_map/all_to_all | solution.py:371
  25.3 2.3 %shard_map.121 = (bf16[1024,128]{1,0:T(8,128)(2,1)S(1)}, bf16[1280,384]{1,0:T(8,128)(2,1)S(1)}, f32[384,1280]{1,0:T(8,128)S(1)}) custom-call(bf16[1024,512]{1,0:T(8,128)(2,1)S(1)} %bitcast.10, bf16[256,512]{1,0:T(8,128)(2,1)S(1)} %bitcast.8, bf16[512,384]{1,0:T(8,128)(2,1)S(1)} %copy-done.1, f32[1,384]{1,0:T(1,128)S(1)} %reshape.31.bias, ...), custom_call_target="tpu_custom_call" | custom-call | flops 629145600 | bytes 5015040 | tf_op jit(solution)/shard_map/pallas_call | solution.py:39
  27.6 1.3 copy-done.11
  28.9 1.0 copy-done.13
  29.9 25.9 %all-to-all-done.got.refs_2_ = bf16[64,72,128]{2,1,0:T(8,128)(2,1)S(1)} async-done(((bf16[64,72,128]{2,1,0:T(8,128)(2,1)}), bf16[64,72,128]{2,1,0:T(8,128)(2,1)S(1)}, u32[]{:S(2)}, u32[]{:S(2)}) %all-to-all-start) | async-done | bytes 1179680 | tf_op jit(solution)/shard_map/all_to_all | solution.py:371
  55.8 12.8 %shard_map.122 = (bf16[64,72,128]{2,1,0:T(8,128)(2,1)S(1)}, bf16[64,64,128]{2,1,0:T(8,128)(2,1)S(1)}, f32[8,128]{1,0:T(8,128)S(1)}) custom-call(s32[1]{0:T(128)} %bitcast.place.refs_0_, s32[512]{0:T(512)S(1)} %copy-done.10, bf16[64,72,128]{2,1,0:T(8,128)(2,1)S(1)} %all-to-all-done.got.refs_2_, bf16[1024,128]{1,0:T(8,128)(2,1)S(1)} %get-tuple-element.15.line_vec), custom_call_target="tpu_custom_call" | custom-call | flops 2147483648 | bytes 3676164 | tf_op jit(solution)/shard_map/pallas_call | solution.py:39
  68.6 37.2 %all_to_all.25.refs_1_ = bf16[64,72,128]{2,1,0:T(8,128)(2,1)S(1)} all-to-all(bf16[64,72,128]{2,1,0:T(8,128)(2,1)S(1)} %get-tuple-element.16), channel_id=1, replica_groups=mesh['archive'=64,'dp'=8] {'archive'}, dimensions={0} | all-to-all | bytes 2359296 | tf_op jit(solution)/shard_map/all_to_all | solution.py:371
  105.8 7.9 %shard_map.123 = (f32[8,128]{1,0:T(8,128)S(1)}, bf16[2048,128]{1,0:T(8,128)(2,1)S(1)}) custom-call(s32[1]{0:T(128)} %bitcast.place.refs_0_, bf16[64,72,128]{2,1,0:T(8,128)(2,1)S(1)} %all_to_all.25.refs_1_, bf16[64,72,128]{2,1,0:T(8,128)(2,1)S(1)} %all-to-all-done.got.refs_2_, bf16[64,64,128]{2,1,0:T(8,128)(2,1)S(1)} %get-tuple-element.17.refs_3_, ...), custom_call_target="tpu_custom_call" | custom-call | flops 3590324224 | bytes 8298500 | tf_op jit(solution)/shard_map/pallas_call | solution.py:39
  113.7 24.1 %all_to_all.26.got = bf16[64,32,128]{2,1,0:T(8,128)(2,1)S(1)} all-to-all(bf16[64,32,128]{2,1,0:T(8,128)(2,1)S(1)} %bitcast.6), channel_id=1, replica_groups=mesh['archive'=64,'dp'=8] {'archive'}, dimensions={0} | all-to-all | bytes 1048576 | tf_op jit(solution)/shard_map/all_to_all | solution.py:371
  137.9 14.5 %all_to_all.27.got = f32[8,32,128]{2,1,0:T(8,128)S(1)} all-to-all(f32[8,32,128]{2,1,0:T(8,128)S(1)} %shard_map.124), channel_id=1, replica_groups=mesh['archive'=64,'dp'=8] {'dp'}, dimensions={0} | all-to-all | bytes 262144 | tf_op jit(solution)/shard_map/all_to_all | solution.py:371
  152.4 0.8 shard_map.125
  153.2 7.2 %all-to-all-start.4 = ((bf16[64,32,128]{2,1,0:T(8,128)(2,1)}), bf16[64,32,128]{2,1,0:T(8,128)(2,1)S(1)}, u32[]{:S(2)}, u32[]{:S(2)}) async-start(bf16[64,32,128]{2,1,0:T(8,128)(2,1)} %shard_map.125), calls=%async_computation.4 | async-start | bytes 1048576 | tf_op jit(solution)/shard_map/all_to_all | solution.py:371
  160.5 0.6 slice_reduce_fusion
  161.1 17.1 %all-to-all-done.4 = bf16[64,32,128]{2,1,0:T(8,128)(2,1)S(1)} async-done(((bf16[64,32,128]{2,1,0:T(8,128)(2,1)}), bf16[64,32,128]{2,1,0:T(8,128)(2,1)S(1)}, u32[]{:S(2)}, u32[]{:S(2)}) %all-to-all-start.4) | async-done | bytes 524320 | tf_op jit(solution)/shard_map/all_to_all | solution.py:371
  178.2 1.1 shard_map.126
  179.3 0.6 reduce.1
  (23 shorter events, 0.1 us)
Async XLA Ops:
  1.3 1.0 copy-start
  2.3 0.9 copy-start.2
  3.3 0.9 copy-start.4
  4.2 0.7 copy-start.6
  4.8 0.7 copy-start.7
  5.5 0.7 copy-start.8
  10.2 15.0 %copy-start.1 = (bf16[512,384]{1,0:T(8,128)(2,1)S(1)}, bf16[512,384]{1,0:T(8,128)(2,1)}, u32[]{:S(2)}) copy-start(bf16[512,384]{1,0:T(8,128)(2,1)} %w_in.3) | copy-start | bytes 1179652
  10.2 15.0 %copy-start.3 = (bf16[8,32,512]{2,1,0:T(8,128)(2,1)S(1)}, bf16[8,32,512]{2,1,0:T(8,128)(2,1)}, u32[]{:S(2)}) copy-start(bf16[8,32,512]{2,1,0:T(8,128)(2,1)} %param.9) | copy-start | bytes 786436
  10.2 15.0 %copy-start.5 = (bf16[384,128]{1,0:T(8,128)(2,1)S(1)}, bf16[384,128]{1,0:T(8,128)(2,1)}, u32[]{:S(2)}) copy-start(bf16[384,128]{1,0:T(8,128)(2,1)} %refs_9_.1) | copy-start | bytes 294916
  10.2 15.0 %copy-start.9 = (bf16[8,128,512]{2,1,0:T(8,128)(2,1)S(1)}, bf16[8,128,512]{2,1,0:T(8,128)(2,1)}, u32[]{:S(2)}) copy-start(bf16[8,128,512]{2,1,0:T(8,128)(2,1)} %param.10) | copy-start | bytes 3145732
  10.2 45.6 %all-to-all-start = ((bf16[64,72,128]{2,1,0:T(8,128)(2,1)}), bf16[64,72,128]{2,1,0:T(8,128)(2,1)S(1)}, u32[]{:S(2)}, u32[]{:S(2)}) async-start(bf16[64,72,128]{2,1,0:T(8,128)(2,1)} %shard_map.120), calls=%async_computation | async-start | bytes 2359296 | tf_op jit(solution)/shard_map/all_to_all | solution.py:371
  25.2 30.6 %copy-start.10 = (s32[512]{0:T(512)S(1)}, s32[512]{0:T(512)}, u32[]{:S(2)}) copy-start(s32[512]{0:T(512)} %counts.1) | copy-start | bytes 6148
  27.6 1.3 copy-start.11
  28.9 1.0 copy-start.13
  55.8 50.0 %copy-start.14 = (bf16[1280,384]{1,0:T(8,128)(2,1)S(1)}, bf16[1280,384]{1,0:T(8,128)(2,1)}, u32[]{:S(2)}) copy-start(bf16[1280,384]{1,0:T(8,128)(2,1)} %copy-done.13) | copy-start | bytes 2949124
  68.6 37.2 %copy-start.12 = (f32[384,1280]{1,0:T(8,128)S(1)}, f32[384,1280]{1,0:T(8,128)}, u32[]{:S(2)}) copy-start(f32[384,1280]{1,0:T(8,128)} %copy-done.11) | copy-start | bytes 5898244
  153.2 24.9 %all-to-all-start.4 = ((bf16[64,32,128]{2,1,0:T(8,128)(2,1)}), bf16[64,32,128]{2,1,0:T(8,128)(2,1)S(1)}, u32[]{:S(2)}, u32[]{:S(2)}) async-start(bf16[64,32,128]{2,1,0:T(8,128)(2,1)} %shard_map.125), calls=%async_computation.4 | async-start | bytes 1048576 | tf_op jit(solution)/shard_map/all_to_all | solution.py:371

commit v2 on v1

--- a/solution.py
+++ b/solution.py
@@ -5,7 +5,7 @@
 from jax import lax
 from jax.experimental import pallas as pl
 from jax.experimental.pallas import tpu as pltpu
-from jax.sharding import PartitionSpec as P
+from jax.sharding import Mesh, PartitionSpec as P
 
 LOSS_SCALE = 4096.0
 SCORE_SCALE = 4.0
@@ -18,6 +18,7 @@
 GELU_A = math.sqrt(2.0 / math.pi)
 GELU_B = 0.044715
 GROUP = 4
+ARCHIVE = ("chip", "core")
 
 f32 = jnp.float32
 bf16 = jnp.bfloat16
@@ -32,14 +33,21 @@
     return hi, (x - hi.astype(f32)).astype(bf16)
 
 
-def call(body, outs, args, smem_count, scratch=(), flops=0, transcendentals=0):
+def split3(x):
+    hi = x.astype(bf16).astype(f32)
+    mid = (x - hi).astype(bf16).astype(f32)
+    return hi, mid, (x - hi - mid).astype(bf16).astype(f32)
+
+
+def call(body, outs, args, smem_count, scratch=(), flops=0, transcendentals=0, where=pltpu.VMEM):
     nbytes = sum(a.size * a.dtype.itemsize for a in list(args) + list(outs))
     vmem = pl.BlockSpec(memory_space=pltpu.VMEM)
     smem = pl.BlockSpec(memory_space=pltpu.SMEM)
+    rest = pl.BlockSpec(memory_space=where)
     return pl.pallas_call(
         body,
         out_shape=tuple(outs),
-        in_specs=[smem] * smem_count + [vmem] * (len(args) - smem_count),
+        in_specs=[smem] * smem_count + [rest] * (len(args) - smem_count),
         out_specs=tuple(vmem for _ in outs),
         scratch_shapes=list(scratch),
         compiler_params=pltpu.CompilerParams(vmem_limit_bytes=40 << 20),
@@ -54,15 +62,18 @@
     return t, (0.5 * pre * (1.0 + t)).astype(bf16)
 
 
-def ask_kernel(mined, home, positive, x, w_in, bias, w_out, send, vec, rid, code, count):
+def ask_kernel(
+    mined, home, positive, x_hbm, w_in_hbm, bias_hbm, w_out_hbm, send, x, w_in, bias, w_out, vec, rid, code, count, goal, sems
+):
     query_count, mined_count = mined.shape
     owner_count = send.shape[0]
     query_len = x.shape[0] // query_count
     line_count = home.shape[0] // owner_count
     rows = CAP * query_len
-    _, hidden = gelu_parts(dot(x[...], w_in[...]) + bias[...])
-    vec[...] = dot(hidden, w_out[...]).astype(bf16)
-    send[...] = jnp.zeros(send.shape, bf16)
+    pairs = ((x_hbm, x), (w_in_hbm, w_in), (bias_hbm, bias), (w_out_hbm, w_out))
+    copies = [pltpu.make_async_copy(a, b, sems.at[i]) for i, (a, b) in enumerate(pairs)]
+    for copy in copies:
+        copy.start()
 
     def clear(owner, carry):
         count[owner] = 0
@@ -71,10 +82,9 @@
             code[c, owner] = int(UNUSED)
         return carry
 
-    lax.fori_loop(0, owner_count, clear, 0)
-
-    def place(query, carry):
-        block = vec[pl.ds(pl.multiple_of(query * query_len, query_len), query_len), :]
+    lax.fori_loop(0, owner_count, clear, 0, unroll=8)
+
+    def assign(query, carry):
         for j in range(mined_count):
             row = home[mined[query, j]]
             owner = row // line_count
@@ -82,10 +92,11 @@
             count[owner] = rank + 1
             rid[rank, owner] = row - owner * line_count
             code[rank, owner] = query + jnp.where(positive[query] == j, 8, 0)
-            send[owner, pl.ds(pl.multiple_of(rank * query_len, query_len), query_len), :] = block
+            goal[query, j] = owner * CAP + rank
         return carry
 
-    lax.fori_loop(0, query_count, place, 0)
+    lax.fori_loop(0, query_count, assign, 0)
+    send[...] = jnp.zeros(send.shape, bf16)
     sub = lax.broadcasted_iota(jnp.int32, (META, LANES), 0)
 
     def label(owner, carry):
@@ -97,12 +108,27 @@
         send[owner, rows : rows + META, :] = tile.astype(f32).astype(bf16)
         return carry
 
-    lax.fori_loop(0, owner_count, label, 0)
-
-
-def head_kernel(xl, xq, w_in, bias, w_out, line_vec, hidden_all, slope_t):
+    lax.fori_loop(0, owner_count, label, 0, unroll=8)
+    for copy in copies:
+        copy.wait()
+    _, hidden = gelu_parts(dot(x[...], w_in[...]) + bias[...])
+    vec[...] = dot(hidden, w_out[...]).astype(bf16)
+
+    def place(query, carry):
+        block = vec[pl.ds(pl.multiple_of(query * query_len, query_len), query_len), :]
+        for j in range(mined_count):
+            owner = goal[query, j] // CAP
+            rank = goal[query, j] % CAP
+            send[owner, pl.ds(pl.multiple_of(rank * query_len, query_len), query_len), :] = block
+        return carry
+
+    lax.fori_loop(0, query_count, place, 0)
+
+
+def head_kernel(xl, xq, w_in, bias, w_out, line_vec, hidden_all, slope_t, mean):
     step = 256
     line_frames = xl.shape[0]
+    total = jnp.zeros((1, hidden_all.shape[1]), f32)
     for first in range(0, line_frames + xq.shape[0], step):
         if first < line_frames:
             x = xl[first : first + step, :]
@@ -118,6 +144,10 @@
         slope_t[:, first : first + size] = slope.T
         if first < line_frames:
             line_vec[first : first + size, :] = dot(hidden, w_out[...]).astype(bf16)
+            total += jnp.sum(hidden.astype(f32), axis=0, keepdims=True)
+    mean[...] = jnp.zeros(mean.shape, f32)
+    for i, k in enumerate(range(0, hidden_all.shape[1], LANES)):
+        mean[4 + i : 5 + i, :] = total[:, k : k + LANES] * (1.0 / line_frames)
 
 
 def spread(meta, first, query_len):
@@ -128,7 +158,7 @@
     return jnp.concatenate(parts, axis=0)
 
 
-def match_kernel(place, counts, got, line_vec, send, weights, own):
+def match_kernel(place, counts, got, line_vec, mean, send, weights, own):
     owner_count = got.shape[0]
     rows = got.shape[1] - META
     query_len = rows // CAP
@@ -186,6 +216,7 @@
         owner_count // GROUP,
         step,
         (jnp.zeros((1, LANES), f32), jnp.full((1, LANES), UNUSED, f32)),
+        unroll=2,
     )
     sub = lax.broadcasted_iota(jnp.int32, (META, LANES), 0)
     own[...] = jnp.where(sub == 0, match_row, code_row)
@@ -194,7 +225,8 @@
     low = match_row - high - middle
     tile = jnp.where(
         sub == 0, high, jnp.where(sub == 1, middle, jnp.where(sub == 2, low, code_row))
-    ).astype(bf16)
+    )
+    tile = jnp.where(sub < 4, tile, mean[...]).astype(bf16)
 
     def label(b, carry):
         send[b, rows : rows + META, :] = tile
@@ -204,7 +236,7 @@
 
 
 def grad_kernel(
-    place, back, got, weights, own, xl, xq, hidden_all, slope_t, w_out, loss, grads, own_scale, ask_scale, line_acc, query_acc, *, loss_factor
+    place, back, got, weights, own, xl, xq, hidden_all, slope_t, w_out, loss, keep, give, base_row, grads, own_scale, ask_scale, line_acc, query_acc, *, loss_factor
 ):
     owner_count = got.shape[0]
     rows = got.shape[1] - META
@@ -306,7 +338,11 @@
     grad_in = None
     grad_out = None
     grad_bias = None
-    ones = jnp.ones((META, 1), bf16)
+    vec_sum = None
+    shared = jnp.sum(jnp.where(sub3 >= 4, meta, 0.0), axis=0) * (1.0 / owner_count)
+    shared = shared.astype(bf16).astype(f32)
+    shared = jnp.concatenate([shared[4 + i : 5 + i, :] for i in range(hid // LANES)], axis=1)
+    base_row[...] = jnp.broadcast_to(shared, base_row.shape)
     spans = ((line_acc, xl, 0, line_total), (query_acc, xq, line_total, query_frames))
     for acc, x, first, span in spans:
         g_hi, g_lo = split2(acc[:, 0:span])
@@ -316,55 +352,91 @@
         ones = jnp.ones((META, span), bf16)
         part_in = dot(p_hi, x[...]) + dot(p_lo, x[...])
         part_out = dot(g_hi, hidden) + dot(g_lo, hidden)
+        part_out -= jnp.sum(g_hi.astype(f32) + g_lo.astype(f32), axis=1, keepdims=True) * shared
+        part_sum = dot(ones, g_hi, 1, 1) + dot(ones, g_lo, 1, 1)
+        vec_sum = part_sum if vec_sum is None else vec_sum + part_sum
         part_bias = dot(ones, p_hi, 1, 1) + dot(ones, p_lo, 1, 1)
         grad_in = part_in if grad_in is None else grad_in + part_in
         grad_out = part_out if grad_out is None else grad_out + part_out
         grad_bias = part_bias if grad_bias is None else grad_bias + part_bias
     base = 0
     for k in range(0, x.shape[1], LANES):
-        grads[base : base + hid, :] = grad_in[:, k : k + LANES].astype(bf16)
+        grads[base : base + hid, :] = grad_in[:, k : k + LANES]
         base += hid
     for k in range(0, hid, LANES):
-        grads[base : base + vec_width, :] = grad_out[:, k : k + LANES].astype(bf16)
+        grads[base : base + vec_width, :] = grad_out[:, k : k + LANES]
         base += vec_width
     rest = grads.shape[0] - base
-    sub = lax.broadcasted_iota(jnp.int32, (rest, LANES), 0)
-    tile = jnp.zeros((rest, LANES), f32)
-    for i, k in enumerate(range(0, hid, LANES)):
-        tile = jnp.where(sub == i, grad_bias[0:1, k : k + LANES], tile)
-    grads[base:, :] = tile.astype(bf16)
-
-
-def sum_archive_kernel(got, send):
+    singles = [grad_bias[0:1, k : k + LANES] for k in range(0, hid, LANES)] + [vec_sum[0:1, :]]
+    grads[base:, :] = tail_tile(singles, rest)
+    half = keep.shape[0]
+    core = place[1]
+    keep[...] = grads[pl.ds(pl.multiple_of(core * half, half), half), :]
+    give[...] = grads[pl.ds(pl.multiple_of((1 - core) * half, half), half), :].astype(bf16)
+
+
+def tail_tile(values, size):
+    sub = lax.broadcasted_iota(jnp.int32, (size, LANES), 0)
+    tile = jnp.zeros((size, LANES), f32)
+    for i, value in enumerate(values):
+        for p, part in enumerate(split3(value)):
+            tile = jnp.where(sub == 3 * i + p, part, tile)
+    return tile
+
+
+def tail_values(tile, count):
+    return [
+        tile[3 * i : 3 * i + 1] + tile[3 * i + 1 : 3 * i + 2] + tile[3 * i + 2 : 3 * i + 3]
+        for i in range(count)
+    ]
+
+
+def sum_core_kernel(place, keep, got, send, *, tail_rows, tail_count):
+    total = keep[...] + got[...].astype(f32)
+    send[...] = total.astype(bf16)
+
+    @pl.when(place[1] == 1)
+    def _():
+        first = total.shape[0] - tail_rows
+        values = tail_values(total[first:, :], tail_count)
+        send[first:, :] = tail_tile(values, tail_rows).astype(bf16)
+
+
+def sum_kernel(got, send):
     part = got[0].astype(f32)
     for k in range(1, got.shape[0]):
         part = part + got[k].astype(f32)
-    for k in range(send.shape[0]):
-        send[k] = part
-
-
-def sum_dp_kernel(got, send):
-    part = got[0]
-    for k in range(1, got.shape[0]):
-        part = part + got[k]
     part = part.astype(bf16)
     for k in range(send.shape[0]):
         send[k] = part
 
 
-def unpack_kernel(got, grad_in, grad_bias, grad_out):
+def unpack_kernel(place, mine, other, base_row, grad_in, grad_bias, grad_out, got):
     feat, hid = grad_in.shape
     vec_width = grad_out.shape[1]
+    half = mine.shape[0]
+    core = place[1]
+    got[pl.ds(pl.multiple_of(core * half, half), half), :] = mine[...]
+    got[pl.ds(pl.multiple_of((1 - core) * half, half), half), :] = other[...]
     base = 0
     for k in range(0, feat, LANES):
         grad_in[k : k + LANES, :] = got[base : base + hid, :].astype(f32).T
         base += hid
-    for k in range(0, hid, LANES):
-        grad_out[k : k + LANES, :] = got[base : base + vec_width, :].astype(f32).T
+    start = base + vec_width * (hid // LANES)
+    values = tail_values(got[start : start + 16, :].astype(f32), hid // LANES + 1)
+    vec_sum = values[-1]
+    sub = lax.broadcasted_iota(jnp.int32, (META, LANES), 0)
+    zero = jnp.zeros((META, LANES), f32)
+    vec_rows = zero
+    for p, part in enumerate(split3(vec_sum)):
+        vec_rows = jnp.where(sub == p, part, vec_rows)
+    vec_rows = vec_rows.astype(bf16)
+    for i, k in enumerate(range(0, hid, LANES)):
+        base_rows = base_row[:, k : k + LANES].astype(bf16)
+        outer = dot(base_rows, vec_rows, 0, 0)
+        grad_out[k : k + LANES, :] = got[base : base + vec_width, :].astype(f32).T + outer
+        grad_bias[0:1, k : k + LANES] = values[i]
         base += vec_width
-    tail = got[base : base + 16, :].astype(f32)
-    for i, k in enumerate(range(0, hid, LANES)):
-        grad_bias[0:1, k : k + LANES] = tail[i : i + 1, :]
 
 
 def exchange(x, axis):
@@ -379,7 +451,8 @@
     query_count, query_len, feat = query_frames.shape
     line_count, line_len, _ = line_frames.shape
     hid, vec_width = w_out.shape
-    owner_count = lax.axis_size("archive")
+    chip_count = lax.axis_size("chip")
+    owner_count = chip_count * lax.axis_size("core")
     dp_count = lax.axis_size("dp")
     loss_factor = LOSS_SCALE / (query_count * owner_count * dp_count)
     frames_q = query_count * query_len
@@ -389,7 +462,7 @@
     xq = query_frames.reshape(frames_q, feat)
     xl = line_frames.reshape(frames_l, feat)
     bias = bias_in.reshape(1, hid)
-    place = lax.axis_index("archive").astype(jnp.int32).reshape(1)
+    place = jnp.stack([lax.axis_index(ARCHIVE), lax.axis_index("core")]).astype(jnp.int32)
     wire = shape_of((owner_count, rows + META, vec_width), bf16)
     head_flops = 2 * hid * (feat + vec_width)
 
@@ -399,20 +472,28 @@
         [mined, line_home, positive, xq, w_in, bias, w_out],
         3,
         [
+            pltpu.VMEM(xq.shape, bf16),
+            pltpu.VMEM(w_in.shape, bf16),
+            pltpu.VMEM(bias.shape, f32),
+            pltpu.VMEM(w_out.shape, bf16),
             pltpu.VMEM((frames_q, vec_width), bf16),
             pltpu.SMEM((CAP, owner_count), jnp.int32),
             pltpu.SMEM((CAP, owner_count), jnp.int32),
             pltpu.SMEM((owner_count,), jnp.int32),
+            pltpu.SMEM(mined.shape, jnp.int32),
+            pltpu.SemaphoreType.DMA((4,)),
         ],
         flops=frames_q * head_flops,
-    )
-    got = exchange(asked, "archive")
-    line_vec, hidden_all, slope_t = call(
+        where=pl.ANY,
+    )
+    got = exchange(asked, ARCHIVE)
+    line_vec, hidden_all, slope_t, mean = call(
         head_kernel,
         [
             shape_of((frames_l, vec_width), bf16),
             shape_of((frames, hid), bf16),
             shape_of((hid, frames), f32),
+            shape_of((META, LANES), f32),
         ],
         [xl, xq, w_in, bias, w_out],
         0,
@@ -427,22 +508,30 @@
             shape_of((owner_count, rows, line_len), bf16),
             shape_of((META, LANES), f32),
         ],
-        [place, frame_count, got, line_vec],
+        [place, frame_count, got, line_vec, mean],
         2,
         flops=2 * match_flops,
     )
-    back = exchange(answer, "archive")
-    flat_rows = owner_count * 16 * -(-(feat * hid + hid * vec_width + hid) // (LANES * 16 * owner_count))
+    back = exchange(answer, ARCHIVE)
+    unit = 16 * owner_count
+    flat_rows = unit * -(-(LANES + (feat + vec_width) * hid // LANES) // unit)
+    half = flat_rows // 2
 
     def grads_body(*refs):
         grad_kernel(*refs, loss_factor=loss_factor)
 
-    loss, partial = call(
+    loss, keep, give, base_row = call(
         grads_body,
-        [shape_of((META, LANES), f32), shape_of((flat_rows, LANES), bf16)],
+        [
+            shape_of((META, LANES), f32),
+            shape_of((half, LANES), f32),
+            shape_of((half, LANES), bf16),
+            shape_of((META, hid), f32),
+        ],
         [place, back, got, weights, own, xl, xq, hidden_all, slope_t, w_out],
         1,
         [
+            pltpu.VMEM((flat_rows, LANES), f32),
             pltpu.VMEM((owner_count, META, LANES), f32),
             pltpu.VMEM((owner_count, META, LANES), f32),
             pltpu.VMEM((vec_width, frames_l), f32),
@@ -450,29 +539,43 @@
         ],
         flops=match_flops + 4 * frames * head_flops,
     )
-    share = flat_rows // owner_count
-    parts = exchange(partial.reshape(owner_count, share, LANES), "archive")
-    (sums,) = call(sum_archive_kernel, [shape_of((dp_count, share, LANES), f32)], [parts], 0)
-    sums = exchange(sums, "dp")
-    (whole,) = call(sum_dp_kernel, [shape_of((owner_count, share, LANES), bf16)], [sums], 0)
-    whole = exchange(whole, "archive")
+    swap = [(0, 1), (1, 0)]
+    share = half // chip_count
+    taken = lax.ppermute(give, "core", swap)
+    tail_rows = flat_rows - (feat + vec_width) * hid // LANES
+
+    def sum_core_body(*refs):
+        sum_core_kernel(*refs, tail_rows=tail_rows, tail_count=hid // LANES + 1)
+
+    (part,) = call(sum_core_body, [shape_of((half, LANES), bf16)], [place, keep, taken], 1)
+    parts = exchange(part.reshape(chip_count, share, LANES), "chip")
+    (part,) = call(sum_kernel, [shape_of((dp_count, share, LANES), bf16)], [parts], 0)
+    parts = exchange(part, "dp")
+    (part,) = call(sum_kernel, [shape_of((chip_count, share, LANES), bf16)], [parts], 0)
+    mine = exchange(part, "chip").reshape(half, LANES)
+    other = lax.ppermute(mine, "core", swap)
     grad_in, grad_bias, grad_out = call(
         unpack_kernel,
         [shape_of((feat, hid), f32), shape_of((1, hid), f32), shape_of((hid, vec_width), f32)],
-        [whole.reshape(flat_rows, LANES)],
-        0,
+        [place, mine, other, base_row],
+        1,
+        [pltpu.VMEM((flat_rows, LANES), bf16)],
     )
     return (loss[:query_count, 0], grad_in, grad_bias.reshape(hid), grad_out)
 
 
 def solution(mesh):
+    devices = mesh.devices
+    archive, dp = devices.shape
+    mesh = Mesh(devices.reshape(archive // 2, 2, dp), ("chip", "core", "dp"))
+    everywhere = ARCHIVE + ("dp",)
     placed = (
-        P(("archive", "dp"), None, None),
-        P("archive", None, None),
+        P(everywhere, None, None),
+        P(ARCHIVE, None, None),
         P(),
         P(),
-        P(("archive", "dp"), None),
-        P(("archive", "dp")),
+        P(everywhere, None),
+        P(everywhere),
         P(),
         P(),
         P(),
@@ -481,6 +584,6 @@
         local,
         mesh=mesh,
         in_specs=placed,
-        out_specs=(P(("archive", "dp")), P(), P(), P()),
+        out_specs=(P(everywhere), P(), P(), P()),
         check_vma=False,
     )

time: 180 us -> 173 us (0.961)
  waiting for transfers between devices: 43 us -> 27.4 us
  blocking collectives: 75.8 us -> 82 us
  starting transfers between devices: 22.2 us -> 24.4 us
    all_to_all x2 -> x1, waiting for transfers between devices: 43 us -> 25.8 us  [exchange(): return lax.all_to_all(x, axis, split_axis=0, concat_axis=0, tiled=True)]
    ppermute x0 -> x2, starting transfers between devices: none -> 9.42 us  [the longest x1 5.95 us: local(): other = lax.ppermute(mine, 'core', swap)]
    all_to_all x2 -> x1, starting transfers between devices: 22.2 us -> 15 us  [exchange(): return lax.all_to_all(x, axis, split_axis=0, concat_axis=0, tiled=True)]
    all_to_all x3 -> x4, blocking collectives: 75.8 us -> 82 us  [exchange(): return lax.all_to_all(x, axis, split_axis=0, concat_axis=0, tiled=True)]
    pallas_call x7 -> x8, Pallas kernels: 29.1 us -> 29 us  [call(): pl.pallas_call(body, out_shape=tuple(outs), in_specs=[smem] * smem_count...]
  transfers between devices with their start and end apart: 2 -> 3, of which waited for: 2 -> 3; matrix products, arithmetic and copies ran while one was open for 0% -> 0% of each run, Pallas kernels for 1% -> 1%
where the time goes in v2:
time: 173 us
  blocking collectives  82 us (47%)
  Pallas kernels  29 us (17%)
  waiting for transfers between devices  27.4 us (16%)
  starting transfers between devices  24.4 us (14%)
  local copies, waits for them, and re-layouts  8.48 us (5%)
    all_to_all x4, blocking collectives, exchange(): return lax.all_to_all(x, axis, split_axis=0, concat_axis=0, tiled=True)  82 us
    pallas_call x8, Pallas kernels, call(): pl.pallas_call(body, out_shape=tuple(outs), in_specs=[smem] * smem_count...  29 us
    all_to_all x1, waiting for transfers between devices, exchange(): return lax.all_to_all(x, axis, split_axis=0, concat_axis=0, tiled=True)  25.8 us
    all_to_all x1, starting transfers between devices, exchange(): return lax.all_to_all(x, axis, split_axis=0, concat_axis=0, tiled=True)  15 us
    unnamed x30, local copies, waits for them, and re-layouts  7.17 us
    ppermute x1, starting transfers between devices, local(): other = lax.ppermute(mine, 'core', swap)  5.95 us
    ppermute x1, starting transfers between devices, local(): taken = lax.ppermute(give, 'core', swap)  3.47 us
  transfers between devices with their start and end apart: 3, of which 3 were waited for; matrix products, arithmetic and copies ran while one was open for 0% of the time, Pallas kernels for 1%

profile of v2, /device:TPU:1, one launch (start us, length us, event | category | flops | bytes accessed | tf_op | source)
XLA Modules:
  0.0 172.7 jit_solution(3013652654443159029)
XLA Ops:
  0.6 0.7 reshape.27.bias_hbm.bias
  1.3 1.0 copy-done
  2.3 0.9 copy-done.2
  3.3 0.9 copy-done.4
  4.2 0.7 copy-done.6
  4.8 0.7 copy-done.7
  5.5 0.7 copy-done.8
  6.2 4.2 %shard_map.120 = bf16[64,72,128]{2,1,0:T(8,128)(2,1)} custom-call(s32[8,6]{1,0:T(8,128)S(1)} %copy-done.6, s32[512]{0:T(512)S(1)} %copy-done.7, s32[8]{0:T(128)S(1)} %copy-done.8, bf16[256,512]{1,0:T(8,128)(2,1)S(1)} %bitcast.9, bf16[512,384]{1,0:T(8,128)(2,1)S(1)} %copy-done, f32[1,384]{1,0:T(1,128)S(1)} %reshape.27.bias_hbm.bias, ...), custom_call_target="tpu_custom_call" | custom-call | flops 125829120 | bytes 1937120 | tf_op jit(solution)/shard_map/pallas_call | solution.py:47
  10.4 15.0 %all-to-all-start = ((bf16[64,72,128]{2,1,0:T(8,128)(2,1)}), bf16[64,72,128]{2,1,0:T(8,128)(2,1)S(1)}, u32[]{:S(2)}, u32[]{:S(2)}) async-start(bf16[64,72,128]{2,1,0:T(8,128)(2,1)} %shard_map.120), calls=%async_computation | async-start | bytes 2359296 | tf_op jit(solution)/shard_map/all_to_all | solution.py:443
  25.5 2.4 %shard_map.121 = (bf16[1024,128]{1,0:T(8,128)(2,1)S(1)}, bf16[1280,384]{1,0:T(8,128)(2,1)S(1)}, f32[384,1280]{1,0:T(8,128)S(1)}, f32[8,128]{1,0:T(8,128)S(1)}) custom-call(bf16[1024,512]{1,0:T(8,128)(2,1)S(1)} %bitcast.12, bf16[256,512]{1,0:T(8,128)(2,1)S(1)} %bitcast.10, bf16[512,384]{1,0:T(8,128)(2,1)S(1)} %copy-done.1, ...), custom_call_target="tpu_custom_call" | custom-call | flops 629145600 | bytes 5019136 | tf_op jit(solution)/shard_map/pallas_call | solution.py:47
  27.9 1.3 copy-done.11
  29.2 1.0 copy-done.13
  30.2 25.8 %all-to-all-done.got.refs_2_ = bf16[64,72,128]{2,1,0:T(8,128)(2,1)S(1)} async-done(((bf16[64,72,128]{2,1,0:T(8,128)(2,1)}), bf16[64,72,128]{2,1,0:T(8,128)(2,1)S(1)}, u32[]{:S(2)}, u32[]{:S(2)}) %all-to-all-start) | async-done | bytes 1179680 | tf_op jit(solution)/shard_map/all_to_all | solution.py:443
  56.0 11.2 %shard_map.122 = (bf16[64,72,128]{2,1,0:T(8,128)(2,1)S(1)}, bf16[64,64,128]{2,1,0:T(8,128)(2,1)S(1)}, f32[8,128]{1,0:T(8,128)S(1)}) custom-call(s32[2]{0:T(128)S(1)} %pad_add_fusion.place.refs_0_, s32[512]{0:T(512)S(1)} %copy-done.10, bf16[64,72,128]{2,1,0:T(8,128)(2,1)S(1)} %all-to-all-done.got.refs_2_, bf16[1024,128]{1,0:T(8,128)(2,1)S(1)} %get-tuple-element.18.line_vec, ...), custom_call_target="tpu_custom_call" | custom-call | flops 2147483648 | bytes 3680264 | tf_op jit(solution)/shard_map/pallas_call | solution.py:47
  67.2 37.2 %all_to_all.25.refs_1_ = bf16[64,72,128]{2,1,0:T(8,128)(2,1)S(1)} all-to-all(bf16[64,72,128]{2,1,0:T(8,128)(2,1)S(1)} %get-tuple-element.20), channel_id=1, replica_groups=mesh['chip'=32,'core'=2,'dp'=8] {'chip','core'}, dimensions={0} | all-to-all | bytes 2359296 | tf_op jit(solution)/shard_map/all_to_all | solution.py:443
  104.4 8.8 %shard_map.123 = (f32[8,128]{1,0:T(8,128)S(1)}, f32[1024,128]{1,0:T(8,128)S(1)}, bf16[1024,128]{1,0:T(8,128)(2,1)S(1)}, f32[8,384]{1,0:T(8,128)S(1)}) custom-call(s32[2]{0:T(128)S(1)} %pad_add_fusion.place.refs_0_, bf16[64,72,128]{2,1,0:T(8,128)(2,1)S(1)} %all_to_all.25.refs_1_, bf16[64,72,128]{2,1,0:T(8,128)(2,1)S(1)} %all-to-all-done.got.refs_2_, ...), custom_call_target="tpu_custom_call" | custom-call | flops 3590324224 | bytes 8572936 | tf_op jit(solution)/shard_map/pallas_call | solution.py:47
  113.2 3.5 %collective-permute-start = (bf16[1024,128]{1,0:T(8,128)(2,1)S(1)}, bf16[1024,128]{1,0:T(8,128)(2,1)S(1)}, u32[]{:S(2)}, u32[]{:S(2)}) collective-permute-start(bf16[1024,128]{1,0:T(8,128)(2,1)S(1)} %get-tuple-element.27), channel_id=1, source_target_pairs={{0,8},{8,0},{1,9},{9,1},{2,10},{10,2},{3,11},{11,3},{4,12},{12,4},... | collective-permute-start | bytes 786440 | tf_op jit(solution)/shard_map/ppermute | solution.py:544
  116.6 1.1 collective-permute-done.refs_2_
  118.4 16.0 %all_to_all.26.got = bf16[32,32,128]{2,1,0:T(8,128)(2,1)S(1)} all-to-all(bf16[32,32,128]{2,1,0:T(8,128)(2,1)S(1)} %bitcast.8), channel_id=1, replica_groups=mesh['chip'=32,'core'=2,'dp'=8] {'chip'}, dimensions={0} | all-to-all | bytes 524288 | tf_op jit(solution)/shard_map/all_to_all | solution.py:443
  134.5 13.8 %all_to_all.27.got = bf16[8,32,128]{2,1,0:T(8,128)(2,1)S(1)} all-to-all(bf16[8,32,128]{2,1,0:T(8,128)(2,1)S(1)} %shard_map.125), channel_id=1, replica_groups=mesh['chip'=32,'core'=2,'dp'=8] {'dp'}, dimensions={0} | all-to-all | bytes 131072 | tf_op jit(solution)/shard_map/all_to_all | solution.py:443
  148.3 15.0 %all_to_all.28 = bf16[32,32,128]{2,1,0:T(8,128)(2,1)S(1)} all-to-all(bf16[32,32,128]{2,1,0:T(8,128)(2,1)S(1)} %shard_map.126), channel_id=1, replica_groups=mesh['chip'=32,'core'=2,'dp'=8] {'chip'}, dimensions={0} | all-to-all | bytes 524288 | tf_op jit(solution)/shard_map/all_to_all | solution.py:443
  163.3 6.0 %collective-permute-start.1 = (bf16[1024,128]{1,0:T(8,128)(2,1)S(1)}, bf16[1024,128]{1,0:T(8,128)(2,1)S(1)}, u32[]{:S(2)}, u32[]{:S(2)}) collective-permute-start(bf16[1024,128]{1,0:T(8,128)(2,1)S(1)} %bitcast.6), channel_id=1, source_target_pairs={{0,8},{8,0},{1,9},{9,1},{2,10},{10,2},{3,11},{11,3},{4,12},{12,4},... | collective-permute-start | bytes 786440 | tf_op jit(solution)/shard_map/ppermute | solution.py:556
  169.2 0.6 slice_reduce_fusion
  170.4 1.7 %shard_map.127 = (f32[512,384]{1,0:T(8,128)}, f32[1,384]{1,0:T(1,128)S(1)}, f32[384,128]{1,0:T(8,128)}) custom-call(s32[2]{0:T(128)S(1)} %pad_add_fusion.place.refs_0_, bf16[1024,128]{1,0:T(8,128)(2,1)S(1)} %bitcast.7, bf16[1024,128]{1,0:T(8,128)(2,1)S(1)} %collective-permute-done.1.other, f32[8,384]{1,0:T(8,128)S(1)} %get-tuple-element.28.base_row), custom_call_target="tpu_custom_call" | custom-call | bytes 1521160 | tf_op jit(solution)/shard_map/pallas_call | solution.py:47
  (28 shorter events, 1.9 us)
Async XLA Ops:
  1.3 1.0 copy-start
  2.3 0.9 copy-start.2
  3.3 0.9 copy-start.4
  4.2 0.7 copy-start.6
  4.8 0.7 copy-start.7
  5.5 0.7 copy-start.8
  10.4 15.1 %copy-start.1 = (bf16[512,384]{1,0:T(8,128)(2,1)S(1)}, bf16[512,384]{1,0:T(8,128)(2,1)}, u32[]{:S(2)}) copy-start(bf16[512,384]{1,0:T(8,128)(2,1)} %w_in.1) | copy-start | bytes 1179652
  10.4 15.1 %copy-start.3 = (bf16[8,32,512]{2,1,0:T(8,128)(2,1)S(1)}, bf16[8,32,512]{2,1,0:T(8,128)(2,1)}, u32[]{:S(2)}) copy-start(bf16[8,32,512]{2,1,0:T(8,128)(2,1)} %param.9) | copy-start | bytes 786436
  10.4 15.1 %copy-start.5 = (bf16[384,128]{1,0:T(8,128)(2,1)S(1)}, bf16[384,128]{1,0:T(8,128)(2,1)}, u32[]{:S(2)}) copy-start(bf16[384,128]{1,0:T(8,128)(2,1)} %refs_9_.1) | copy-start | bytes 294916
  10.4 15.0 %copy-start.9 = (bf16[8,128,512]{2,1,0:T(8,128)(2,1)S(1)}, bf16[8,128,512]{2,1,0:T(8,128)(2,1)}, u32[]{:S(2)}) copy-start(bf16[8,128,512]{2,1,0:T(8,128)(2,1)} %param.10) | copy-start | bytes 3145732
  10.4 45.6 %all-to-all-start = ((bf16[64,72,128]{2,1,0:T(8,128)(2,1)}), bf16[64,72,128]{2,1,0:T(8,128)(2,1)S(1)}, u32[]{:S(2)}, u32[]{:S(2)}) async-start(bf16[64,72,128]{2,1,0:T(8,128)(2,1)} %shard_map.120), calls=%async_computation | async-start | bytes 2359296 | tf_op jit(solution)/shard_map/all_to_all | solution.py:443
  25.4 30.6 %copy-start.10 = (s32[512]{0:T(512)S(1)}, s32[512]{0:T(512)}, u32[]{:S(2)}) copy-start(s32[512]{0:T(512)} %counts.1) | copy-start | bytes 6148
  27.9 1.3 copy-start.11
  29.2 1.0 copy-start.13
  56.0 48.4 %copy-start.14 = (bf16[1280,384]{1,0:T(8,128)(2,1)S(1)}, bf16[1280,384]{1,0:T(8,128)(2,1)}, u32[]{:S(2)}) copy-start(bf16[1280,384]{1,0:T(8,128)(2,1)} %copy-done.13) | copy-start | bytes 2949124
  67.2 37.2 %copy-start.12 = (f32[384,1280]{1,0:T(8,128)S(1)}, f32[384,1280]{1,0:T(8,128)}, u32[]{:S(2)}) copy-start(f32[384,1280]{1,0:T(8,128)} %copy-done.11) | copy-start | bytes 5898244
  113.2 4.6 %collective-permute-start = (bf16[1024,128]{1,0:T(8,128)(2,1)S(1)}, bf16[1024,128]{1,0:T(8,128)(2,1)S(1)}, u32[]{:S(2)}, u32[]{:S(2)}) collective-permute-start(bf16[1024,128]{1,0:T(8,128)(2,1)S(1)} %get-tuple-element.27), channel_id=1, source_target_pairs={{0,8},{8,0},{1,9},{9,1},{2,10},{10,2},{3,11},{11,3},{4,12},{12,4},... | collective-permute-start | bytes 786440 | tf_op jit(solution)/shard_map/ppermute | solution.py:544
  163.3 7.1 %collective-permute-start.1 = (bf16[1024,128]{1,0:T(8,128)(2,1)S(1)}, bf16[1024,128]{1,0:T(8,128)(2,1)S(1)}, u32[]{:S(2)}, u32[]{:S(2)}) collective-permute-start(bf16[1024,128]{1,0:T(8,128)(2,1)S(1)} %bitcast.6), channel_id=1, source_target_pairs={{0,8},{8,0},{1,9},{9,1},{2,10},{10,2},{3,11},{11,3},{4,12},{12,4},... | collective-permute-start | bytes 786440 | tf_op jit(solution)/shard_map/ppermute | solution.py:556

commit v3 on v2

--- a/solution.py
+++ b/solution.py
@@ -17,7 +17,8 @@
 FLOOR = -1e30
 GELU_A = math.sqrt(2.0 / math.pi)
 GELU_B = 0.044715
-GROUP = 4
+GROUP = 32
+WIDE = 64
 ARCHIVE = ("chip", "core")
 
 f32 = jnp.float32
@@ -39,7 +40,7 @@
     return hi, mid, (x - hi - mid).astype(bf16).astype(f32)
 
 
-def call(body, outs, args, smem_count, scratch=(), flops=0, transcendentals=0, where=pltpu.VMEM):
+def call(body, outs, args, smem_count, scratch=(), flops=0, transcendentals=0, where=pltpu.VMEM, limit=40 << 20):
     nbytes = sum(a.size * a.dtype.itemsize for a in list(args) + list(outs))
     vmem = pl.BlockSpec(memory_space=pltpu.VMEM)
     smem = pl.BlockSpec(memory_space=pltpu.SMEM)
@@ -50,7 +51,7 @@
         in_specs=[smem] * smem_count + [rest] * (len(args) - smem_count),
         out_specs=tuple(vmem for _ in outs),
         scratch_shapes=list(scratch),
-        compiler_params=pltpu.CompilerParams(vmem_limit_bytes=40 << 20),
+        compiler_params=pltpu.CompilerParams(vmem_limit_bytes=limit),
         cost_estimate=pl.CostEstimate(
             flops=flops, bytes_accessed=nbytes, transcendentals=transcendentals
         ),
@@ -63,14 +64,22 @@
 
 
 def ask_kernel(
-    mined, home, positive, x_hbm, w_in_hbm, bias_hbm, w_out_hbm, send, x, w_in, bias, w_out, vec, rid, code, count, goal, sems
+    mined_hbm, home_hbm, positive_hbm, x_hbm, w_in_hbm, bias_hbm, w_out_hbm, send, mined, home, positive, x, w_in, bias, w_out, vec, rid, code, count, goal, sems
 ):
     query_count, mined_count = mined.shape
     owner_count = send.shape[0]
     query_len = x.shape[0] // query_count
     line_count = home.shape[0] // owner_count
     rows = CAP * query_len
-    pairs = ((x_hbm, x), (w_in_hbm, w_in), (bias_hbm, bias), (w_out_hbm, w_out))
+    pairs = (
+        (mined_hbm, mined),
+        (home_hbm, home),
+        (positive_hbm, positive),
+        (x_hbm, x),
+        (w_in_hbm, w_in),
+        (bias_hbm, bias),
+        (w_out_hbm, w_out),
+    )
     copies = [pltpu.make_async_copy(a, b, sems.at[i]) for i, (a, b) in enumerate(pairs)]
     for copy in copies:
         copy.start()
@@ -83,6 +92,9 @@
         return carry
 
     lax.fori_loop(0, owner_count, clear, 0, unroll=8)
+    send[...] = jnp.zeros(send.shape, bf16)
+    for copy in copies[:3]:
+        copy.wait()
 
     def assign(query, carry):
         for j in range(mined_count):
@@ -96,7 +108,6 @@
         return carry
 
     lax.fori_loop(0, query_count, assign, 0)
-    send[...] = jnp.zeros(send.shape, bf16)
     sub = lax.broadcasted_iota(jnp.int32, (META, LANES), 0)
 
     def label(owner, carry):
@@ -109,9 +120,9 @@
         return carry
 
     lax.fori_loop(0, owner_count, label, 0, unroll=8)
-    for copy in copies:
+    for copy in copies[3:]:
         copy.wait()
-    _, hidden = gelu_parts(dot(x[...], w_in[...]) + bias[...])
+    _, hidden = gelu_parts(dot(x[...], w_in[...]) + bias[...].reshape(1, -1))
     vec[...] = dot(hidden, w_out[...]).astype(bf16)
 
     def place(query, carry):
@@ -125,7 +136,7 @@
     lax.fori_loop(0, query_count, place, 0)
 
 
-def head_kernel(xl, xq, w_in, bias, w_out, line_vec, hidden_all, slope_t, mean):
+def head_kernel(xl, xq, w_in, bias, w_out, line_vec, line_vec_t, hidden_all, slope_t, mean):
     step = 256
     line_frames = xl.shape[0]
     total = jnp.zeros((1, hidden_all.shape[1]), f32)
@@ -135,7 +146,7 @@
         else:
             x = xq[first - line_frames : first - line_frames + step, :]
         size = x.shape[0]
-        pre = dot(x, w_in[...]) + bias[...]
+        pre = dot(x, w_in[...]) + bias[...].reshape(1, -1)
         t, hidden = gelu_parts(pre)
         slope = 0.5 * (1.0 + t) + 0.5 * pre * (1.0 - t * t) * GELU_A * (
             1.0 + 3.0 * GELU_B * pre * pre
@@ -143,7 +154,11 @@
         hidden_all[first : first + size, :] = hidden
         slope_t[:, first : first + size] = slope.T
         if first < line_frames:
-            line_vec[first : first + size, :] = dot(hidden, w_out[...]).astype(bf16)
+            vec = dot(hidden, w_out[...])
+            for k in range(0, size, LANES):
+                line = (first + k) // LANES
+                line_vec[line] = vec[k : k + LANES].astype(bf16)
+                line_vec_t[line] = vec[k : k + LANES].T.astype(bf16)
             total += jnp.sum(hidden.astype(f32), axis=0, keepdims=True)
     mean[...] = jnp.zeros(mean.shape, f32)
     for i, k in enumerate(range(0, hidden_all.shape[1], LANES)):
@@ -158,81 +173,70 @@
     return jnp.concatenate(parts, axis=0)
 
 
-def match_kernel(place, counts, got, line_vec, mean, send, weights, own):
+def match_kernel(
+    place, counts, got, line_vec, line_vec_t, mean, send, weights, own, pads, label_rows, ids, sums, sem
+):
     owner_count = got.shape[0]
     rows = got.shape[1] - META
+    group = min(GROUP, owner_count)
     query_len = rows // CAP
-    line_total = line_vec.shape[0]
-    line_count = line_total // LANES
-    scale = SCORE_SCALE / math.sqrt(line_vec.shape[1])
-    lines = line_vec[...]
+    line_count, _, vec_width = line_vec.shape
+    scale = SCORE_SCALE / math.sqrt(vec_width)
+    shape3 = (owner_count, META, LANES)
+    lane3 = lax.broadcasted_iota(jnp.int32, shape3, 2)
+    sub3 = lax.broadcasted_iota(jnp.int32, shape3, 1)
+    owner3 = lax.broadcasted_iota(jnp.int32, shape3, 0)
     lane1 = lax.broadcasted_iota(jnp.int32, (1, LANES), 1)
-    pads = [
-        jnp.where(lane1 < counts[place[0] * line_count + r], 0.0, FLOOR) for r in range(line_count)
-    ]
-    total = GROUP * rows
-    lane = lax.broadcasted_iota(jnp.int32, (total, LANES), 1)
-    row = lax.broadcasted_iota(jnp.int32, (total, LANES), 0)
-    target = row // rows + HALF * ((row // query_len) % CAP)
+    sub = lax.broadcasted_iota(jnp.int32, (META, LANES), 0)
+    meta = got[:, rows : rows + META, :].astype(f32)
+    labels = jnp.sum(jnp.where(lane3 == owner3 + HALF * (sub3 % CAP), meta, 0.0), axis=0)
+    covered = lane1 % HALF < owner_count
+    rid_row = labels[0:1] + labels[1:2]
+    rid_row = jnp.where(covered & (rid_row < line_count), rid_row, 0.0)
+    code_row = jnp.where(covered, labels[2:3] + labels[3:4], UNUSED)
+    label_rows[...] = jnp.broadcast_to(rid_row, (META, LANES)).astype(jnp.int32)
+    copy = pltpu.make_async_copy(label_rows, ids, sem)
+    copy.start()
+    for r in range(line_count):
+        pads[r : r + 1, :] = jnp.where(lane1 < counts[place[0] * line_count + r], 0.0, FLOOR)
+    sums[...] = jnp.zeros(sums.shape, f32)
+    copy.wait()
 
     def step(g, carry):
-        match_row, code_row = carry
-        first = g * GROUP
-        queries = got[pl.ds(first, GROUP), 0:rows, :].reshape(total, LANES)
-        meta = got[pl.ds(first, GROUP), rows : rows + META, :].astype(f32)
-        rid = spread(meta, 0, query_len)
-        logits = dot(queries, lines, 1, 1) * scale
-        chosen = jnp.zeros((total, LANES), f32)
-        for r in range(line_count):
-            part = logits[:, r * LANES : (r + 1) * LANES] + pads[r]
-            chosen = jnp.where(rid == r, part, chosen)
-        peak = jnp.max(chosen, axis=1, keepdims=True)
-        scaled = jnp.exp(chosen - peak)
-        totals = jnp.sum(scaled, axis=1, keepdims=True)
-        log_total = peak + jnp.log(totals)
-        weight = (scaled * (1.0 / totals)).astype(bf16)
-        weights[pl.ds(first, GROUP)] = weight.reshape(GROUP, rows, LANES)
-        rid_b = rid.astype(bf16)
-        zero = jnp.zeros((total, LANES), bf16)
-        wide = jnp.concatenate(
-            [jnp.where(rid_b == r, weight, zero) for r in range(line_count)], axis=1
-        )
-        send[pl.ds(first, GROUP), 0:rows, :] = (
-            dot(wide, lines).astype(bf16).reshape(GROUP, rows, LANES)
-        )
-        mine = (lane == target + first) & (rid < line_count)
-        match_row += jnp.sum(
-            jnp.where(mine, log_total * (1.0 / query_len), 0.0), axis=0, keepdims=True
-        )
-        for b in range(GROUP):
+        first = g * group
+        for b in range(group):
             for c in range(CAP):
-                code_row = jnp.where(
-                    lane1 == first + b + HALF * c, meta[b, 2 + c : 3 + c, :], code_row
-                )
-        return match_row, code_row
-
-    match_row, code_row = lax.fori_loop(
-        0,
-        owner_count // GROUP,
-        step,
-        (jnp.zeros((1, LANES), f32), jnp.full((1, LANES), UNUSED, f32)),
-        unroll=2,
-    )
-    sub = lax.broadcasted_iota(jnp.int32, (META, LANES), 0)
+                slot = first + b + HALF * c
+                r = ids[0, slot]
+                span = pl.ds(c * query_len, query_len)
+                logits = dot(got[first + b, span, :], line_vec_t[r]) * scale
+                logits = logits + pads[pl.ds(r, 1), :]
+                peak = jnp.max(logits, axis=1, keepdims=True)
+                scaled = jnp.exp(logits - peak)
+                totals = jnp.sum(scaled, axis=1, keepdims=True)
+                log_total = peak + jnp.log(totals)
+                weight = (scaled * (1.0 / totals)).astype(bf16)
+                weights[first + b, span, :] = weight
+                send[first + b, span, :] = dot(weight, line_vec[r]).astype(bf16)
+                mean_log = jnp.sum(log_total, axis=0, keepdims=True) * (1.0 / query_len)
+                sums[pl.ds(slot, 1), :] = jnp.broadcast_to(mean_log, (1, LANES))
+        return carry
+
+    lax.fori_loop(0, owner_count // group, step, 0)
+    lane = lax.broadcasted_iota(jnp.int32, sums.shape, 1)
+    row = lax.broadcasted_iota(jnp.int32, sums.shape, 0)
+    match_row = jnp.sum(jnp.where(lane == row, sums[...], 0.0), axis=0, keepdims=True)
     own[...] = jnp.where(sub == 0, match_row, code_row)
-    high = match_row.astype(bf16).astype(f32)
-    middle = (match_row - high).astype(bf16).astype(f32)
-    low = match_row - high - middle
-    tile = jnp.where(
-        sub == 0, high, jnp.where(sub == 1, middle, jnp.where(sub == 2, low, code_row))
-    )
-    tile = jnp.where(sub < 4, tile, mean[...]).astype(bf16)
+    tile = mean[...]
+    for p, part in enumerate(split3(match_row)):
+        tile = jnp.where(sub == p, part, tile)
+    tile = jnp.where(sub == 3, code_row, tile).astype(bf16)
 
     def label(b, carry):
         send[b, rows : rows + META, :] = tile
         return carry
 
-    lax.fori_loop(0, owner_count, label, 0)
+    lax.fori_loop(0, owner_count, label, 0, unroll=8)
 
 
 def grad_kernel(
@@ -240,6 +244,7 @@
 ):
     owner_count = got.shape[0]
     rows = got.shape[1] - META
+    wide_count = min(WIDE, owner_count)
     query_len = rows // CAP
     line_total = xl.shape[0]
     line_count = line_total // LANES
@@ -297,7 +302,7 @@
         jnp.sum(jnp.where(aim, both, 0.0), axis=2, keepdims=True), shape3
     )
 
-    size = GROUP * rows
+    size = wide_count * rows
     line_acc[...] = jnp.zeros(line_acc.shape, f32)
     query_acc[...] = jnp.zeros(query_acc.shape, f32)
     frame = (lax.broadcasted_iota(jnp.int32, (size, LANES), 0) % query_len).astype(f32)
@@ -306,22 +311,22 @@
     one = jnp.ones((size, LANES), bf16)
 
     def step(g, carry):
-        first = g * GROUP
-        queries = got[pl.ds(first, GROUP), 0:rows, :].reshape(size, LANES)
-        rid = spread(got[pl.ds(first, GROUP), rows : rows + META, :].astype(f32), 0, query_len)
+        first = g * wide_count
+        queries = got[pl.ds(first, wide_count), 0:rows, :].reshape(size, LANES)
+        rid = spread(got[pl.ds(first, wide_count), rows : rows + META, :].astype(f32), 0, query_len)
         rid = rid.astype(bf16)
-        scale = spread(own_scale[pl.ds(first, GROUP)], 0, query_len)
-        weight = weights[pl.ds(first, GROUP)].reshape(size, LANES).astype(f32)
+        scale = spread(own_scale[pl.ds(first, wide_count)], 0, query_len)
+        weight = weights[pl.ds(first, wide_count)].reshape(size, LANES).astype(f32)
         score = (weight * scale).astype(bf16)
         wide = jnp.concatenate(
             [jnp.where(rid == r, score, zero) for r in range(line_count)], axis=1
         )
         line_acc[...] += dot(queries, wide, 0, 0)
 
-        labels = ask_scale[pl.ds(first, GROUP)]
+        labels = ask_scale[pl.ds(first, wide_count)]
         scale = spread(labels, 0, query_len)
         target = spread(labels, CAP, query_len) * float(query_len) + frame
-        pulled = back[pl.ds(first, GROUP), 0:rows, :].reshape(size, LANES).astype(f32)
+        pulled = back[pl.ds(first, wide_count), 0:rows, :].reshape(size, LANES).astype(f32)
         pulled = (pulled * scale).astype(bf16)
         wide = jnp.concatenate(
             [
@@ -333,7 +338,7 @@
         query_acc[...] += dot(pulled, wide, 0, 0)
         return carry
 
-    lax.fori_loop(0, owner_count // GROUP, step, 0)
+    lax.fori_loop(0, owner_count // wide_count, step, 0)
 
     grad_in = None
     grad_out = None
@@ -402,13 +407,15 @@
         send[first:, :] = tail_tile(values, tail_rows).astype(bf16)
 
 
-def sum_kernel(got, send):
-    part = got[0].astype(f32)
-    for k in range(1, got.shape[0]):
-        part = part + got[k].astype(f32)
-    part = part.astype(bf16)
-    for k in range(send.shape[0]):
-        send[k] = part
+def sum_kernel(got, send, *, share):
+    rows = got.shape[0]
+    block = max(share, META)
+    part = jnp.sum(got[...].astype(f32).reshape(rows // block, block, LANES), axis=0)
+    if share < block:
+        part = sum(part[i : i + share] for i in range(0, block, share))
+        part = jnp.concatenate([part] * (block // share), axis=0)
+    part = jnp.broadcast_to(part[None], (rows // block, block, LANES)).reshape(rows, LANES)
+    send[...] = part.astype(bf16)
 
 
 def unpack_kernel(place, mine, other, base_row, grad_in, grad_bias, grad_out, got):
@@ -435,7 +442,7 @@
         base_rows = base_row[:, k : k + LANES].astype(bf16)
         outer = dot(base_rows, vec_rows, 0, 0)
         grad_out[k : k + LANES, :] = got[base : base + vec_width, :].astype(f32).T + outer
-        grad_bias[0:1, k : k + LANES] = values[i]
+        grad_bias[k : k + LANES] = values[i].reshape(LANES)
         base += vec_width
 
 
@@ -461,7 +468,6 @@
     rows = CAP * query_len
     xq = query_frames.reshape(frames_q, feat)
     xl = line_frames.reshape(frames_l, feat)
-    bias = bias_in.reshape(1, hid)
     place = jnp.stack([lax.axis_index(ARCHIVE), lax.axis_index("core")]).astype(jnp.int32)
     wire = shape_of((owner_count, rows + META, vec_width), bf16)
     head_flops = 2 * hid * (feat + vec_width)
@@ -469,33 +475,38 @@
     (asked,) = call(
         ask_kernel,
         [wire],
-        [mined, line_home, positive, xq, w_in, bias, w_out],
-        3,
+        [mined, line_home, positive, xq, w_in, bias_in, w_out],
+        0,
         [
+            pltpu.SMEM(mined.shape, jnp.int32),
+            pltpu.SMEM(line_home.shape, jnp.int32),
+            pltpu.SMEM(positive.shape, jnp.int32),
             pltpu.VMEM(xq.shape, bf16),
             pltpu.VMEM(w_in.shape, bf16),
-            pltpu.VMEM(bias.shape, f32),
+            pltpu.VMEM(bias_in.shape, f32),
             pltpu.VMEM(w_out.shape, bf16),
             pltpu.VMEM((frames_q, vec_width), bf16),
             pltpu.SMEM((CAP, owner_count), jnp.int32),
             pltpu.SMEM((CAP, owner_count), jnp.int32),
             pltpu.SMEM((owner_count,), jnp.int32),
             pltpu.SMEM(mined.shape, jnp.int32),
-            pltpu.SemaphoreType.DMA((4,)),
+            pltpu.SemaphoreType.DMA((7,)),
         ],
         flops=frames_q * head_flops,
-        where=pl.ANY,
+        where=pltpu.HBM,
+        limit=63 << 20,
     )
     got = exchange(asked, ARCHIVE)
-    line_vec, hidden_all, slope_t, mean = call(
+    line_vec, line_vec_t, hidden_all, slope_t, mean = call(
         head_kernel,
         [
-            shape_of((frames_l, vec_width), bf16),
+            shape_of((line_count, line_len, vec_width), bf16),
+            shape_of((line_count, vec_width, line_len), bf16),
             shape_of((frames, hid), bf16),
             shape_of((hid, frames), f32),
             shape_of((META, LANES), f32),
         ],
-        [xl, xq, w_in, bias, w_out],
+        [xl, xq, w_in, bias_in, w_out],
         0,
         flops=frames * head_flops,
         transcendentals=frames * hid,
@@ -508,8 +519,15 @@
             shape_of((owner_count, rows, line_len), bf16),
             shape_of((META, LANES), f32),
         ],
-        [place, frame_count, got, line_vec, mean],
+        [place, frame_count, got, line_vec, line_vec_t, mean],
         2,
+        [
+            pltpu.VMEM((line_count, LANES), f32),
+            pltpu.VMEM((META, LANES), jnp.int32),
+            pltpu.SMEM((META, LANES), jnp.int32),
+            pltpu.VMEM((LANES, LANES), f32),
+            pltpu.SemaphoreType.DMA(()),
+        ],
         flops=2 * match_flops,
     )
     back = exchange(answer, ARCHIVE)
@@ -540,7 +558,8 @@
         flops=match_flops + 4 * frames * head_flops,
     )
     swap = [(0, 1), (1, 0)]
-    share = half // chip_count
+    peers = chip_count * dp_count
+    share = half // peers
     taken = lax.ppermute(give, "core", swap)
     tail_rows = flat_rows - (feat + vec_width) * hid // LANES
 
@@ -548,20 +567,23 @@
         sum_core_kernel(*refs, tail_rows=tail_rows, tail_count=hid // LANES + 1)
 
     (part,) = call(sum_core_body, [shape_of((half, LANES), bf16)], [place, keep, taken], 1)
-    parts = exchange(part.reshape(chip_count, share, LANES), "chip")
-    (part,) = call(sum_kernel, [shape_of((dp_count, share, LANES), bf16)], [parts], 0)
-    parts = exchange(part, "dp")
-    (part,) = call(sum_kernel, [shape_of((chip_count, share, LANES), bf16)], [parts], 0)
-    mine = exchange(part, "chip").reshape(half, LANES)
+    spread_out = ("chip", "dp")
+    parts = exchange(part.reshape(peers, share, LANES), spread_out).reshape(half, LANES)
+
+    def sum_body(*refs):
+        sum_kernel(*refs, share=share)
+
+    (part,) = call(sum_body, [shape_of((half, LANES), bf16)], [parts], 0)
+    mine = exchange(part.reshape(peers, share, LANES), spread_out).reshape(half, LANES)
     other = lax.ppermute(mine, "core", swap)
     grad_in, grad_bias, grad_out = call(
         unpack_kernel,
-        [shape_of((feat, hid), f32), shape_of((1, hid), f32), shape_of((hid, vec_width), f32)],
+        [shape_of((feat, hid), f32), shape_of((hid,), f32), shape_of((hid, vec_width), f32)],
         [place, mine, other, base_row],
         1,
         [pltpu.VMEM((flat_rows, LANES), bf16)],
     )
-    return (loss[:query_count, 0], grad_in, grad_bias.reshape(hid), grad_out)
+    return (loss[:query_count, 0], grad_in, grad_bias, grad_out)
 
 
 def solution(mesh):

time: 173 us -> 163 us (0.942)
  Pallas kernels: 29 us -> 20.1 us
  blocking collectives: 82 us -> 87.8 us
  local copies, waits for them, and re-layouts: 8.48 us -> 2.96 us
    pallas_call x8 -> x7, Pallas kernels: 29 us -> 20.1 us  [call(): pl.pallas_call(body, out_shape=tuple(outs), in_specs=[smem] * smem_count...]
    all_to_all x4 -> x3, blocking collectives: 82 us -> 87.8 us  [exchange(): return lax.all_to_all(x, axis, split_axis=0, concat_axis=0, tiled=True)]
    unnamed x30 -> x20, local copies, waits for them, and re-layouts: 7.17 us -> 2.33 us
  transfers between devices with their start and end apart: 3 -> 3, of which waited for: 3 -> 3; matrix products, arithmetic and copies ran while one was open for 0% -> 0% of each run, Pallas kernels for 1% -> 2%
where the time goes in v3:
time: 163 us
  blocking collectives  87.8 us (54%)
  waiting for transfers between devices  27.4 us (17%)
  starting transfers between devices  23.6 us (14%)
  Pallas kernels  20.1 us (12%)
  local copies, waits for them, and re-layouts  2.96 us (2%)
    all_to_all x3, blocking collectives, exchange(): return lax.all_to_all(x, axis, split_axis=0, concat_axis=0, tiled=True)  87.8 us
    all_to_all x1, waiting for transfers between devices, exchange(): return lax.all_to_all(x, axis, split_axis=0, concat_axis=0, tiled=True)  25.7 us
    pallas_call x7, Pallas kernels, call(): pl.pallas_call(body, out_shape=tuple(outs), in_specs=[smem] * smem_count...  20.1 us
    all_to_all x1, starting transfers between devices, exchange(): return lax.all_to_all(x, axis, split_axis=0, concat_axis=0, tiled=True)  15 us
    ppermute x1, starting transfers between devices, local(): other = lax.ppermute(mine, 'core', swap)  5.14 us
    ppermute x1, starting transfers between devices, local(): taken = lax.ppermute(give, 'core', swap)  3.46 us
  transfers between devices with their start and end apart: 3, of which 3 were waited for; matrix products, arithmetic and copies ran while one was open for 0% of the time, Pallas kernels for 2%

profile of v3, /device:TPU:1, one launch (start us, length us, event | category | flops | bytes accessed | tf_op | source)
XLA Modules:
  0.0 162.7 jit_solution(17817868269870652032)
XLA Ops:
  0.6 3.5 %shard_map.120 = bf16[64,72,128]{2,1,0:T(8,128)(2,1)} custom-call(s32[8,6]{1,0:T(8,128)} %mined_hbm.1, s32[512]{0:T(512)} %home_hbm.1, s32[8]{0:T(128)} %positive_hbm.1, bf16[256,512]{1,0:T(8,128)(2,1)} %bitcast.13, bf16[512,384]{1,0:T(8,128)(2,1)} %w_in.1, f32[384]{0:T(512)} %bias.1, bf16[384,128]{1,0:T(8,128)(2,1)} %refs_9_.1), custom_call_target="tpu_custom_call" | custom-call | flops 125829120 | bytes 1937120 | tf_op jit(solution)/shard_map/pallas_call | solution.py:48
  4.2 0.0 copy-start
  4.2 0.0 copy-start.1
  4.2 0.0 copy-start.2
  4.2 15.0 %all-to-all-start = ((bf16[64,72,128]{2,1,0:T(8,128)(2,1)}), bf16[64,72,128]{2,1,0:T(8,128)(2,1)S(1)}, u32[]{:S(2)}, u32[]{:S(2)}) async-start(bf16[64,72,128]{2,1,0:T(8,128)(2,1)} %shard_map.120), calls=%async_computation | async-start | bytes 2359296 | tf_op jit(solution)/shard_map/all_to_all | solution.py:450
  19.2 0.0 copy-start.5
  19.3 2.4 %shard_map.121 = (bf16[8,128,128]{2,1,0:T(8,128)(2,1)S(1)}, bf16[8,128,128]{2,1,0:T(8,128)(2,1)S(1)}, bf16[1280,384]{1,0:T(8,128)(2,1)S(1)}, f32[384,1280]{1,0:T(8,128)S(1)}, f32[8,128]{1,0:T(8,128)S(1)}) custom-call(bf16[1024,512]{1,0:T(8,128)(2,1)S(1)} %bitcast.16, bf16[256,512]{1,0:T(8,128)(2,1)S(1)} %bitcast.14, bf16[512,384]{1,0:T(8,128)(2,1)S(1)} %copy-done, ...), custom_call_target="tpu_custom_call" | custom-call | flops 629145600 | bytes 5281280 | tf_op jit(solution)/shard_map/pallas_call | solution.py:48
  21.8 1.3 copy-done.6
  23.1 1.0 copy-done.8
  24.0 0.1 pad_add_fusion.place.refs_0_
  24.1 25.7 %all-to-all-done.got.refs_2_ = bf16[64,72,128]{2,1,0:T(8,128)(2,1)S(1)} async-done(((bf16[64,72,128]{2,1,0:T(8,128)(2,1)}), bf16[64,72,128]{2,1,0:T(8,128)(2,1)S(1)}, u32[]{:S(2)}, u32[]{:S(2)}) %all-to-all-start) | async-done | bytes 1179680 | tf_op jit(solution)/shard_map/all_to_all | solution.py:450
  49.8 5.8 %shard_map.122 = (bf16[64,72,128]{2,1,0:T(8,128)(2,1)S(1)}, bf16[64,64,128]{2,1,0:T(8,128)(2,1)S(1)}, f32[8,128]{1,0:T(8,128)S(1)}) custom-call(s32[2]{0:T(128)S(1)} %pad_add_fusion.place.refs_0_, s32[512]{0:T(512)S(1)} %copy-done.5, bf16[64,72,128]{2,1,0:T(8,128)(2,1)S(1)} %all-to-all-done.got.refs_2_, bf16[8,128,128]{2,1,0:T(8,128)(2,1)S(1)} %get-tuple-element.19.line_vec, ...), custom_call_target="tpu_custom_call" | custom-call | flops 2147483648 | bytes 3942408 | tf_op jit(solution)/shard_map/pallas_call | solution.py:48
  55.7 37.2 %all_to_all.20.refs_1_ = bf16[64,72,128]{2,1,0:T(8,128)(2,1)S(1)} all-to-all(bf16[64,72,128]{2,1,0:T(8,128)(2,1)S(1)} %get-tuple-element.22), channel_id=1, replica_groups=mesh['chip'=32,'core'=2,'dp'=8] {'chip','core'}, dimensions={0} | all-to-all | bytes 2359296 | tf_op jit(solution)/shard_map/all_to_all | solution.py:450
  92.9 5.8 %shard_map.123 = (f32[8,128]{1,0:T(8,128)S(1)}, f32[1024,128]{1,0:T(8,128)S(1)}, bf16[1024,128]{1,0:T(8,128)(2,1)S(1)}, f32[8,384]{1,0:T(8,128)S(1)}) custom-call(s32[2]{0:T(128)S(1)} %pad_add_fusion.place.refs_0_, bf16[64,72,128]{2,1,0:T(8,128)(2,1)S(1)} %all_to_all.20.refs_1_, bf16[64,72,128]{2,1,0:T(8,128)(2,1)S(1)} %all-to-all-done.got.refs_2_, ...), custom_call_target="tpu_custom_call" | custom-call | flops 3590324224 | bytes 8572936 | tf_op jit(solution)/shard_map/pallas_call | solution.py:48
  98.6 3.5 %collective-permute-start = (bf16[1024,128]{1,0:T(8,128)(2,1)S(1)}, bf16[1024,128]{1,0:T(8,128)(2,1)S(1)}, u32[]{:S(2)}, u32[]{:S(2)}) collective-permute-start(bf16[1024,128]{1,0:T(8,128)(2,1)S(1)} %get-tuple-element.29), channel_id=1, source_target_pairs={{0,8},{8,0},{1,9},{9,1},{2,10},{10,2},{3,11},{11,3},{4,12},{12,4},... | collective-permute-start | bytes 786440 | tf_op jit(solution)/shard_map/ppermute | solution.py:563
  102.1 1.1 collective-permute-done.refs_2_
  103.2 0.6 shard_map.124
  103.8 28.5 %all_to_all.21 = bf16[256,4,128]{2,1,0:T(4,128)(2,1)S(1)} all-to-all(bf16[256,4,128]{2,1,0:T(4,128)(2,1)S(1)} %bitcast.12), channel_id=1, replica_groups=mesh['chip'=32,'core'=2,'dp'=8] {'chip','dp'}, dimensions={0} | all-to-all | bytes 524288 | tf_op jit(solution)/shard_map/all_to_all | solution.py:450
  132.3 0.2 shard_map.125
  132.5 22.2 %all_to_all.22 = bf16[256,4,128]{2,1,0:T(4,128)(2,1)S(1)} all-to-all(bf16[256,4,128]{2,1,0:T(4,128)(2,1)S(1)} %bitcast.11), channel_id=1, replica_groups=mesh['chip'=32,'core'=2,'dp'=8] {'chip','dp'}, dimensions={0} | all-to-all | bytes 524288 | tf_op jit(solution)/shard_map/all_to_all | solution.py:450
  154.7 5.1 %collective-permute-start.1 = (bf16[1024,128]{1,0:T(8,128)(2,1)S(1)}, bf16[1024,128]{1,0:T(8,128)(2,1)S(1)}, u32[]{:S(2)}, u32[]{:S(2)}) collective-permute-start(bf16[1024,128]{1,0:T(8,128)(2,1)S(1)} %bitcast.8), channel_id=1, source_target_pairs={{0,8},{8,0},{1,9},{9,1},{2,10},{10,2},{3,11},{11,3},{4,12},{12,4},... | collective-permute-start | bytes 786440 | tf_op jit(solution)/shard_map/ppermute | solution.py:578
  159.8 0.6 slice_reduce_fusion
  160.5 0.5 collective-permute-done.1.other
  161.0 1.7 %shard_map.126 = (f32[512,384]{1,0:T(8,128)}, f32[384]{0:T(512)}, f32[384,128]{1,0:T(8,128)}) custom-call(s32[2]{0:T(128)S(1)} %pad_add_fusion.place.refs_0_, bf16[1024,128]{1,0:T(8,128)(2,1)S(1)} %bitcast.9, bf16[1024,128]{1,0:T(8,128)(2,1)S(1)} %collective-permute-done.1.other, f32[8,384]{1,0:T(8,128)S(1)} %get-tuple-element.30.base_row), custom_call_target="tpu_custom_call" | custom-call | bytes 1521160 | tf_op jit(solution)/shard_map/pallas_call | solution.py:48
  (14 shorter events, 0.0 us)
Async XLA Ops:
  4.2 15.1 %copy-start = (bf16[512,384]{1,0:T(8,128)(2,1)S(1)}, bf16[512,384]{1,0:T(8,128)(2,1)}, u32[]{:S(2)}) copy-start(bf16[512,384]{1,0:T(8,128)(2,1)} %w_in.1) | copy-start | bytes 1179652
  4.2 15.1 %copy-start.1 = (bf16[8,32,512]{2,1,0:T(8,128)(2,1)S(1)}, bf16[8,32,512]{2,1,0:T(8,128)(2,1)}, u32[]{:S(2)}) copy-start(bf16[8,32,512]{2,1,0:T(8,128)(2,1)} %param.9) | copy-start | bytes 786436
  4.2 15.1 %copy-start.2 = (bf16[384,128]{1,0:T(8,128)(2,1)S(1)}, bf16[384,128]{1,0:T(8,128)(2,1)}, u32[]{:S(2)}) copy-start(bf16[384,128]{1,0:T(8,128)(2,1)} %refs_9_.1) | copy-start | bytes 294916
  4.2 15.1 %copy-start.3 = (f32[384]{0:T(512)S(1)}, f32[384]{0:T(512)}, u32[]{:S(2)}) copy-start(f32[384]{0:T(512)} %bias.1) | copy-start | bytes 4612
  4.2 15.1 %copy-start.4 = (bf16[8,128,512]{2,1,0:T(8,128)(2,1)S(1)}, bf16[8,128,512]{2,1,0:T(8,128)(2,1)}, u32[]{:S(2)}) copy-start(bf16[8,128,512]{2,1,0:T(8,128)(2,1)} %param.10) | copy-start | bytes 3145732
  4.2 45.6 %all-to-all-start = ((bf16[64,72,128]{2,1,0:T(8,128)(2,1)}), bf16[64,72,128]{2,1,0:T(8,128)(2,1)S(1)}, u32[]{:S(2)}, u32[]{:S(2)}) async-start(bf16[64,72,128]{2,1,0:T(8,128)(2,1)} %shard_map.120), calls=%async_computation | async-start | bytes 2359296 | tf_op jit(solution)/shard_map/all_to_all | solution.py:450
  19.2 30.6 %copy-start.5 = (s32[512]{0:T(512)S(1)}, s32[512]{0:T(512)}, u32[]{:S(2)}) copy-start(s32[512]{0:T(512)} %counts.1) | copy-start | bytes 6148
  21.8 1.3 copy-start.6
  23.1 1.0 copy-start.8
  49.8 43.0 %copy-start.9 = (bf16[1280,384]{1,0:T(8,128)(2,1)S(1)}, bf16[1280,384]{1,0:T(8,128)(2,1)}, u32[]{:S(2)}) copy-start(bf16[1280,384]{1,0:T(8,128)(2,1)} %copy-done.8) | copy-start | bytes 2949124
  55.7 37.2 %copy-start.7 = (f32[384,1280]{1,0:T(8,128)S(1)}, f32[384,1280]{1,0:T(8,128)}, u32[]{:S(2)}) copy-start(f32[384,1280]{1,0:T(8,128)} %copy-done.6) | copy-start | bytes 5898244
  98.6 4.6 %collective-permute-start = (bf16[1024,128]{1,0:T(8,128)(2,1)S(1)}, bf16[1024,128]{1,0:T(8,128)(2,1)S(1)}, u32[]{:S(2)}, u32[]{:S(2)}) collective-permute-start(bf16[1024,128]{1,0:T(8,128)(2,1)S(1)} %get-tuple-element.29), channel_id=1, source_target_pairs={{0,8},{8,0},{1,9},{9,1},{2,10},{10,2},{3,11},{11,3},{4,12},{12,4},... | collective-permute-start | bytes 786440 | tf_op jit(solution)/shard_map/ppermute | solution.py:563
  154.7 6.3 %collective-permute-start.1 = (bf16[1024,128]{1,0:T(8,128)(2,1)S(1)}, bf16[1024,128]{1,0:T(8,128)(2,1)S(1)}, u32[]{:S(2)}, u32[]{:S(2)}) collective-permute-start(bf16[1024,128]{1,0:T(8,128)(2,1)S(1)} %bitcast.8), channel_id=1, source_target_pairs={{0,8},{8,0},{1,9},{9,1},{2,10},{10,2},{3,11},{11,3},{4,12},{12,4},... | collective-permute-start | bytes 786440 | tf_op jit(solution)/shard_map/ppermute | solution.py:578

commit v4 on v3

--- a/solution.py
+++ b/solution.py
@@ -17,7 +17,7 @@
 FLOOR = -1e30
 GELU_A = math.sqrt(2.0 / math.pi)
 GELU_B = 0.044715
-GROUP = 32
+GROUP = 64
 WIDE = 64
 ARCHIVE = ("chip", "core")
 
@@ -201,6 +201,7 @@
         pads[r : r + 1, :] = jnp.where(lane1 < counts[place[0] * line_count + r], 0.0, FLOOR)
     sums[...] = jnp.zeros(sums.shape, f32)
     copy.wait()
+    ones = jnp.ones((LANES, LANES), bf16)
 
     def step(g, carry):
         first = g * group
@@ -213,13 +214,15 @@
                 logits = logits + pads[pl.ds(r, 1), :]
                 peak = jnp.max(logits, axis=1, keepdims=True)
                 scaled = jnp.exp(logits - peak)
-                totals = jnp.sum(scaled, axis=1, keepdims=True)
+                scaled = scaled.astype(bf16)
+                both = dot(scaled, jnp.concatenate([line_vec[r], ones], axis=1))
+                totals = both[:, vec_width:]
+                inverse = 1.0 / totals
+                weights[first + b, span, :] = (scaled.astype(f32) * inverse).astype(bf16)
+                send[first + b, span, :] = (both[:, :vec_width] * inverse).astype(bf16)
                 log_total = peak + jnp.log(totals)
-                weight = (scaled * (1.0 / totals)).astype(bf16)
-                weights[first + b, span, :] = weight
-                send[first + b, span, :] = dot(weight, line_vec[r]).astype(bf16)
                 mean_log = jnp.sum(log_total, axis=0, keepdims=True) * (1.0 / query_len)
-                sums[pl.ds(slot, 1), :] = jnp.broadcast_to(mean_log, (1, LANES))
+                sums[pl.ds(slot, 1), :] = mean_log
         return carry
 
     lax.fori_loop(0, owner_count // group, step, 0)
@@ -407,15 +410,10 @@
         send[first:, :] = tail_tile(values, tail_rows).astype(bf16)
 
 
-def sum_kernel(got, send, *, share):
-    rows = got.shape[0]
-    block = max(share, META)
-    part = jnp.sum(got[...].astype(f32).reshape(rows // block, block, LANES), axis=0)
-    if share < block:
-        part = sum(part[i : i + share] for i in range(0, block, share))
-        part = jnp.concatenate([part] * (block // share), axis=0)
-    part = jnp.broadcast_to(part[None], (rows // block, block, LANES)).reshape(rows, LANES)
-    send[...] = part.astype(bf16)
+def sum_kernel(got, send):
+    part = jnp.sum(got[...].astype(f32), axis=0).astype(bf16)
+    for k in range(send.shape[0]):
+        send[k] = part
 
 
 def unpack_kernel(place, mine, other, base_row, grad_in, grad_bias, grad_out, got):
@@ -558,8 +556,7 @@
         flops=match_flops + 4 * frames * head_flops,
     )
     swap = [(0, 1), (1, 0)]
-    peers = chip_count * dp_count
-    share = half // peers
+    share = half // chip_count
     taken = lax.ppermute(give, "core", swap)
     tail_rows = flat_rows - (feat + vec_width) * hid // LANES
 
@@ -567,14 +564,11 @@
         sum_core_kernel(*refs, tail_rows=tail_rows, tail_count=hid // LANES + 1)
 
     (part,) = call(sum_core_body, [shape_of((half, LANES), bf16)], [place, keep, taken], 1)
-    spread_out = ("chip", "dp")
-    parts = exchange(part.reshape(peers, share, LANES), spread_out).reshape(half, LANES)
-
-    def sum_body(*refs):
-        sum_kernel(*refs, share=share)
-
-    (part,) = call(sum_body, [shape_of((half, LANES), bf16)], [parts], 0)
-    mine = exchange(part.reshape(peers, share, LANES), spread_out).reshape(half, LANES)
+    parts = exchange(part.reshape(chip_count, share, LANES), "chip")
+    (part,) = call(sum_kernel, [shape_of((dp_count, share, LANES), bf16)], [parts], 0)
+    parts = exchange(part, "dp")
+    (part,) = call(sum_kernel, [shape_of((chip_count, share, LANES), bf16)], [parts], 0)
+    mine = exchange(part, "chip").reshape(half, LANES)
     other = lax.ppermute(mine, "core", swap)
     grad_in, grad_bias, grad_out = call(
         unpack_kernel,

time: 163 us -> 156 us (0.957)
  blocking collectives: 87.8 us -> 82 us
  Pallas kernels: 20.1 us -> 18 us
    all_to_all x3 -> x4, blocking collectives: 87.8 us -> 82 us  [exchange(): return lax.all_to_all(x, axis, split_axis=0, concat_axis=0, tiled=True)]
    pallas_call x7 -> x8, Pallas kernels: 20.1 us -> 18 us  [call(): pl.pallas_call(body, out_shape=tuple(outs), in_specs=[smem] * smem_count...]
where the time goes in v4:
time: 156 us
  blocking collectives  82 us (53%)
  waiting for transfers between devices  27.4 us (18%)
  starting transfers between devices  24.4 us (16%)
  Pallas kernels  18 us (12%)
  local copies, waits for them, and re-layouts  2.96 us (2%)
    all_to_all x4, blocking collectives, exchange(): return lax.all_to_all(x, axis, split_axis=0, concat_axis=0, tiled=True)  82 us
    all_to_all x1, waiting for transfers between devices, exchange(): return lax.all_to_all(x, axis, split_axis=0, concat_axis=0, tiled=True)  25.7 us
    pallas_call x8, Pallas kernels, call(): pl.pallas_call(body, out_shape=tuple(outs), in_specs=[smem] * smem_count...  18 us
    all_to_all x1, starting transfers between devices, exchange(): return lax.all_to_all(x, axis, split_axis=0, concat_axis=0, tiled=True)  15 us
    ppermute x1, starting transfers between devices, local(): other = lax.ppermute(mine, 'core', swap)  5.95 us
    ppermute x1, starting transfers between devices, local(): taken = lax.ppermute(give, 'core', swap)  3.46 us
  transfers between devices with their start and end apart: 3, of which 3 were waited for; matrix products, arithmetic and copies ran while one was open for 0% of the time, Pallas kernels for 2%

profile of v4, /device:TPU:1, one launch (start us, length us, event | category | flops | bytes accessed | tf_op | source)
XLA Modules:
  0.0 155.6 jit_solution(3627146706745556070)
XLA Ops:
  0.6 3.5 %shard_map.120 = bf16[64,72,128]{2,1,0:T(8,128)(2,1)} custom-call(s32[8,6]{1,0:T(8,128)} %mined_hbm.1, s32[512]{0:T(512)} %home_hbm.1, s32[8]{0:T(128)} %positive_hbm.1, bf16[256,512]{1,0:T(8,128)(2,1)} %bitcast.9, bf16[512,384]{1,0:T(8,128)(2,1)} %w_in.1, f32[384]{0:T(512)} %bias.1, bf16[384,128]{1,0:T(8,128)(2,1)} %refs_9_.1), custom_call_target="tpu_custom_call" | custom-call | flops 125829120 | bytes 1937120 | tf_op jit(solution)/shard_map/pallas_call | solution.py:48
  4.2 0.0 copy-start
  4.2 0.0 copy-start.1
  4.2 0.0 copy-start.2
  4.2 15.0 %all-to-all-start = ((bf16[64,72,128]{2,1,0:T(8,128)(2,1)}), bf16[64,72,128]{2,1,0:T(8,128)(2,1)S(1)}, u32[]{:S(2)}, u32[]{:S(2)}) async-start(bf16[64,72,128]{2,1,0:T(8,128)(2,1)} %shard_map.120), calls=%async_computation | async-start | bytes 2359296 | tf_op jit(solution)/shard_map/all_to_all | solution.py:448
  19.2 0.0 copy-start.5
  19.3 2.4 %shard_map.121 = (bf16[8,128,128]{2,1,0:T(8,128)(2,1)S(1)}, bf16[8,128,128]{2,1,0:T(8,128)(2,1)S(1)}, bf16[1280,384]{1,0:T(8,128)(2,1)S(1)}, f32[384,1280]{1,0:T(8,128)S(1)}, f32[8,128]{1,0:T(8,128)S(1)}) custom-call(bf16[1024,512]{1,0:T(8,128)(2,1)S(1)} %bitcast.12, bf16[256,512]{1,0:T(8,128)(2,1)S(1)} %bitcast.10, bf16[512,384]{1,0:T(8,128)(2,1)S(1)} %copy-done, ...), custom_call_target="tpu_custom_call" | custom-call | flops 629145600 | bytes 5281280 | tf_op jit(solution)/shard_map/pallas_call | solution.py:48
  21.8 1.3 copy-done.6
  23.1 1.0 copy-done.8
  24.0 0.1 pad_add_fusion.place.refs_0_
  24.1 25.7 %all-to-all-done.got.refs_2_ = bf16[64,72,128]{2,1,0:T(8,128)(2,1)S(1)} async-done(((bf16[64,72,128]{2,1,0:T(8,128)(2,1)}), bf16[64,72,128]{2,1,0:T(8,128)(2,1)S(1)}, u32[]{:S(2)}, u32[]{:S(2)}) %all-to-all-start) | async-done | bytes 1179680 | tf_op jit(solution)/shard_map/all_to_all | solution.py:448
  49.8 3.9 %shard_map.122 = (bf16[64,72,128]{2,1,0:T(8,128)(2,1)S(1)}, bf16[64,64,128]{2,1,0:T(8,128)(2,1)S(1)}, f32[8,128]{1,0:T(8,128)S(1)}) custom-call(s32[2]{0:T(128)S(1)} %pad_add_fusion.place.refs_0_, s32[512]{0:T(512)S(1)} %copy-done.5, bf16[64,72,128]{2,1,0:T(8,128)(2,1)S(1)} %all-to-all-done.got.refs_2_, bf16[8,128,128]{2,1,0:T(8,128)(2,1)S(1)} %get-tuple-element.19.line_vec, ...), custom_call_target="tpu_custom_call" | custom-call | flops 2147483648 | bytes 3942408 | tf_op jit(solution)/shard_map/pallas_call | solution.py:48
  53.7 37.2 %all_to_all.25.refs_1_ = bf16[64,72,128]{2,1,0:T(8,128)(2,1)S(1)} all-to-all(bf16[64,72,128]{2,1,0:T(8,128)(2,1)S(1)} %get-tuple-element.22), channel_id=1, replica_groups=mesh['chip'=32,'core'=2,'dp'=8] {'chip','core'}, dimensions={0} | all-to-all | bytes 2359296 | tf_op jit(solution)/shard_map/all_to_all | solution.py:448
  90.9 5.8 %shard_map.123 = (f32[8,128]{1,0:T(8,128)S(1)}, f32[1024,128]{1,0:T(8,128)S(1)}, bf16[1024,128]{1,0:T(8,128)(2,1)S(1)}, f32[8,384]{1,0:T(8,128)S(1)}) custom-call(s32[2]{0:T(128)S(1)} %pad_add_fusion.place.refs_0_, bf16[64,72,128]{2,1,0:T(8,128)(2,1)S(1)} %all_to_all.25.refs_1_, bf16[64,72,128]{2,1,0:T(8,128)(2,1)S(1)} %all-to-all-done.got.refs_2_, ...), custom_call_target="tpu_custom_call" | custom-call | flops 3590324224 | bytes 8572936 | tf_op jit(solution)/shard_map/pallas_call | solution.py:48
  96.6 3.5 %collective-permute-start = (bf16[1024,128]{1,0:T(8,128)(2,1)S(1)}, bf16[1024,128]{1,0:T(8,128)(2,1)S(1)}, u32[]{:S(2)}, u32[]{:S(2)}) collective-permute-start(bf16[1024,128]{1,0:T(8,128)(2,1)S(1)} %get-tuple-element.29), channel_id=1, source_target_pairs={{0,8},{8,0},{1,9},{9,1},{2,10},{10,2},{3,11},{11,3},{4,12},{12,4},... | collective-permute-start | bytes 786440 | tf_op jit(solution)/shard_map/ppermute | solution.py:560
  100.1 1.1 collective-permute-done.refs_2_
  101.3 0.6 shard_map.124
  101.9 16.0 %all_to_all.26.got = bf16[32,32,128]{2,1,0:T(8,128)(2,1)S(1)} all-to-all(bf16[32,32,128]{2,1,0:T(8,128)(2,1)S(1)} %bitcast.8), channel_id=1, replica_groups=mesh['chip'=32,'core'=2,'dp'=8] {'chip'}, dimensions={0} | all-to-all | bytes 524288 | tf_op jit(solution)/shard_map/all_to_all | solution.py:448
  117.9 13.8 %all_to_all.27.got = bf16[8,32,128]{2,1,0:T(8,128)(2,1)S(1)} all-to-all(bf16[8,32,128]{2,1,0:T(8,128)(2,1)S(1)} %shard_map.125), channel_id=1, replica_groups=mesh['chip'=32,'core'=2,'dp'=8] {'dp'}, dimensions={0} | all-to-all | bytes 131072 | tf_op jit(solution)/shard_map/all_to_all | solution.py:448
  131.8 15.0 %all_to_all.28 = bf16[32,32,128]{2,1,0:T(8,128)(2,1)S(1)} all-to-all(bf16[32,32,128]{2,1,0:T(8,128)(2,1)S(1)} %shard_map.126), channel_id=1, replica_groups=mesh['chip'=32,'core'=2,'dp'=8] {'chip'}, dimensions={0} | all-to-all | bytes 524288 | tf_op jit(solution)/shard_map/all_to_all | solution.py:448
  146.8 6.0 %collective-permute-start.1 = (bf16[1024,128]{1,0:T(8,128)(2,1)S(1)}, bf16[1024,128]{1,0:T(8,128)(2,1)S(1)}, u32[]{:S(2)}, u32[]{:S(2)}) collective-permute-start(bf16[1024,128]{1,0:T(8,128)(2,1)S(1)} %bitcast.6), channel_id=1, source_target_pairs={{0,8},{8,0},{1,9},{9,1},{2,10},{10,2},{3,11},{11,3},{4,12},{12,4},... | collective-permute-start | bytes 786440 | tf_op jit(solution)/shard_map/ppermute | solution.py:572
  152.7 0.6 slice_reduce_fusion
  153.3 0.5 collective-permute-done.1.other
  153.9 1.7 %shard_map.127 = (f32[512,384]{1,0:T(8,128)}, f32[384]{0:T(512)}, f32[384,128]{1,0:T(8,128)}) custom-call(s32[2]{0:T(128)S(1)} %pad_add_fusion.place.refs_0_, bf16[1024,128]{1,0:T(8,128)(2,1)S(1)} %bitcast.7, bf16[1024,128]{1,0:T(8,128)(2,1)S(1)} %collective-permute-done.1.other, f32[8,384]{1,0:T(8,128)S(1)} %get-tuple-element.30.base_row), custom_call_target="tpu_custom_call" | custom-call | bytes 1521160 | tf_op jit(solution)/shard_map/pallas_call | solution.py:48
  (16 shorter events, 0.1 us)
Async XLA Ops:
  4.2 15.1 %copy-start = (bf16[512,384]{1,0:T(8,128)(2,1)S(1)}, bf16[512,384]{1,0:T(8,128)(2,1)}, u32[]{:S(2)}) copy-start(bf16[512,384]{1,0:T(8,128)(2,1)} %w_in.1) | copy-start | bytes 1179652
  4.2 15.1 %copy-start.1 = (bf16[8,32,512]{2,1,0:T(8,128)(2,1)S(1)}, bf16[8,32,512]{2,1,0:T(8,128)(2,1)}, u32[]{:S(2)}) copy-start(bf16[8,32,512]{2,1,0:T(8,128)(2,1)} %param.9) | copy-start | bytes 786436
  4.2 15.1 %copy-start.2 = (bf16[384,128]{1,0:T(8,128)(2,1)S(1)}, bf16[384,128]{1,0:T(8,128)(2,1)}, u32[]{:S(2)}) copy-start(bf16[384,128]{1,0:T(8,128)(2,1)} %refs_9_.1) | copy-start | bytes 294916
  4.2 15.1 %copy-start.3 = (f32[384]{0:T(512)S(1)}, f32[384]{0:T(512)}, u32[]{:S(2)}) copy-start(f32[384]{0:T(512)} %bias.1) | copy-start | bytes 4612
  4.2 15.1 %copy-start.4 = (bf16[8,128,512]{2,1,0:T(8,128)(2,1)S(1)}, bf16[8,128,512]{2,1,0:T(8,128)(2,1)}, u32[]{:S(2)}) copy-start(bf16[8,128,512]{2,1,0:T(8,128)(2,1)} %param.10) | copy-start | bytes 3145732
  4.2 45.6 %all-to-all-start = ((bf16[64,72,128]{2,1,0:T(8,128)(2,1)}), bf16[64,72,128]{2,1,0:T(8,128)(2,1)S(1)}, u32[]{:S(2)}, u32[]{:S(2)}) async-start(bf16[64,72,128]{2,1,0:T(8,128)(2,1)} %shard_map.120), calls=%async_computation | async-start | bytes 2359296 | tf_op jit(solution)/shard_map/all_to_all | solution.py:448
  19.2 30.6 %copy-start.5 = (s32[512]{0:T(512)S(1)}, s32[512]{0:T(512)}, u32[]{:S(2)}) copy-start(s32[512]{0:T(512)} %counts.1) | copy-start | bytes 6148
  21.8 1.3 copy-start.6
  23.1 1.0 copy-start.8
  49.8 41.0 %copy-start.9 = (bf16[1280,384]{1,0:T(8,128)(2,1)S(1)}, bf16[1280,384]{1,0:T(8,128)(2,1)}, u32[]{:S(2)}) copy-start(bf16[1280,384]{1,0:T(8,128)(2,1)} %copy-done.8) | copy-start | bytes 2949124
  53.7 37.2 %copy-start.7 = (f32[384,1280]{1,0:T(8,128)S(1)}, f32[384,1280]{1,0:T(8,128)}, u32[]{:S(2)}) copy-start(f32[384,1280]{1,0:T(8,128)} %copy-done.6) | copy-start | bytes 5898244
  96.6 4.6 %collective-permute-start = (bf16[1024,128]{1,0:T(8,128)(2,1)S(1)}, bf16[1024,128]{1,0:T(8,128)(2,1)S(1)}, u32[]{:S(2)}, u32[]{:S(2)}) collective-permute-start(bf16[1024,128]{1,0:T(8,128)(2,1)S(1)} %get-tuple-element.29), channel_id=1, source_target_pairs={{0,8},{8,0},{1,9},{9,1},{2,10},{10,2},{3,11},{11,3},{4,12},{12,4},... | collective-permute-start | bytes 786440 | tf_op jit(solution)/shard_map/ppermute | solution.py:560
  146.8 7.1 %collective-permute-start.1 = (bf16[1024,128]{1,0:T(8,128)(2,1)S(1)}, bf16[1024,128]{1,0:T(8,128)(2,1)S(1)}, u32[]{:S(2)}, u32[]{:S(2)}) collective-permute-start(bf16[1024,128]{1,0:T(8,128)(2,1)S(1)} %bitcast.6), channel_id=1, source_target_pairs={{0,8},{8,0},{1,9},{9,1},{2,10},{10,2},{3,11},{11,3},{4,12},{12,4},... | collective-permute-start | bytes 786440 | tf_op jit(solution)/shard_map/ppermute | solution.py:572

commit v5 on v4

--- a/solution.py
+++ b/solution.py
@@ -13,12 +13,12 @@
 CAP = 2
 HALF = LANES // CAP
 META = 8
+ASK_ROWS = 2
+BACK_ROWS = 4
 UNUSED = 100.0
 FLOOR = -1e30
 GELU_A = math.sqrt(2.0 / math.pi)
 GELU_B = 0.044715
-GROUP = 64
-WIDE = 64
 ARCHIVE = ("chip", "core")
 
 f32 = jnp.float32
@@ -64,13 +64,13 @@
 
 
 def ask_kernel(
-    mined_hbm, home_hbm, positive_hbm, x_hbm, w_in_hbm, bias_hbm, w_out_hbm, send, mined, home, positive, x, w_in, bias, w_out, vec, rid, code, count, goal, sems
+    mined_hbm, home_hbm, positive_hbm, x_hbm, w_in_hbm, bias_hbm, w_out_hbm, send, mined, home, positive, x, w_in, bias, w_out, vec, stage, rid, code, count, goal_owner, goal_rank, sems
 ):
     query_count, mined_count = mined.shape
-    owner_count = send.shape[0]
+    owner_count, rows, _ = stage.shape
     query_len = x.shape[0] // query_count
     line_count = home.shape[0] // owner_count
-    rows = CAP * query_len
+    stride = rows + ASK_ROWS
     pairs = (
         (mined_hbm, mined),
         (home_hbm, home),
@@ -92,7 +92,7 @@
         return carry
 
     lax.fori_loop(0, owner_count, clear, 0, unroll=8)
-    send[...] = jnp.zeros(send.shape, bf16)
+    stage[...] = jnp.zeros(stage.shape, bf16)
     for copy in copies[:3]:
         copy.wait()
 
@@ -104,22 +104,21 @@
             count[owner] = rank + 1
             rid[rank, owner] = row - owner * line_count
             code[rank, owner] = query + jnp.where(positive[query] == j, 8, 0)
-            goal[query, j] = owner * CAP + rank
+            goal_owner[query, j] = owner
+            goal_rank[query, j] = rank * query_len
         return carry
 
-    lax.fori_loop(0, query_count, assign, 0)
-    sub = lax.broadcasted_iota(jnp.int32, (META, LANES), 0)
-
-    def label(owner, carry):
+    lax.fori_loop(0, query_count, assign, 0, unroll=2)
+    sub = lax.broadcasted_iota(jnp.int32, (ASK_ROWS, LANES), 0)
+    low = lax.broadcasted_iota(jnp.int32, (ASK_ROWS, LANES), 1) < HALF
+    for owner in range(owner_count):
         tile = jnp.where(
             sub == 0,
-            rid[0, owner],
-            jnp.where(sub == 1, rid[1, owner], jnp.where(sub == 2, code[0, owner], code[1, owner])),
+            jnp.where(low, rid[0, owner], rid[1, owner]),
+            jnp.where(low, code[0, owner], code[1, owner]),
         )
-        send[owner, rows : rows + META, :] = tile.astype(f32).astype(bf16)
-        return carry
-
-    lax.fori_loop(0, owner_count, label, 0, unroll=8)
+        first = owner * stride + rows
+        send[first : first + ASK_ROWS, :] = tile.astype(f32).astype(bf16)
     for copy in copies[3:]:
         copy.wait()
     _, hidden = gelu_parts(dot(x[...], w_in[...]) + bias[...].reshape(1, -1))
@@ -128,12 +127,13 @@
     def place(query, carry):
         block = vec[pl.ds(pl.multiple_of(query * query_len, query_len), query_len), :]
         for j in range(mined_count):
-            owner = goal[query, j] // CAP
-            rank = goal[query, j] % CAP
-            send[owner, pl.ds(pl.multiple_of(rank * query_len, query_len), query_len), :] = block
+            first = pl.multiple_of(goal_rank[query, j], query_len)
+            stage[goal_owner[query, j], pl.ds(first, query_len), :] = block
         return carry
 
-    lax.fori_loop(0, query_count, place, 0)
+    lax.fori_loop(0, query_count, place, 0, unroll=4)
+    for owner in range(owner_count):
+        send[owner * stride : owner * stride + rows, :] = stage[owner]
 
 
 def head_kernel(xl, xq, w_in, bias, w_out, line_vec, line_vec_t, hidden_all, slope_t, mean):
@@ -160,9 +160,7 @@
                 line_vec[line] = vec[k : k + LANES].astype(bf16)
                 line_vec_t[line] = vec[k : k + LANES].T.astype(bf16)
             total += jnp.sum(hidden.astype(f32), axis=0, keepdims=True)
-    mean[...] = jnp.zeros(mean.shape, f32)
-    for i, k in enumerate(range(0, hidden_all.shape[1], LANES)):
-        mean[4 + i : 5 + i, :] = total[:, k : k + LANES] * (1.0 / line_frames)
+    mean[...] = jnp.broadcast_to(total * (1.0 / line_frames), mean.shape)
 
 
 def spread(meta, first, query_len):
@@ -176,84 +174,81 @@
 def match_kernel(
     place, counts, got, line_vec, line_vec_t, mean, send, weights, own, pads, label_rows, ids, sums, sem
 ):
-    owner_count = got.shape[0]
-    rows = got.shape[1] - META
-    group = min(GROUP, owner_count)
+    owner_count, rows, _ = weights.shape
     query_len = rows // CAP
+    stride, out_stride = rows + ASK_ROWS, rows + BACK_ROWS
     line_count, _, vec_width = line_vec.shape
     scale = SCORE_SCALE / math.sqrt(vec_width)
-    shape3 = (owner_count, META, LANES)
-    lane3 = lax.broadcasted_iota(jnp.int32, shape3, 2)
-    sub3 = lax.broadcasted_iota(jnp.int32, shape3, 1)
-    owner3 = lax.broadcasted_iota(jnp.int32, shape3, 0)
     lane1 = lax.broadcasted_iota(jnp.int32, (1, LANES), 1)
-    sub = lax.broadcasted_iota(jnp.int32, (META, LANES), 0)
-    meta = got[:, rows : rows + META, :].astype(f32)
-    labels = jnp.sum(jnp.where(lane3 == owner3 + HALF * (sub3 % CAP), meta, 0.0), axis=0)
-    covered = lane1 % HALF < owner_count
-    rid_row = labels[0:1] + labels[1:2]
-    rid_row = jnp.where(covered & (rid_row < line_count), rid_row, 0.0)
-    code_row = jnp.where(covered, labels[2:3] + labels[3:4], UNUSED)
+    lane2 = lax.broadcasted_iota(jnp.int32, (ASK_ROWS, LANES), 1) % HALF
+    labels = jnp.full((ASK_ROWS, LANES), UNUSED, f32)
+    for b in range(owner_count):
+        first = b * stride + rows
+        labels = jnp.where(lane2 == b, got[first : first + ASK_ROWS, :].astype(f32), labels)
+    rid_row, code_row = labels[0:1], labels[1:2]
+    rid_row = jnp.where(rid_row < line_count, rid_row, 0.0)
     label_rows[...] = jnp.broadcast_to(rid_row, (META, LANES)).astype(jnp.int32)
     copy = pltpu.make_async_copy(label_rows, ids, sem)
     copy.start()
     for r in range(line_count):
         pads[r : r + 1, :] = jnp.where(lane1 < counts[place[0] * line_count + r], 0.0, FLOOR)
     sums[...] = jnp.zeros(sums.shape, f32)
+    ones = jnp.ones((LANES, LANES), bf16)
     copy.wait()
-    ones = jnp.ones((LANES, LANES), bf16)
-
-    def step(g, carry):
-        first = g * group
-        for b in range(group):
-            for c in range(CAP):
-                slot = first + b + HALF * c
-                r = ids[0, slot]
-                span = pl.ds(c * query_len, query_len)
-                logits = dot(got[first + b, span, :], line_vec_t[r]) * scale
-                logits = logits + pads[pl.ds(r, 1), :]
-                peak = jnp.max(logits, axis=1, keepdims=True)
-                scaled = jnp.exp(logits - peak)
-                scaled = scaled.astype(bf16)
-                both = dot(scaled, jnp.concatenate([line_vec[r], ones], axis=1))
-                totals = both[:, vec_width:]
-                inverse = 1.0 / totals
-                weights[first + b, span, :] = (scaled.astype(f32) * inverse).astype(bf16)
-                send[first + b, span, :] = (both[:, :vec_width] * inverse).astype(bf16)
-                log_total = peak + jnp.log(totals)
-                mean_log = jnp.sum(log_total, axis=0, keepdims=True) * (1.0 / query_len)
-                sums[pl.ds(slot, 1), :] = mean_log
-        return carry
-
-    lax.fori_loop(0, owner_count // group, step, 0)
+    for b in range(owner_count):
+        for c in range(CAP):
+            slot = b + HALF * c
+            r = ids[0, slot]
+            first = b * stride + c * query_len
+            logits = dot(got[first : first + query_len, :], line_vec_t[r]) * scale
+            logits = logits + pads[pl.ds(r, 1), :]
+            peak = jnp.max(logits, axis=1, keepdims=True)
+            scaled = jnp.exp(logits - peak).astype(bf16)
+            both = dot(scaled, jnp.concatenate([line_vec[r], ones], axis=1))
+            totals = both[:, vec_width:]
+            inverse = 1.0 / totals
+            weights[b, c * query_len : (c + 1) * query_len, :] = (
+                scaled.astype(f32) * inverse
+            ).astype(bf16)
+            first = b * out_stride + c * query_len
+            send[first : first + query_len, :] = (both[:, :vec_width] * inverse).astype(bf16)
+            log_total = peak + jnp.log(totals)
+            sums[slot : slot + 1, :] = jnp.sum(log_total, axis=0, keepdims=True) * (1.0 / query_len)
     lane = lax.broadcasted_iota(jnp.int32, sums.shape, 1)
     row = lax.broadcasted_iota(jnp.int32, sums.shape, 0)
     match_row = jnp.sum(jnp.where(lane == row, sums[...], 0.0), axis=0, keepdims=True)
-    own[...] = jnp.where(sub == 0, match_row, code_row)
-    tile = mean[...]
-    for p, part in enumerate(split3(match_row)):
-        tile = jnp.where(sub == p, part, tile)
-    tile = jnp.where(sub == 3, code_row, tile).astype(bf16)
-
-    def label(b, carry):
-        send[b, rows : rows + META, :] = tile
-        return carry
-
-    lax.fori_loop(0, owner_count, label, 0, unroll=8)
+    high, low = (part.astype(f32) for part in split2(match_row))
+    blocks = own_blocks(mean.shape[1])
+    mean_row = mean[:, 0:LANES]
+    for k in range(1, blocks):
+        mean_row = jnp.where(place[0] % blocks == k, mean[:, k * LANES : (k + 1) * LANES], mean_row)
+    sub = lax.broadcasted_iota(jnp.int32, (META, LANES), 0)
+    own[...] = jnp.where(sub == 0, high + low, jnp.where(sub == 1, code_row, rid_row))
+    sub = lax.broadcasted_iota(jnp.int32, (BACK_ROWS, LANES), 0)
+    tile = jnp.where(
+        sub == 0, high, jnp.where(sub == 1, low, jnp.where(sub == 2, code_row, mean_row[0:1]))
+    ).astype(bf16)
+    for b in range(owner_count):
+        first = b * out_stride + rows
+        send[first : first + BACK_ROWS, :] = tile
+
+
+def own_blocks(hid):
+    return hid // LANES
 
 
 def grad_kernel(
     place, back, got, weights, own, xl, xq, hidden_all, slope_t, w_out, loss, keep, give, base_row, grads, own_scale, ask_scale, line_acc, query_acc, *, loss_factor
 ):
-    owner_count = got.shape[0]
-    rows = got.shape[1] - META
-    wide_count = min(WIDE, owner_count)
+    owner_count, rows, _ = weights.shape
+    stride, back_stride = rows + ASK_ROWS, rows + BACK_ROWS
     query_len = rows // CAP
     line_total = xl.shape[0]
     line_count = line_total // LANES
     query_frames = xq.shape[0]
     vec_width = w_out.shape[1]
     hid = w_out.shape[0]
+    blocks = own_blocks(hid)
     me = place[0]
 
     shape3 = (owner_count, META, LANES)
@@ -261,21 +256,33 @@
     sub3 = lax.broadcasted_iota(jnp.int32, shape3, 1)
     owner3 = lax.broadcasted_iota(jnp.int32, shape3, 0)
     subf = sub3.astype(f32)
-    meta = back[:, rows : rows + META, :].astype(f32)
-    match = jnp.sum(jnp.where(sub3 < 3, meta, 0.0), axis=1, keepdims=True)
-    code = jnp.sum(jnp.where(sub3 == 3, meta, 0.0), axis=1, keepdims=True)
-    match = jnp.broadcast_to(match, shape3)
-    code = jnp.broadcast_to(code, shape3)
+    matches, codes = [], []
+    shared = [jnp.zeros((1, LANES), f32) for _ in range(blocks)]
+    for owner in range(owner_count):
+        first = owner * back_stride + rows
+        tile = back[first : first + BACK_ROWS, :].astype(f32)
+        matches.append(jnp.broadcast_to(tile[0:1] + tile[1:2], (1, META, LANES)))
+        codes.append(jnp.broadcast_to(tile[2:3], (1, META, LANES)))
+        shared[owner % blocks] += tile[3:4]
+    match = jnp.concatenate(matches, axis=0)
+    code = jnp.concatenate(codes, axis=0)
+    shared = [
+        part * (1.0 / ((owner_count - k + blocks - 1) // blocks)) for k, part in enumerate(shared)
+    ]
+    shared = jnp.concatenate(shared, axis=1).astype(bf16).astype(f32)
+    base_row[...] = jnp.broadcast_to(shared, base_row.shape)
     is_pos = (code >= 8.0) & (code < 16.0)
     query_of = jnp.where(is_pos, code - 8.0, code)
     here = query_of == subf
     peak = jnp.max(jnp.where(here, match, FLOOR), axis=0)
     peak = jnp.maximum(peak, pltpu.roll(peak, HALF, 1))
-    total = jnp.sum(jnp.where(here, jnp.exp(match - peak[None]), 0.0), axis=0)
+    raised = jnp.where(here, jnp.exp(match - peak[None]), 0.0)
+    total = jnp.sum(raised, axis=0)
     total = total + pltpu.roll(total, HALF, 1)
+    total = jnp.where(total > 0.0, total, 1.0)
     chosen = jnp.sum(jnp.where(here & is_pos, match, 0.0), axis=0)
     chosen = chosen + pltpu.roll(chosen, HALF, 1)
-    log_total = peak + jnp.log(jnp.where(total > 0.0, total, 1.0))
+    log_total = peak + jnp.log(total)
     lane2 = lax.broadcasted_iota(jnp.int32, (META, LANES), 1)
     sub2 = lax.broadcasted_iota(jnp.int32, (META, LANES), 0).astype(f32)
     picked = jnp.sum(jnp.where(lane2 == me, log_total - chosen, 0.0), axis=1, keepdims=True)
@@ -289,68 +296,59 @@
     own_query = jnp.where(own_pos, own_code - 8.0, own_code)
     own_grad = jnp.exp(jnp.minimum(own_match - log_total, 0.0)) - jnp.where(own_pos, 1.0, 0.0)
     own_grad = factor * jnp.sum(jnp.where(own_query == sub2, own_grad, 0.0), axis=0, keepdims=True)
-    aim = lane3 == owner3 + HALF * sub3
+    both = jnp.where(lane2 >= 0, jnp.where(sub2 < CAP, own_grad, own[2:3, :]), 0.0)
+    slot3 = HALF * (sub3 % CAP)
     own_scale[...] = jnp.broadcast_to(
         jnp.sum(
-            jnp.where(aim, jnp.broadcast_to(own_grad[None], shape3), 0.0), axis=2, keepdims=True
+            jnp.where(lane3 == owner3 + slot3, jnp.broadcast_to(both[None], shape3), 0.0),
+            axis=2,
+            keepdims=True,
         ),
         shape3,
     )
 
-    ask_grad = jnp.exp(jnp.minimum(match - log_total[None], 0.0)) - jnp.where(is_pos, 1.0, 0.0)
-    ask_grad = factor * jnp.sum(jnp.where(here, ask_grad, 0.0), axis=1, keepdims=True)
+    ask_grad = raised * (1.0 / total)[None] - jnp.where(here & is_pos, 1.0, 0.0)
+    ask_grad = factor * jnp.sum(ask_grad, axis=1, keepdims=True)
     both = jnp.where(sub3 < CAP, jnp.broadcast_to(ask_grad, shape3), query_of)
-    aim = lane3 == me + HALF * (sub3 % CAP)
     ask_scale[...] = jnp.broadcast_to(
-        jnp.sum(jnp.where(aim, both, 0.0), axis=2, keepdims=True), shape3
-    )
-
-    size = wide_count * rows
-    line_acc[...] = jnp.zeros(line_acc.shape, f32)
-    query_acc[...] = jnp.zeros(query_acc.shape, f32)
+        jnp.sum(jnp.where(lane3 == me + slot3, both, 0.0), axis=2, keepdims=True), shape3
+    )
+
+    size = owner_count * rows
     frame = (lax.broadcasted_iota(jnp.int32, (size, LANES), 0) % query_len).astype(f32)
     lane = lax.broadcasted_iota(jnp.int32, (size, LANES), 1).astype(f32)
     zero = jnp.zeros((size, LANES), bf16)
     one = jnp.ones((size, LANES), bf16)
 
-    def step(g, carry):
-        first = g * wide_count
-        queries = got[pl.ds(first, wide_count), 0:rows, :].reshape(size, LANES)
-        rid = spread(got[pl.ds(first, wide_count), rows : rows + META, :].astype(f32), 0, query_len)
-        rid = rid.astype(bf16)
-        scale = spread(own_scale[pl.ds(first, wide_count)], 0, query_len)
-        weight = weights[pl.ds(first, wide_count)].reshape(size, LANES).astype(f32)
-        score = (weight * scale).astype(bf16)
-        wide = jnp.concatenate(
-            [jnp.where(rid == r, score, zero) for r in range(line_count)], axis=1
-        )
-        line_acc[...] += dot(queries, wide, 0, 0)
-
-        labels = ask_scale[pl.ds(first, wide_count)]
-        scale = spread(labels, 0, query_len)
-        target = spread(labels, CAP, query_len) * float(query_len) + frame
-        pulled = back[pl.ds(first, wide_count), 0:rows, :].reshape(size, LANES).astype(f32)
-        pulled = (pulled * scale).astype(bf16)
-        wide = jnp.concatenate(
-            [
-                jnp.where(target == lane + float(k), one, zero)
-                for k in range(0, query_acc.shape[1], LANES)
-            ],
-            axis=1,
-        )
-        query_acc[...] += dot(pulled, wide, 0, 0)
-        return carry
-
-    lax.fori_loop(0, owner_count // wide_count, step, 0)
+    labels = own_scale[...]
+    queries = jnp.concatenate(
+        [got[b * stride : b * stride + rows, :] for b in range(owner_count)], axis=0
+    )
+    rid = spread(labels, CAP, query_len).astype(bf16)
+    weight = weights[...].reshape(size, LANES).astype(f32)
+    score = (weight * spread(labels, 0, query_len)).astype(bf16)
+    wide = jnp.concatenate([jnp.where(rid == r, score, zero) for r in range(line_count)], axis=1)
+    line_acc[...] = dot(queries, wide, 0, 0)
+
+    labels = ask_scale[...]
+    target = spread(labels, CAP, query_len) * float(query_len) + frame
+    pulled = jnp.concatenate(
+        [back[b * back_stride : b * back_stride + rows, :] for b in range(owner_count)], axis=0
+    )
+    pulled = (pulled.astype(f32) * spread(labels, 0, query_len)).astype(bf16)
+    wide = jnp.concatenate(
+        [
+            jnp.where(target == lane + float(k), one, zero)
+            for k in range(0, query_acc.shape[1], LANES)
+        ],
+        axis=1,
+    )
+    query_acc[...] = dot(pulled, wide, 0, 0)
 
     grad_in = None
     grad_out = None
     grad_bias = None
     vec_sum = None
-    shared = jnp.sum(jnp.where(sub3 >= 4, meta, 0.0), axis=0) * (1.0 / owner_count)
-    shared = shared.astype(bf16).astype(f32)
-    shared = jnp.concatenate([shared[4 + i : 5 + i, :] for i in range(hid // LANES)], axis=1)
-    base_row[...] = jnp.broadcast_to(shared, base_row.shape)
     spans = ((line_acc, xl, 0, line_total), (query_acc, xq, line_total, query_frames))
     for acc, x, first, span in spans:
         g_hi, g_lo = split2(acc[:, 0:span])
@@ -358,7 +356,7 @@
         p_hi, p_lo = split2(grad_hidden * slope_t[:, first : first + span])
         hidden = hidden_all[first : first + span, :]
         ones = jnp.ones((META, span), bf16)
-        part_in = dot(p_hi, x[...]) + dot(p_lo, x[...])
+        part_in = dot(p_hi, x[...])
         part_out = dot(g_hi, hidden) + dot(g_lo, hidden)
         part_out -= jnp.sum(g_hi.astype(f32) + g_lo.astype(f32), axis=1, keepdims=True) * shared
         part_sum = dot(ones, g_hi, 1, 1) + dot(ones, g_lo, 1, 1)
@@ -448,6 +446,11 @@
     return lax.all_to_all(x, axis, split_axis=0, concat_axis=0, tiled=True)
 
 
+def exchange_rows(x, axis, peers, tile):
+    blocks = x.reshape(peers, x.shape[0] // (peers * tile), tile, x.shape[1])
+    return exchange(blocks, axis).reshape(x.shape)
+
+
 def shape_of(shape, dtype):
     return jax.ShapeDtypeStruct(shape, dtype)
 
@@ -467,12 +470,13 @@
     xq = query_frames.reshape(frames_q, feat)
     xl = line_frames.reshape(frames_l, feat)
     place = jnp.stack([lax.axis_index(ARCHIVE), lax.axis_index("core")]).astype(jnp.int32)
-    wire = shape_of((owner_count, rows + META, vec_width), bf16)
+    ask_wire = shape_of((owner_count * (rows + ASK_ROWS), vec_width), bf16)
+    back_wire = shape_of((owner_count * (rows + BACK_ROWS), vec_width), bf16)
     head_flops = 2 * hid * (feat + vec_width)
 
     (asked,) = call(
         ask_kernel,
-        [wire],
+        [ask_wire],
         [mined, line_home, positive, xq, w_in, bias_in, w_out],
         0,
         [
@@ -484,9 +488,11 @@
             pltpu.VMEM(bias_in.shape, f32),
             pltpu.VMEM(w_out.shape, bf16),
             pltpu.VMEM((frames_q, vec_width), bf16),
+            pltpu.VMEM((owner_count, rows, vec_width), bf16),
             pltpu.SMEM((CAP, owner_count), jnp.int32),
             pltpu.SMEM((CAP, owner_count), jnp.int32),
             pltpu.SMEM((owner_count,), jnp.int32),
+            pltpu.SMEM(mined.shape, jnp.int32),
             pltpu.SMEM(mined.shape, jnp.int32),
             pltpu.SemaphoreType.DMA((7,)),
         ],
@@ -494,7 +500,7 @@
         where=pltpu.HBM,
         limit=63 << 20,
     )
-    got = exchange(asked, ARCHIVE)
+    got = exchange_rows(asked, ARCHIVE, owner_count, ASK_ROWS)
     line_vec, line_vec_t, hidden_all, slope_t, mean = call(
         head_kernel,
         [
@@ -502,7 +508,7 @@
             shape_of((line_count, vec_width, line_len), bf16),
             shape_of((frames, hid), bf16),
             shape_of((hid, frames), f32),
-            shape_of((META, LANES), f32),
+            shape_of((META, hid), f32),
         ],
         [xl, xq, w_in, bias_in, w_out],
         0,
@@ -513,7 +519,7 @@
     answer, weights, own = call(
         match_kernel,
         [
-            wire,
+            back_wire,
             shape_of((owner_count, rows, line_len), bf16),
             shape_of((META, LANES), f32),
         ],
@@ -528,7 +534,7 @@
         ],
         flops=2 * match_flops,
     )
-    back = exchange(answer, ARCHIVE)
+    back = exchange_rows(answer, ARCHIVE, owner_count, BACK_ROWS)
     unit = 16 * owner_count
     flat_rows = unit * -(-(LANES + (feat + vec_width) * hid // LANES) // unit)
     half = flat_rows // 2

time: 156 us -> 153 us (0.981)
  waiting for transfers between devices: 27.4 us -> 25.4 us
    all_to_all x1, waiting for transfers between devices: 25.7 us -> 23.8 us  [exchange(): return lax.all_to_all(x, axis, split_axis=0, concat_axis=0, tiled=True)]
where the time goes in v5:
time: 153 us; the launch traced here: 152 us
  blocking collectives  80.5 us (53%)
  waiting for transfers between devices  25.4 us (17%)
  starting transfers between devices  24.3 us (16%)
  Pallas kernels  18 us (12%)
  local copies, waits for them, and re-layouts  2.94 us (2%)
    all_to_all x4, blocking collectives, exchange(): return lax.all_to_all(x, axis, split_axis=0, concat_axis=0, tiled=True)  80.5 us
    all_to_all x1, waiting for transfers between devices, exchange(): return lax.all_to_all(x, axis, split_axis=0, concat_axis=0, tiled=True)  23.8 us
    pallas_call x8, Pallas kernels, call(): pl.pallas_call(body, out_shape=tuple(outs), in_specs=[smem] * smem_count...  18 us
    all_to_all x1, starting transfers between devices, exchange(): return lax.all_to_all(x, axis, split_axis=0, concat_axis=0, tiled=True)  15 us
    ppermute x1, starting transfers between devices, local(): other = lax.ppermute(mine, 'core', swap)  5.95 us
    ppermute x1, starting transfers between devices, local(): taken = lax.ppermute(give, 'core', swap)  3.4 us
  transfers between devices with their start and end apart: 3, of which 3 were waited for; matrix products, arithmetic and copies ran while one was open for 0% of the time, Pallas kernels for 2%

profile of v5, /device:TPU:1, one launch (start us, length us, event | category | flops | bytes accessed | tf_op | source)
XLA Modules:
  0.0 152.1 jit_solution(17404143647704708110)
XLA Ops:
  0.6 3.3 %shard_map.120 = bf16[4224,128]{1,0:T(8,128)(2,1)} custom-call(s32[8,6]{1,0:T(8,128)} %mined_hbm.1, s32[512]{0:T(512)} %home_hbm.1, s32[8]{0:T(128)} %positive_hbm.1, bf16[256,512]{1,0:T(8,128)(2,1)} %bitcast.17, bf16[512,384]{1,0:T(8,128)(2,1)} %w_in.1, f32[384]{0:T(512)} %bias.1, bf16[384,128]{1,0:T(8,128)(2,1)} %refs_9_.1), custom_call_target="tpu_custom_call" | custom-call | flops 125829120 | bytes 1838816 | tf_op jit(solution)/shard_map/pallas_call | solution.py:48
  4.0 0.0 copy-start
  4.0 0.0 copy-start.1
  4.0 0.0 copy-start.3
  4.0 0.0 copy-start.4
  4.0 15.0 %all-to-all-start = ((bf16[64,33,2,128]{3,2,1,0:T(2,128)(2,1)}), bf16[64,33,2,128]{3,2,1,0:T(2,128)(2,1)S(1)}, u32[]{:S(2)}, u32[]{:S(2)}) async-start(bf16[64,33,2,128]{3,2,1,0:T(2,128)(2,1)} %bitcast.22), calls=%async_computation | async-start | bytes 2162688 | tf_op jit(solution)/shard_map/all_to_all | solution.py:446
  19.1 2.4 %shard_map.121 = (bf16[8,128,128]{2,1,0:T(8,128)(2,1)S(1)}, bf16[8,128,128]{2,1,0:T(8,128)(2,1)S(1)}, bf16[1280,384]{1,0:T(8,128)(2,1)S(1)}, f32[384,1280]{1,0:T(8,128)S(1)}, f32[8,384]{1,0:T(8,128)S(1)}) custom-call(bf16[1024,512]{1,0:T(8,128)(2,1)S(1)} %bitcast.20, bf16[256,512]{1,0:T(8,128)(2,1)S(1)} %bitcast.18, bf16[512,384]{1,0:T(8,128)(2,1)S(1)} %copy-done, ...), custom_call_target="tpu_custom_call" | custom-call | flops 629145600 | bytes 5289472 | tf_op jit(solution)/shard_map/pallas_call | solution.py:48
  21.5 1.3 copy-done.6
  22.8 1.0 copy-done.8
  23.8 0.1 pad_add_fusion.place.refs_0_
  23.9 23.8 %all-to-all-done = bf16[64,33,2,128]{3,2,1,0:T(2,128)(2,1)S(1)} async-done(((bf16[64,33,2,128]{3,2,1,0:T(2,128)(2,1)}), bf16[64,33,2,128]{3,2,1,0:T(2,128)(2,1)S(1)}, u32[]{:S(2)}, u32[]{:S(2)}) %all-to-all-start) | async-done | bytes 1081376 | tf_op jit(solution)/shard_map/all_to_all | solution.py:446
  47.6 3.9 %shard_map.122 = (bf16[4352,128]{1,0:T(8,128)(2,1)S(1)}, bf16[64,64,128]{2,1,0:T(8,128)(2,1)S(1)}, f32[8,128]{1,0:T(8,128)S(1)}) custom-call(s32[2]{0:T(128)S(1)} %pad_add_fusion.place.refs_0_, s32[512]{0:T(512)S(1)} %copy-done.5, bf16[4224,128]{1,0:T(8,128)(2,1)S(1)} %bitcast.12, bf16[8,128,128]{2,1,0:T(8,128)(2,1)S(1)} %get-tuple-element.19.line_vec, ...), custom_call_target="tpu_custom_call" | custom-call | flops 2147483648 | bytes 3786760 | tf_op jit(solution)/shard_map/pallas_call | solution.py:48
  51.5 35.7 %all_to_all.25 = bf16[64,17,4,128]{3,2,1,0:T(4,128)(2,1)S(1)} all-to-all(bf16[64,17,4,128]{3,2,1,0:T(4,128)(2,1)S(1)} %bitcast.11), channel_id=1, replica_groups=mesh['chip'=32,'core'=2,'dp'=8] {'chip','core'}, dimensions={0} | all-to-all | bytes 2228224 | tf_op jit(solution)/shard_map/all_to_all | solution.py:446
  87.2 6.0 %shard_map.123 = (f32[8,128]{1,0:T(8,128)S(1)}, f32[1024,128]{1,0:T(8,128)S(1)}, bf16[1024,128]{1,0:T(8,128)(2,1)S(1)}, f32[8,384]{1,0:T(8,128)S(1)}) custom-call(s32[2]{0:T(128)S(1)} %pad_add_fusion.place.refs_0_, bf16[4352,128]{1,0:T(8,128)(2,1)S(1)} %bitcast.10, bf16[4224,128]{1,0:T(8,128)(2,1)S(1)} %bitcast.13, ...), custom_call_target="tpu_custom_call" | custom-call | flops 3590324224 | bytes 8409096 | tf_op jit(solution)/shard_map/pallas_call | solution.py:48
  93.2 3.4 %collective-permute-start = (bf16[1024,128]{1,0:T(8,128)(2,1)S(1)}, bf16[1024,128]{1,0:T(8,128)(2,1)S(1)}, u32[]{:S(2)}, u32[]{:S(2)}) collective-permute-start(bf16[1024,128]{1,0:T(8,128)(2,1)S(1)} %get-tuple-element.29), channel_id=1, source_target_pairs={{0,8},{8,0},{1,9},{9,1},{2,10},{10,2},{3,11},{11,3},{4,12},{12,4},... | collective-permute-start | bytes 786440 | tf_op jit(solution)/shard_map/ppermute | solution.py:566
  96.6 1.1 collective-permute-done.refs_2_
  97.8 0.6 shard_map.124
  98.4 16.0 %all_to_all.26.got = bf16[32,32,128]{2,1,0:T(8,128)(2,1)S(1)} all-to-all(bf16[32,32,128]{2,1,0:T(8,128)(2,1)S(1)} %bitcast.16), channel_id=1, replica_groups=mesh['chip'=32,'core'=2,'dp'=8] {'chip'}, dimensions={0} | all-to-all | bytes 524288 | tf_op jit(solution)/shard_map/all_to_all | solution.py:446
  114.4 13.8 %all_to_all.27.got = bf16[8,32,128]{2,1,0:T(8,128)(2,1)S(1)} all-to-all(bf16[8,32,128]{2,1,0:T(8,128)(2,1)S(1)} %shard_map.125), channel_id=1, replica_groups=mesh['chip'=32,'core'=2,'dp'=8] {'dp'}, dimensions={0} | all-to-all | bytes 131072 | tf_op jit(solution)/shard_map/all_to_all | solution.py:446
  128.3 15.0 %all_to_all.28 = bf16[32,32,128]{2,1,0:T(8,128)(2,1)S(1)} all-to-all(bf16[32,32,128]{2,1,0:T(8,128)(2,1)S(1)} %shard_map.126), channel_id=1, replica_groups=mesh['chip'=32,'core'=2,'dp'=8] {'chip'}, dimensions={0} | all-to-all | bytes 524288 | tf_op jit(solution)/shard_map/all_to_all | solution.py:446
  143.3 6.0 %collective-permute-start.1 = (bf16[1024,128]{1,0:T(8,128)(2,1)S(1)}, bf16[1024,128]{1,0:T(8,128)(2,1)S(1)}, u32[]{:S(2)}, u32[]{:S(2)}) collective-permute-start(bf16[1024,128]{1,0:T(8,128)(2,1)S(1)} %bitcast.14), channel_id=1, source_target_pairs={{0,8},{8,0},{1,9},{9,1},{2,10},{10,2},{3,11},{11,3},{4,12},{12,4},... | collective-permute-start | bytes 786440 | tf_op jit(solution)/shard_map/ppermute | solution.py:578
  149.2 0.6 slice_reduce_fusion
  149.8 0.5 collective-permute-done.1.other
  150.4 1.7 %shard_map.127 = (f32[512,384]{1,0:T(8,128)}, f32[384]{0:T(512)}, f32[384,128]{1,0:T(8,128)}) custom-call(s32[2]{0:T(128)S(1)} %pad_add_fusion.place.refs_0_, bf16[1024,128]{1,0:T(8,128)(2,1)S(1)} %bitcast.15, bf16[1024,128]{1,0:T(8,128)(2,1)S(1)} %collective-permute-done.1.other, f32[8,384]{1,0:T(8,128)S(1)} %get-tuple-element.30.base_row), custom_call_target="tpu_custom_call" | custom-call | bytes 1521160 | tf_op jit(solution)/shard_map/pallas_call | solution.py:48
  (16 shorter events, 0.1 us)
Async XLA Ops:
  4.0 15.1 %copy-start = (bf16[512,384]{1,0:T(8,128)(2,1)S(1)}, bf16[512,384]{1,0:T(8,128)(2,1)}, u32[]{:S(2)}) copy-start(bf16[512,384]{1,0:T(8,128)(2,1)} %w_in.1) | copy-start | bytes 1179652
  4.0 15.1 %copy-start.1 = (bf16[8,32,512]{2,1,0:T(8,128)(2,1)S(1)}, bf16[8,32,512]{2,1,0:T(8,128)(2,1)}, u32[]{:S(2)}) copy-start(bf16[8,32,512]{2,1,0:T(8,128)(2,1)} %param.9) | copy-start | bytes 786436
  4.0 15.1 %copy-start.2 = (bf16[384,128]{1,0:T(8,128)(2,1)S(1)}, bf16[384,128]{1,0:T(8,128)(2,1)}, u32[]{:S(2)}) copy-start(bf16[384,128]{1,0:T(8,128)(2,1)} %refs_9_.1) | copy-start | bytes 294916
  4.0 15.1 %copy-start.3 = (f32[384]{0:T(512)S(1)}, f32[384]{0:T(512)}, u32[]{:S(2)}) copy-start(f32[384]{0:T(512)} %bias.1) | copy-start | bytes 4612
  4.0 15.0 %copy-start.4 = (bf16[8,128,512]{2,1,0:T(8,128)(2,1)S(1)}, bf16[8,128,512]{2,1,0:T(8,128)(2,1)}, u32[]{:S(2)}) copy-start(bf16[8,128,512]{2,1,0:T(8,128)(2,1)} %param.10) | copy-start | bytes 3145732
  4.0 43.6 %all-to-all-start = ((bf16[64,33,2,128]{3,2,1,0:T(2,128)(2,1)}), bf16[64,33,2,128]{3,2,1,0:T(2,128)(2,1)S(1)}, u32[]{:S(2)}, u32[]{:S(2)}) async-start(bf16[64,33,2,128]{3,2,1,0:T(2,128)(2,1)} %bitcast.22), calls=%async_computation | async-start | bytes 2162688 | tf_op jit(solution)/shard_map/all_to_all | solution.py:446
  19.1 28.6 %copy-start.5 = (s32[512]{0:T(512)S(1)}, s32[512]{0:T(512)}, u32[]{:S(2)}) copy-start(s32[512]{0:T(512)} %counts.1) | copy-start | bytes 6148
  21.5 1.3 copy-start.6
  22.8 1.0 copy-start.8
  47.6 39.6 %copy-start.9 = (bf16[1280,384]{1,0:T(8,128)(2,1)S(1)}, bf16[1280,384]{1,0:T(8,128)(2,1)}, u32[]{:S(2)}) copy-start(bf16[1280,384]{1,0:T(8,128)(2,1)} %copy-done.8) | copy-start | bytes 2949124
  51.5 35.7 %copy-start.7 = (f32[384,1280]{1,0:T(8,128)S(1)}, f32[384,1280]{1,0:T(8,128)}, u32[]{:S(2)}) copy-start(f32[384,1280]{1,0:T(8,128)} %copy-done.6) | copy-start | bytes 5898244
  93.2 4.5 %collective-permute-start = (bf16[1024,128]{1,0:T(8,128)(2,1)S(1)}, bf16[1024,128]{1,0:T(8,128)(2,1)S(1)}, u32[]{:S(2)}, u32[]{:S(2)}) collective-permute-start(bf16[1024,128]{1,0:T(8,128)(2,1)S(1)} %get-tuple-element.29), channel_id=1, source_target_pairs={{0,8},{8,0},{1,9},{9,1},{2,10},{10,2},{3,11},{11,3},{4,12},{12,4},... | collective-permute-start | bytes 786440 | tf_op jit(solution)/shard_map/ppermute | solution.py:566
  143.3 7.1 %collective-permute-start.1 = (bf16[1024,128]{1,0:T(8,128)(2,1)S(1)}, bf16[1024,128]{1,0:T(8,128)(2,1)S(1)}, u32[]{:S(2)}, u32[]{:S(2)}) collective-permute-start(bf16[1024,128]{1,0:T(8,128)(2,1)S(1)} %bitcast.14), channel_id=1, source_target_pairs={{0,8},{8,0},{1,9},{9,1},{2,10},{10,2},{3,11},{11,3},{4,12},{12,4},... | collective-permute-start | bytes 786440 | tf_op jit(solution)/shard_map/ppermute | solution.py:578

commit v6 on v5

--- a/solution.py
+++ b/solution.py
@@ -15,6 +15,7 @@
 META = 8
 ASK_ROWS = 2
 BACK_ROWS = 4
+GROUP = 8
 UNUSED = 100.0
 FLOOR = -1e30
 GELU_A = math.sqrt(2.0 / math.pi)
@@ -233,15 +234,41 @@
         send[first : first + BACK_ROWS, :] = tile
 
 
+def widen_kernel(weights, own, got, wide, queries, labels):
+    owner_count, rows, _ = weights.shape
+    query_len = rows // CAP
+    stride = rows + ASK_ROWS
+    size = GROUP * rows
+    lane = lax.broadcasted_iota(jnp.int32, (LANES, LANES), 1)
+    row = lax.broadcasted_iota(jnp.int32, (LANES, LANES), 0)
+    rid = jnp.sum(jnp.where(lane == row, own[2:3, :], 0.0), axis=1, keepdims=True)
+    labels[...] = jnp.broadcast_to(rid, (LANES, LANES))
+    zero = jnp.zeros((size, LANES), bf16)
+    for first in range(0, owner_count, GROUP):
+        weight = weights[first : first + GROUP].reshape(size, LANES)
+        parts = []
+        for b in range(first, first + GROUP):
+            for c in range(CAP):
+                slot = b + HALF * c
+                parts.append(jnp.broadcast_to(labels[slot : slot + 1, :], (query_len, LANES)))
+            queries[b * rows : (b + 1) * rows, :] = got[b * stride : b * stride + rows, :]
+        rid = jnp.concatenate(parts, axis=0).astype(bf16)
+        for r in range(wide.shape[1] // LANES):
+            wide[first * rows : first * rows + size, r * LANES : (r + 1) * LANES] = jnp.where(
+                rid == r, weight, zero
+            )
+
+
 def own_blocks(hid):
     return hid // LANES
 
 
 def grad_kernel(
-    place, back, got, weights, own, xl, xq, hidden_all, slope_t, w_out, loss, keep, give, base_row, grads, own_scale, ask_scale, line_acc, query_acc, *, loss_factor
+    place, back, queries, wide, own, xl, xq, hidden_all, slope_t, w_out, loss, keep, give, base_row, grads, own_scale, ask_scale, line_acc, query_acc, *, loss_factor
 ):
-    owner_count, rows, _ = weights.shape
-    stride, back_stride = rows + ASK_ROWS, rows + BACK_ROWS
+    owner_count = own_scale.shape[0]
+    rows = queries.shape[0] // owner_count
+    back_stride = rows + BACK_ROWS
     query_len = rows // CAP
     line_total = xl.shape[0]
     line_count = line_total // LANES
@@ -296,7 +323,7 @@
     own_query = jnp.where(own_pos, own_code - 8.0, own_code)
     own_grad = jnp.exp(jnp.minimum(own_match - log_total, 0.0)) - jnp.where(own_pos, 1.0, 0.0)
     own_grad = factor * jnp.sum(jnp.where(own_query == sub2, own_grad, 0.0), axis=0, keepdims=True)
-    both = jnp.where(lane2 >= 0, jnp.where(sub2 < CAP, own_grad, own[2:3, :]), 0.0)
+    both = jnp.broadcast_to(own_grad, (META, LANES))
     slot3 = HALF * (sub3 % CAP)
     own_scale[...] = jnp.broadcast_to(
         jnp.sum(
@@ -317,18 +344,11 @@
     size = owner_count * rows
     frame = (lax.broadcasted_iota(jnp.int32, (size, LANES), 0) % query_len).astype(f32)
     lane = lax.broadcasted_iota(jnp.int32, (size, LANES), 1).astype(f32)
+    one = jnp.ones((size, LANES), bf16)
     zero = jnp.zeros((size, LANES), bf16)
-    one = jnp.ones((size, LANES), bf16)
-
-    labels = own_scale[...]
-    queries = jnp.concatenate(
-        [got[b * stride : b * stride + rows, :] for b in range(owner_count)], axis=0
-    )
-    rid = spread(labels, CAP, query_len).astype(bf16)
-    weight = weights[...].reshape(size, LANES).astype(f32)
-    score = (weight * spread(labels, 0, query_len)).astype(bf16)
-    wide = jnp.concatenate([jnp.where(rid == r, score, zero) for r in range(line_count)], axis=1)
-    line_acc[...] = dot(queries, wide, 0, 0)
+
+    scaled = (queries[...].astype(f32) * spread(own_scale[...], 0, query_len)).astype(bf16)
+    line_acc[...] = dot(scaled, wide[...], 0, 0)
 
     labels = ask_scale[...]
     target = spread(labels, CAP, query_len) * float(query_len) + frame
@@ -336,14 +356,14 @@
         [back[b * back_stride : b * back_stride + rows, :] for b in range(owner_count)], axis=0
     )
     pulled = (pulled.astype(f32) * spread(labels, 0, query_len)).astype(bf16)
-    wide = jnp.concatenate(
+    hits = jnp.concatenate(
         [
             jnp.where(target == lane + float(k), one, zero)
             for k in range(0, query_acc.shape[1], LANES)
         ],
         axis=1,
     )
-    query_acc[...] = dot(pulled, wide, 0, 0)
+    query_acc[...] = dot(pulled, hits, 0, 0)
 
     grad_in = None
     grad_out = None
@@ -353,7 +373,8 @@
     for acc, x, first, span in spans:
         g_hi, g_lo = split2(acc[:, 0:span])
         grad_hidden = dot(w_out[...], g_hi) + dot(w_out[...], g_lo)
-        p_hi, p_lo = split2(grad_hidden * slope_t[:, first : first + span])
+        grad_pre = grad_hidden * slope_t[:, first : first + span]
+        p_hi = grad_pre.astype(bf16)
         hidden = hidden_all[first : first + span, :]
         ones = jnp.ones((META, span), bf16)
         part_in = dot(p_hi, x[...])
@@ -361,10 +382,11 @@
         part_out -= jnp.sum(g_hi.astype(f32) + g_lo.astype(f32), axis=1, keepdims=True) * shared
         part_sum = dot(ones, g_hi, 1, 1) + dot(ones, g_lo, 1, 1)
         vec_sum = part_sum if vec_sum is None else vec_sum + part_sum
-        part_bias = dot(ones, p_hi, 1, 1) + dot(ones, p_lo, 1, 1)
+        part_bias = sum(grad_pre[:, k : k + LANES] for k in range(0, span, LANES))
         grad_in = part_in if grad_in is None else grad_in + part_in
         grad_out = part_out if grad_out is None else grad_out + part_out
         grad_bias = part_bias if grad_bias is None else grad_bias + part_bias
+    grad_bias = jnp.sum(grad_bias.T, axis=0, keepdims=True)
     base = 0
     for k in range(0, x.shape[1], LANES):
         grads[base : base + hid, :] = grad_in[:, k : k + LANES]
@@ -535,6 +557,15 @@
         flops=2 * match_flops,
     )
     back = exchange_rows(answer, ARCHIVE, owner_count, BACK_ROWS)
+    slot_rows = owner_count * rows
+    wide, queries = call(
+        widen_kernel,
+        [shape_of((slot_rows, frames_l), bf16), shape_of((slot_rows, vec_width), bf16)],
+        [weights, own, got],
+        0,
+        [pltpu.VMEM((LANES, LANES), f32)],
+        flops=slot_rows * frames_l,
+    )
     unit = 16 * owner_count
     flat_rows = unit * -(-(LANES + (feat + vec_width) * hid // LANES) // unit)
     half = flat_rows // 2
@@ -550,7 +581,7 @@
             shape_of((half, LANES), bf16),
             shape_of((META, hid), f32),
         ],
-        [place, back, got, weights, own, xl, xq, hidden_all, slope_t, w_out],
+        [place, back, queries, wide, own, xl, xq, hidden_all, slope_t, w_out],
         1,
         [
             pltpu.VMEM((flat_rows, LANES), f32),

time: 153 us -> 161 us (1.052)
  blocking collectives: 80.5 us -> 44.8 us
  waiting for transfers between devices: 25.4 us -> 46.3 us
  local copies, waits for them, and re-layouts: 2.94 us -> 14.3 us
  starting transfers between devices: 24.3 us -> 30.9 us
  Pallas kernels: 18 us -> 23.5 us
    all_to_all x4 -> x3, blocking collectives: 80.5 us -> 44.8 us  [exchange(): return lax.all_to_all(x, axis, split_axis=0, concat_axis=0, tiled=True)]
    all_to_all x1 -> x2, waiting for transfers between devices: 23.8 us -> 44.7 us  [exchange(): return lax.all_to_all(x, axis, split_axis=0, concat_axis=0, tiled=True)]
    unnamed x20 -> x32, local copies, waits for them, and re-layouts: 2.31 us -> 13.7 us
    all_to_all x1 -> x2, starting transfers between devices: 15 us -> 21.5 us  [exchange(): return lax.all_to_all(x, axis, split_axis=0, concat_axis=0, tiled=True)]
    pallas_call x8 -> x9, Pallas kernels: 18 us -> 23.5 us  [call(): pl.pallas_call(body, out_shape=tuple(outs), in_specs=[smem] * smem_count...]
  transfers between devices with their start and end apart: 3 -> 4, of which waited for: 3 -> 4; matrix products, arithmetic and copies ran while one was open for 0% -> 0% of each run, Pallas kernels for 2% -> 3%
where the time goes in v6:
time: 161 us
  waiting for transfers between devices  46.3 us (29%)
  blocking collectives  44.8 us (28%)
  starting transfers between devices  30.9 us (19%)
  Pallas kernels  23.5 us (15%)
  local copies, waits for them, and re-layouts  14.3 us (9%)
    all_to_all x3, blocking collectives, exchange(): return lax.all_to_all(x, axis, split_axis=0, concat_axis=0, tiled=True)  44.8 us
    all_to_all x2, waiting for transfers between devices, exchange(): return lax.all_to_all(x, axis, split_axis=0, concat_axis=0, tiled=True)  44.7 us
    pallas_call x9, Pallas kernels, call(): pl.pallas_call(body, out_shape=tuple(outs), in_specs=[smem] * smem_count...  23.5 us
    all_to_all x2, starting transfers between devices, exchange(): return lax.all_to_all(x, axis, split_axis=0, concat_axis=0, tiled=True)  21.5 us
    unnamed x32, local copies, waits for them, and re-layouts  13.7 us
    ppermute x1, starting transfers between devices, local(): other = lax.ppermute(mine, 'core', swap)  5.95 us
    ppermute x1, starting transfers between devices, local(): taken = lax.ppermute(give, 'core', swap)  3.41 us
  transfers between devices with their start and end apart: 4, of which 4 were waited for; matrix products, arithmetic and copies ran while one was open for 0% of the time, Pallas kernels for 3%

profile of v6, /device:TPU:1, one launch (start us, length us, event | category | flops | bytes accessed | tf_op | source)
XLA Modules:
  0.0 160.7 jit_solution(14432979407475893368)
XLA Ops:
  0.6 3.4 %shard_map.120 = bf16[4224,128]{1,0:T(8,128)(2,1)} custom-call(s32[8,6]{1,0:T(8,128)} %mined_hbm.1, s32[512]{0:T(512)} %home_hbm.1, s32[8]{0:T(128)} %positive_hbm.1, bf16[256,512]{1,0:T(8,128)(2,1)} %bitcast.13, bf16[512,384]{1,0:T(8,128)(2,1)} %w_in.1, f32[384]{0:T(512)} %bias.1, bf16[384,128]{1,0:T(8,128)(2,1)} %refs_9_.1), custom_call_target="tpu_custom_call" | custom-call | flops 125829120 | bytes 1838816 | tf_op jit(solution)/shard_map/pallas_call | solution.py:49
  4.1 15.0 %all-to-all-start = ((bf16[64,33,2,128]{3,2,1,0:T(2,128)(2,1)}), bf16[64,33,2,128]{3,2,1,0:T(2,128)(2,1)S(1)}, u32[]{:S(2)}, u32[]{:S(2)}) async-start(bf16[64,33,2,128]{3,2,1,0:T(2,128)(2,1)} %bitcast.21), calls=%async_computation | async-start | bytes 2162688 | tf_op jit(solution)/shard_map/all_to_all | solution.py:468
  19.1 2.4 %shard_map.121 = (bf16[8,128,128]{2,1,0:T(8,128)(2,1)S(1)}, bf16[8,128,128]{2,1,0:T(8,128)(2,1)S(1)}, bf16[1280,384]{1,0:T(8,128)(2,1)S(1)}, f32[384,1280]{1,0:T(8,128)S(1)}, f32[8,384]{1,0:T(8,128)S(1)}) custom-call(bf16[1024,512]{1,0:T(8,128)(2,1)S(1)} %bitcast.16, bf16[256,512]{1,0:T(8,128)(2,1)S(1)} %bitcast.14, bf16[512,384]{1,0:T(8,128)(2,1)S(1)} %copy-done.13, ...), custom_call_target="tpu_custom_call" | custom-call | flops 629145600 | bytes 5289472 | tf_op jit(solution)/shard_map/pallas_call | solution.py:49
  21.6 1.3 copy-done.1
  22.9 1.0 copy-done.9
  24.0 23.7 %all-to-all-done = bf16[64,33,2,128]{3,2,1,0:T(2,128)(2,1)S(1)} async-done(((bf16[64,33,2,128]{3,2,1,0:T(2,128)(2,1)}), bf16[64,33,2,128]{3,2,1,0:T(2,128)(2,1)S(1)}, u32[]{:S(2)}, u32[]{:S(2)}) %all-to-all-start) | async-done | bytes 1081376 | tf_op jit(solution)/shard_map/all_to_all | solution.py:468
  47.7 4.9 %shard_map.122 = (bf16[4352,128]{1,0:T(8,128)(2,1)}, bf16[64,64,128]{2,1,0:T(8,128)(2,1)S(1)}, f32[8,128]{1,0:T(8,128)S(1)}) custom-call(s32[2]{0:T(128)S(1)} %pad_add_fusion.place.refs_0_, s32[512]{0:T(512)S(1)} %copy-done.15, bf16[4224,128]{1,0:T(8,128)(2,1)S(1)} %bitcast.11, bf16[8,128,128]{2,1,0:T(8,128)(2,1)S(1)} %get-tuple-element.21.line_vec, ...), custom_call_target="tpu_custom_call" | custom-call | flops 2147483648 | bytes 3786760 | tf_op jit(solution)/shard_map/pallas_call | solution.py:49
  53.5 6.5 %all-to-all-start.1 = ((bf16[64,17,4,128]{3,2,1,0:T(4,128)(2,1)}), bf16[64,17,4,128]{3,2,1,0:T(4,128)(2,1)S(1)}, u32[]{:S(2)}, u32[]{:S(2)}) async-start(bf16[64,17,4,128]{3,2,1,0:T(4,128)(2,1)} %bitcast.6), calls=%async_computation.1 | async-start | bytes 2228224 | tf_op jit(solution)/shard_map/all_to_all | solution.py:468
  60.1 1.2 copy-done.8
  61.3 2.7 %shard_map.123 = (bf16[4096,1024]{1,0:T(8,128)(2,1)S(1)}, bf16[4096,128]{1,0:T(8,128)(2,1)S(1)}) custom-call(bf16[64,64,128]{2,1,0:T(8,128)(2,1)S(1)} %copy-done.8, f32[8,128]{1,0:T(8,128)S(1)} %get-tuple-element.26.own.refs_4_, bf16[4224,128]{1,0:T(8,128)(2,1)S(1)} %bitcast.12), custom_call_target="tpu_custom_call" | custom-call | flops 4194304 | bytes 11571200 | tf_op jit(solution)/shard_map/pallas_call | solution.py:49
  64.1 3.2 %copy-done = bf16[4096,1024]{1,0:T(8,128)(2,1)} copy-done((bf16[4096,1024]{1,0:T(8,128)(2,1)}, bf16[4096,1024]{1,0:T(8,128)(2,1)S(1)}, u32[]{:S(2)}) %copy-start) | copy-done | bytes 8388632
  67.3 1.0 copy-done.5
  68.3 21.0 %all-to-all-done.1 = bf16[64,17,4,128]{3,2,1,0:T(4,128)(2,1)S(1)} async-done(((bf16[64,17,4,128]{3,2,1,0:T(4,128)(2,1)}), bf16[64,17,4,128]{3,2,1,0:T(4,128)(2,1)S(1)}, u32[]{:S(2)}, u32[]{:S(2)}) %all-to-all-start.1) | async-done | bytes 1114144 | tf_op jit(solution)/shard_map/all_to_all | solution.py:468
  89.3 1.5 copy-done.2
  90.8 1.2 copy-done.6
  92.1 1.2 copy-done.10
  94.2 7.6 %shard_map.124 = (f32[8,128]{1,0:T(8,128)S(1)}, f32[1024,128]{1,0:T(8,128)S(1)}, bf16[1024,128]{1,0:T(8,128)(2,1)S(1)}, f32[8,384]{1,0:T(8,128)S(1)}) custom-call(s32[2]{0:T(128)S(1)} %pad_add_fusion.place.refs_0_, bf16[4352,128]{1,0:T(8,128)(2,1)S(1)} %bitcast.10, bf16[4096,128]{1,0:T(8,128)(2,1)S(1)} %copy-done.6, bf16[4096,1024]{1,0:T(8,128)(2,1)} %copy-done, ...), custom_call_target="tpu_custom_call" | custom-call | flops 3590324224 | bytes 15716360 | tf_op jit(solution)/shard_map/pallas_call | solution.py:49
  101.8 3.4 %collective-permute-start = (bf16[1024,128]{1,0:T(8,128)(2,1)S(1)}, bf16[1024,128]{1,0:T(8,128)(2,1)S(1)}, u32[]{:S(2)}, u32[]{:S(2)}) collective-permute-start(bf16[1024,128]{1,0:T(8,128)(2,1)S(1)} %get-tuple-element.33), channel_id=1, source_target_pairs={{0,8},{8,0},{1,9},{9,1},{2,10},{10,2},{3,11},{11,3},{4,12},{12,4},... | collective-permute-start | bytes 786440 | tf_op jit(solution)/shard_map/ppermute | solution.py:597
  105.2 1.1 collective-permute-done.refs_2_
  107.0 16.0 %all_to_all.25.got = bf16[32,32,128]{2,1,0:T(8,128)(2,1)S(1)} all-to-all(bf16[32,32,128]{2,1,0:T(8,128)(2,1)S(1)} %bitcast.20), channel_id=1, replica_groups=mesh['chip'=32,'core'=2,'dp'=8] {'chip'}, dimensions={0} | all-to-all | bytes 524288 | tf_op jit(solution)/shard_map/all_to_all | solution.py:468
  123.1 13.8 %all_to_all.26.got = bf16[8,32,128]{2,1,0:T(8,128)(2,1)S(1)} all-to-all(bf16[8,32,128]{2,1,0:T(8,128)(2,1)S(1)} %shard_map.126), channel_id=1, replica_groups=mesh['chip'=32,'core'=2,'dp'=8] {'dp'}, dimensions={0} | all-to-all | bytes 131072 | tf_op jit(solution)/shard_map/all_to_all | solution.py:468
  136.9 15.0 %all_to_all.27 = bf16[32,32,128]{2,1,0:T(8,128)(2,1)S(1)} all-to-all(bf16[32,32,128]{2,1,0:T(8,128)(2,1)S(1)} %shard_map.127), channel_id=1, replica_groups=mesh['chip'=32,'core'=2,'dp'=8] {'chip'}, dimensions={0} | all-to-all | bytes 524288 | tf_op jit(solution)/shard_map/all_to_all | solution.py:468
  151.9 6.0 %collective-permute-start.1 = (bf16[1024,128]{1,0:T(8,128)(2,1)S(1)}, bf16[1024,128]{1,0:T(8,128)(2,1)S(1)}, u32[]{:S(2)}, u32[]{:S(2)}) collective-permute-start(bf16[1024,128]{1,0:T(8,128)(2,1)S(1)} %bitcast.18), channel_id=1, source_target_pairs={{0,8},{8,0},{1,9},{9,1},{2,10},{10,2},{3,11},{11,3},{4,12},{12,4},... | collective-permute-start | bytes 786440 | tf_op jit(solution)/shard_map/ppermute | solution.py:609
  159.0 1.7 %shard_map.128 = (f32[512,384]{1,0:T(8,128)}, f32[384]{0:T(512)}, f32[384,128]{1,0:T(8,128)}) custom-call(s32[2]{0:T(128)S(1)} %pad_add_fusion.place.refs_0_, bf16[1024,128]{1,0:T(8,128)(2,1)S(1)} %bitcast.19, bf16[1024,128]{1,0:T(8,128)(2,1)S(1)} %collective-permute-done.1.other, f32[8,384]{1,0:T(8,128)S(1)} %get-tuple-element.34.base_row), custom_call_target="tpu_custom_call" | custom-call | bytes 1521160 | tf_op jit(solution)/shard_map/pallas_call | solution.py:49
  (30 shorter events, 3.8 us)
Async XLA Ops:
  4.0 15.1 %copy-start.3 = (bf16[8,32,512]{2,1,0:T(8,128)(2,1)S(1)}, bf16[8,32,512]{2,1,0:T(8,128)(2,1)}, u32[]{:S(2)}) copy-start(bf16[8,32,512]{2,1,0:T(8,128)(2,1)} %param.9) | copy-start | bytes 786436
  4.0 15.1 %copy-start.4 = (bf16[8,128,512]{2,1,0:T(8,128)(2,1)S(1)}, bf16[8,128,512]{2,1,0:T(8,128)(2,1)}, u32[]{:S(2)}) copy-start(bf16[8,128,512]{2,1,0:T(8,128)(2,1)} %param.10) | copy-start | bytes 3145732
  4.0 15.1 %copy-start.11 = (bf16[384,128]{1,0:T(8,128)(2,1)S(1)}, bf16[384,128]{1,0:T(8,128)(2,1)}, u32[]{:S(2)}) copy-start(bf16[384,128]{1,0:T(8,128)(2,1)} %refs_9_.1) | copy-start | bytes 294916
  4.1 15.1 %copy-start.13 = (bf16[512,384]{1,0:T(8,128)(2,1)S(1)}, bf16[512,384]{1,0:T(8,128)(2,1)}, u32[]{:S(2)}) copy-start(bf16[512,384]{1,0:T(8,128)(2,1)} %w_in.1) | copy-start | bytes 1179652
  4.1 15.0 %copy-start.14 = (f32[384]{0:T(512)S(1)}, f32[384]{0:T(512)}, u32[]{:S(2)}) copy-start(f32[384]{0:T(512)} %bias.1) | copy-start | bytes 4612
  4.1 43.6 %all-to-all-start = ((bf16[64,33,2,128]{3,2,1,0:T(2,128)(2,1)}), bf16[64,33,2,128]{3,2,1,0:T(2,128)(2,1)S(1)}, u32[]{:S(2)}, u32[]{:S(2)}) async-start(bf16[64,33,2,128]{3,2,1,0:T(2,128)(2,1)} %bitcast.21), calls=%async_computation | async-start | bytes 2162688 | tf_op jit(solution)/shard_map/all_to_all | solution.py:468
  19.1 28.6 %copy-start.15 = (s32[512]{0:T(512)S(1)}, s32[512]{0:T(512)}, u32[]{:S(2)}) copy-start(s32[512]{0:T(512)} %counts.1) | copy-start | bytes 6148
  21.6 1.3 copy-start.1
  22.9 1.0 copy-start.9
  52.5 1.0 copy-start.7
  53.5 35.8 %all-to-all-start.1 = ((bf16[64,17,4,128]{3,2,1,0:T(4,128)(2,1)}), bf16[64,17,4,128]{3,2,1,0:T(4,128)(2,1)S(1)}, u32[]{:S(2)}, u32[]{:S(2)}) async-start(bf16[64,17,4,128]{3,2,1,0:T(4,128)(2,1)} %bitcast.6), calls=%async_computation.1 | async-start | bytes 2228224 | tf_op jit(solution)/shard_map/all_to_all | solution.py:468
  60.1 1.2 copy-start.8
  64.0 3.3 %copy-start = (bf16[4096,1024]{1,0:T(8,128)(2,1)}, bf16[4096,1024]{1,0:T(8,128)(2,1)S(1)}, u32[]{:S(2)}) copy-start(bf16[4096,1024]{1,0:T(8,128)(2,1)S(1)} %get-tuple-element.28.refs_3_) | copy-start | bytes 25165828
  67.3 1.0 copy-start.5
  89.3 1.5 copy-start.2
  90.8 1.2 copy-start.6
  92.1 1.2 copy-start.10
  93.3 0.9 copy-start.12
  101.8 4.6 %collective-permute-start = (bf16[1024,128]{1,0:T(8,128)(2,1)S(1)}, bf16[1024,128]{1,0:T(8,128)(2,1)S(1)}, u32[]{:S(2)}, u32[]{:S(2)}) collective-permute-start(bf16[1024,128]{1,0:T(8,128)(2,1)S(1)} %get-tuple-element.33), channel_id=1, source_target_pairs={{0,8},{8,0},{1,9},{9,1},{2,10},{10,2},{3,11},{11,3},{4,12},{12,4},... | collective-permute-start | bytes 786440 | tf_op jit(solution)/shard_map/ppermute | solution.py:597
  151.9 7.1 %collective-permute-start.1 = (bf16[1024,128]{1,0:T(8,128)(2,1)S(1)}, bf16[1024,128]{1,0:T(8,128)(2,1)S(1)}, u32[]{:S(2)}, u32[]{:S(2)}) collective-permute-start(bf16[1024,128]{1,0:T(8,128)(2,1)S(1)} %bitcast.18), channel_id=1, source_target_pairs={{0,8},{8,0},{1,9},{9,1},{2,10},{10,2},{3,11},{11,3},{4,12},{12,4},... | collective-permute-start | bytes 786440 | tf_op jit(solution)/shard_map/ppermute | solution.py:609

commit v7 on v5

--- a/solution.py
+++ b/solution.py
@@ -353,7 +353,8 @@
     for acc, x, first, span in spans:
         g_hi, g_lo = split2(acc[:, 0:span])
         grad_hidden = dot(w_out[...], g_hi) + dot(w_out[...], g_lo)
-        p_hi, p_lo = split2(grad_hidden * slope_t[:, first : first + span])
+        grad_pre = grad_hidden * slope_t[:, first : first + span]
+        p_hi = grad_pre.astype(bf16)
         hidden = hidden_all[first : first + span, :]
         ones = jnp.ones((META, span), bf16)
         part_in = dot(p_hi, x[...])
@@ -361,10 +362,11 @@
         part_out -= jnp.sum(g_hi.astype(f32) + g_lo.astype(f32), axis=1, keepdims=True) * shared
         part_sum = dot(ones, g_hi, 1, 1) + dot(ones, g_lo, 1, 1)
         vec_sum = part_sum if vec_sum is None else vec_sum + part_sum
-        part_bias = dot(ones, p_hi, 1, 1) + dot(ones, p_lo, 1, 1)
+        part_bias = sum(grad_pre[:, k : k + LANES] for k in range(0, span, LANES))
         grad_in = part_in if grad_in is None else grad_in + part_in
         grad_out = part_out if grad_out is None else grad_out + part_out
         grad_bias = part_bias if grad_bias is None else grad_bias + part_bias
+    grad_bias = jnp.sum(grad_bias.T, axis=0, keepdims=True)
     base = 0
     for k in range(0, x.shape[1], LANES):
         grads[base : base + hid, :] = grad_in[:, k : k + LANES]

time: 153 us -> 151 us (0.987)
  no operation moved by 1% of the time
where the time goes in v7:
time: 151 us
  blocking collectives  80.5 us (53%)
  waiting for transfers between devices  25.4 us (17%)
  starting transfers between devices  24.3 us (16%)
  Pallas kernels  16.5 us (11%)
  local copies, waits for them, and re-layouts  2.94 us (2%)
    all_to_all x4, blocking collectives, exchange(): return lax.all_to_all(x, axis, split_axis=0, concat_axis=0, tiled=True)  80.5 us
    all_to_all x1, waiting for transfers between devices, exchange(): return lax.all_to_all(x, axis, split_axis=0, concat_axis=0, tiled=True)  23.8 us
    pallas_call x8, Pallas kernels, call(): pl.pallas_call(body, out_shape=tuple(outs), in_specs=[smem] * smem_count...  16.5 us
    all_to_all x1, starting transfers between devices, exchange(): return lax.all_to_all(x, axis, split_axis=0, concat_axis=0, tiled=True)  15 us
    ppermute x1, starting transfers between devices, local(): other = lax.ppermute(mine, 'core', swap)  5.95 us
    ppermute x1, starting transfers between devices, local(): taken = lax.ppermute(give, 'core', swap)  3.41 us
  transfers between devices with their start and end apart: 3, of which 3 were waited for; matrix products, arithmetic and copies ran while one was open for 0% of the time, Pallas kernels for 2%

profile of v7, /device:TPU:1, one launch (start us, length us, event | category | flops | bytes accessed | tf_op | source)
XLA Modules:
  0.0 150.6 jit_solution(2245374666833765396)
XLA Ops:
  0.6 3.3 %shard_map.120 = bf16[4224,128]{1,0:T(8,128)(2,1)} custom-call(s32[8,6]{1,0:T(8,128)} %mined_hbm.1, s32[512]{0:T(512)} %home_hbm.1, s32[8]{0:T(128)} %positive_hbm.1, bf16[256,512]{1,0:T(8,128)(2,1)} %bitcast.17, bf16[512,384]{1,0:T(8,128)(2,1)} %w_in.1, f32[384]{0:T(512)} %bias.1, bf16[384,128]{1,0:T(8,128)(2,1)} %refs_9_.1), custom_call_target="tpu_custom_call" | custom-call | flops 125829120 | bytes 1838816 | tf_op jit(solution)/shard_map/pallas_call | solution.py:48
  4.0 0.0 copy-start
  4.0 0.0 copy-start.1
  4.0 0.0 copy-start.3
  4.0 0.0 copy-start.4
  4.0 15.0 %all-to-all-start = ((bf16[64,33,2,128]{3,2,1,0:T(2,128)(2,1)}), bf16[64,33,2,128]{3,2,1,0:T(2,128)(2,1)S(1)}, u32[]{:S(2)}, u32[]{:S(2)}) async-start(bf16[64,33,2,128]{3,2,1,0:T(2,128)(2,1)} %bitcast.22), calls=%async_computation | async-start | bytes 2162688 | tf_op jit(solution)/shard_map/all_to_all | solution.py:448
  19.1 2.4 %shard_map.121 = (bf16[8,128,128]{2,1,0:T(8,128)(2,1)S(1)}, bf16[8,128,128]{2,1,0:T(8,128)(2,1)S(1)}, bf16[1280,384]{1,0:T(8,128)(2,1)S(1)}, f32[384,1280]{1,0:T(8,128)S(1)}, f32[8,384]{1,0:T(8,128)S(1)}) custom-call(bf16[1024,512]{1,0:T(8,128)(2,1)S(1)} %bitcast.20, bf16[256,512]{1,0:T(8,128)(2,1)S(1)} %bitcast.18, bf16[512,384]{1,0:T(8,128)(2,1)S(1)} %copy-done, ...), custom_call_target="tpu_custom_call" | custom-call | flops 629145600 | bytes 5289472 | tf_op jit(solution)/shard_map/pallas_call | solution.py:48
  21.5 1.3 copy-done.6
  22.8 1.0 copy-done.8
  23.8 0.1 pad_add_fusion.place.refs_0_
  23.9 23.8 %all-to-all-done = bf16[64,33,2,128]{3,2,1,0:T(2,128)(2,1)S(1)} async-done(((bf16[64,33,2,128]{3,2,1,0:T(2,128)(2,1)}), bf16[64,33,2,128]{3,2,1,0:T(2,128)(2,1)S(1)}, u32[]{:S(2)}, u32[]{:S(2)}) %all-to-all-start) | async-done | bytes 1081376 | tf_op jit(solution)/shard_map/all_to_all | solution.py:448
  47.6 3.9 %shard_map.122 = (bf16[4352,128]{1,0:T(8,128)(2,1)S(1)}, bf16[64,64,128]{2,1,0:T(8,128)(2,1)S(1)}, f32[8,128]{1,0:T(8,128)S(1)}) custom-call(s32[2]{0:T(128)S(1)} %pad_add_fusion.place.refs_0_, s32[512]{0:T(512)S(1)} %copy-done.5, bf16[4224,128]{1,0:T(8,128)(2,1)S(1)} %bitcast.12, bf16[8,128,128]{2,1,0:T(8,128)(2,1)S(1)} %get-tuple-element.19.line_vec, ...), custom_call_target="tpu_custom_call" | custom-call | flops 2147483648 | bytes 3786760 | tf_op jit(solution)/shard_map/pallas_call | solution.py:48
  51.5 35.7 %all_to_all.25 = bf16[64,17,4,128]{3,2,1,0:T(4,128)(2,1)S(1)} all-to-all(bf16[64,17,4,128]{3,2,1,0:T(4,128)(2,1)S(1)} %bitcast.11), channel_id=1, replica_groups=mesh['chip'=32,'core'=2,'dp'=8] {'chip','core'}, dimensions={0} | all-to-all | bytes 2228224 | tf_op jit(solution)/shard_map/all_to_all | solution.py:448
  87.2 4.5 %shard_map.123 = (f32[8,128]{1,0:T(8,128)S(1)}, f32[1024,128]{1,0:T(8,128)S(1)}, bf16[1024,128]{1,0:T(8,128)(2,1)S(1)}, f32[8,384]{1,0:T(8,128)S(1)}) custom-call(s32[2]{0:T(128)S(1)} %pad_add_fusion.place.refs_0_, bf16[4352,128]{1,0:T(8,128)(2,1)S(1)} %bitcast.10, bf16[4224,128]{1,0:T(8,128)(2,1)S(1)} %bitcast.13, ...), custom_call_target="tpu_custom_call" | custom-call | flops 3590324224 | bytes 8409096 | tf_op jit(solution)/shard_map/pallas_call | solution.py:48
  91.7 3.4 %collective-permute-start = (bf16[1024,128]{1,0:T(8,128)(2,1)S(1)}, bf16[1024,128]{1,0:T(8,128)(2,1)S(1)}, u32[]{:S(2)}, u32[]{:S(2)}) collective-permute-start(bf16[1024,128]{1,0:T(8,128)(2,1)S(1)} %get-tuple-element.29), channel_id=1, source_target_pairs={{0,8},{8,0},{1,9},{9,1},{2,10},{10,2},{3,11},{11,3},{4,12},{12,4},... | collective-permute-start | bytes 786440 | tf_op jit(solution)/shard_map/ppermute | solution.py:568
  95.1 1.1 collective-permute-done.refs_2_
  96.3 0.6 shard_map.124
  96.9 16.0 %all_to_all.26.got = bf16[32,32,128]{2,1,0:T(8,128)(2,1)S(1)} all-to-all(bf16[32,32,128]{2,1,0:T(8,128)(2,1)S(1)} %bitcast.16), channel_id=1, replica_groups=mesh['chip'=32,'core'=2,'dp'=8] {'chip'}, dimensions={0} | all-to-all | bytes 524288 | tf_op jit(solution)/shard_map/all_to_all | solution.py:448
  112.9 13.8 %all_to_all.27.got = bf16[8,32,128]{2,1,0:T(8,128)(2,1)S(1)} all-to-all(bf16[8,32,128]{2,1,0:T(8,128)(2,1)S(1)} %shard_map.125), channel_id=1, replica_groups=mesh['chip'=32,'core'=2,'dp'=8] {'dp'}, dimensions={0} | all-to-all | bytes 131072 | tf_op jit(solution)/shard_map/all_to_all | solution.py:448
  126.8 15.0 %all_to_all.28 = bf16[32,32,128]{2,1,0:T(8,128)(2,1)S(1)} all-to-all(bf16[32,32,128]{2,1,0:T(8,128)(2,1)S(1)} %shard_map.126), channel_id=1, replica_groups=mesh['chip'=32,'core'=2,'dp'=8] {'chip'}, dimensions={0} | all-to-all | bytes 524288 | tf_op jit(solution)/shard_map/all_to_all | solution.py:448
  141.8 6.0 %collective-permute-start.1 = (bf16[1024,128]{1,0:T(8,128)(2,1)S(1)}, bf16[1024,128]{1,0:T(8,128)(2,1)S(1)}, u32[]{:S(2)}, u32[]{:S(2)}) collective-permute-start(bf16[1024,128]{1,0:T(8,128)(2,1)S(1)} %bitcast.14), channel_id=1, source_target_pairs={{0,8},{8,0},{1,9},{9,1},{2,10},{10,2},{3,11},{11,3},{4,12},{12,4},... | collective-permute-start | bytes 786440 | tf_op jit(solution)/shard_map/ppermute | solution.py:580
  147.7 0.6 slice_reduce_fusion
  148.3 0.5 collective-permute-done.1.other
  148.8 1.7 %shard_map.127 = (f32[512,384]{1,0:T(8,128)}, f32[384]{0:T(512)}, f32[384,128]{1,0:T(8,128)}) custom-call(s32[2]{0:T(128)S(1)} %pad_add_fusion.place.refs_0_, bf16[1024,128]{1,0:T(8,128)(2,1)S(1)} %bitcast.15, bf16[1024,128]{1,0:T(8,128)(2,1)S(1)} %collective-permute-done.1.other, f32[8,384]{1,0:T(8,128)S(1)} %get-tuple-element.30.base_row), custom_call_target="tpu_custom_call" | custom-call | bytes 1521160 | tf_op jit(solution)/shard_map/pallas_call | solution.py:48
  (16 shorter events, 0.1 us)
Async XLA Ops:
  4.0 15.1 %copy-start = (bf16[512,384]{1,0:T(8,128)(2,1)S(1)}, bf16[512,384]{1,0:T(8,128)(2,1)}, u32[]{:S(2)}) copy-start(bf16[512,384]{1,0:T(8,128)(2,1)} %w_in.1) | copy-start | bytes 1179652
  4.0 15.1 %copy-start.1 = (bf16[8,32,512]{2,1,0:T(8,128)(2,1)S(1)}, bf16[8,32,512]{2,1,0:T(8,128)(2,1)}, u32[]{:S(2)}) copy-start(bf16[8,32,512]{2,1,0:T(8,128)(2,1)} %param.9) | copy-start | bytes 786436
  4.0 15.1 %copy-start.2 = (bf16[384,128]{1,0:T(8,128)(2,1)S(1)}, bf16[384,128]{1,0:T(8,128)(2,1)}, u32[]{:S(2)}) copy-start(bf16[384,128]{1,0:T(8,128)(2,1)} %refs_9_.1) | copy-start | bytes 294916
  4.0 15.1 %copy-start.3 = (f32[384]{0:T(512)S(1)}, f32[384]{0:T(512)}, u32[]{:S(2)}) copy-start(f32[384]{0:T(512)} %bias.1) | copy-start | bytes 4612
  4.0 15.0 %copy-start.4 = (bf16[8,128,512]{2,1,0:T(8,128)(2,1)S(1)}, bf16[8,128,512]{2,1,0:T(8,128)(2,1)}, u32[]{:S(2)}) copy-start(bf16[8,128,512]{2,1,0:T(8,128)(2,1)} %param.10) | copy-start | bytes 3145732
  4.0 43.6 %all-to-all-start = ((bf16[64,33,2,128]{3,2,1,0:T(2,128)(2,1)}), bf16[64,33,2,128]{3,2,1,0:T(2,128)(2,1)S(1)}, u32[]{:S(2)}, u32[]{:S(2)}) async-start(bf16[64,33,2,128]{3,2,1,0:T(2,128)(2,1)} %bitcast.22), calls=%async_computation | async-start | bytes 2162688 | tf_op jit(solution)/shard_map/all_to_all | solution.py:448
  19.1 28.6 %copy-start.5 = (s32[512]{0:T(512)S(1)}, s32[512]{0:T(512)}, u32[]{:S(2)}) copy-start(s32[512]{0:T(512)} %counts.1) | copy-start | bytes 6148
  21.5 1.3 copy-start.6
  22.8 1.0 copy-start.8
  47.6 39.6 %copy-start.9 = (bf16[1280,384]{1,0:T(8,128)(2,1)S(1)}, bf16[1280,384]{1,0:T(8,128)(2,1)}, u32[]{:S(2)}) copy-start(bf16[1280,384]{1,0:T(8,128)(2,1)} %copy-done.8) | copy-start | bytes 2949124
  51.5 35.7 %copy-start.7 = (f32[384,1280]{1,0:T(8,128)S(1)}, f32[384,1280]{1,0:T(8,128)}, u32[]{:S(2)}) copy-start(f32[384,1280]{1,0:T(8,128)} %copy-done.6) | copy-start | bytes 5898244
  91.7 4.6 %collective-permute-start = (bf16[1024,128]{1,0:T(8,128)(2,1)S(1)}, bf16[1024,128]{1,0:T(8,128)(2,1)S(1)}, u32[]{:S(2)}, u32[]{:S(2)}) collective-permute-start(bf16[1024,128]{1,0:T(8,128)(2,1)S(1)} %get-tuple-element.29), channel_id=1, source_target_pairs={{0,8},{8,0},{1,9},{9,1},{2,10},{10,2},{3,11},{11,3},{4,12},{12,4},... | collective-permute-start | bytes 786440 | tf_op jit(solution)/shard_map/ppermute | solution.py:568
  141.8 7.1 %collective-permute-start.1 = (bf16[1024,128]{1,0:T(8,128)(2,1)S(1)}, bf16[1024,128]{1,0:T(8,128)(2,1)S(1)}, u32[]{:S(2)}, u32[]{:S(2)}) collective-permute-start(bf16[1024,128]{1,0:T(8,128)(2,1)S(1)} %bitcast.14), channel_id=1, source_target_pairs={{0,8},{8,0},{1,9},{9,1},{2,10},{10,2},{3,11},{11,3},{4,12},{12,4},... | collective-permute-start | bytes 786440 | tf_op jit(solution)/shard_map/ppermute | solution.py:580

commit v8 on v7

--- a/solution.py
+++ b/solution.py
@@ -91,7 +91,7 @@
             code[c, owner] = int(UNUSED)
         return carry
 
-    lax.fori_loop(0, owner_count, clear, 0, unroll=8)
+    lax.fori_loop(0, owner_count, clear, 0, unroll=True)
     stage[...] = jnp.zeros(stage.shape, bf16)
     for copy in copies[:3]:
         copy.wait()
@@ -108,7 +108,12 @@
             goal_rank[query, j] = rank * query_len
         return carry
 
-    lax.fori_loop(0, query_count, assign, 0, unroll=2)
+    lax.fori_loop(0, query_count, assign, 0, unroll=True)
+    for copy in copies[3:]:
+        copy.wait()
+    _, hidden = gelu_parts(dot(x[...], w_in[...]) + bias[...].reshape(1, -1))
+    vec[...] = dot(hidden, w_out[...]).astype(bf16)
+
     sub = lax.broadcasted_iota(jnp.int32, (ASK_ROWS, LANES), 0)
     low = lax.broadcasted_iota(jnp.int32, (ASK_ROWS, LANES), 1) < HALF
     for owner in range(owner_count):
@@ -119,11 +124,6 @@
         )
         first = owner * stride + rows
         send[first : first + ASK_ROWS, :] = tile.astype(f32).astype(bf16)
-    for copy in copies[3:]:
-        copy.wait()
-    _, hidden = gelu_parts(dot(x[...], w_in[...]) + bias[...].reshape(1, -1))
-    vec[...] = dot(hidden, w_out[...]).astype(bf16)
-
     def place(query, carry):
         block = vec[pl.ds(pl.multiple_of(query * query_len, query_len), query_len), :]
         for j in range(mined_count):
@@ -131,7 +131,7 @@
             stage[goal_owner[query, j], pl.ds(first, query_len), :] = block
         return carry
 
-    lax.fori_loop(0, query_count, place, 0, unroll=4)
+    lax.fori_loop(0, query_count, place, 0, unroll=True)
     for owner in range(owner_count):
         send[owner * stride : owner * stride + rows, :] = stage[owner]
 
@@ -572,11 +572,12 @@
         sum_core_kernel(*refs, tail_rows=tail_rows, tail_count=hid // LANES + 1)
 
     (part,) = call(sum_core_body, [shape_of((half, LANES), bf16)], [place, keep, taken], 1)
-    parts = exchange(part.reshape(chip_count, share, LANES), "chip")
+    parts = exchange_rows(part, "chip", chip_count, 4).reshape(chip_count, share, LANES)
     (part,) = call(sum_kernel, [shape_of((dp_count, share, LANES), bf16)], [parts], 0)
-    parts = exchange(part, "dp")
+    part = part.reshape(dp_count * share, LANES)
+    parts = exchange_rows(part, "dp", dp_count, 4).reshape(dp_count, share, LANES)
     (part,) = call(sum_kernel, [shape_of((chip_count, share, LANES), bf16)], [parts], 0)
-    mine = exchange(part, "chip").reshape(half, LANES)
+    mine = exchange_rows(part.reshape(half, LANES), "chip", chip_count, 4)
     other = lax.ppermute(mine, "core", swap)
     grad_in, grad_bias, grad_out = call(
         unpack_kernel,

time: 151 us -> 151 us (level)
  no operation moved by 1% of the time
where the time goes in v8:
time: 151 us; the launch traced here: 150 us
  blocking collectives  80.5 us (53%)
  waiting for transfers between devices  25.4 us (17%)
  starting transfers between devices  24.3 us (16%)
  Pallas kernels  16.3 us (11%)
  local copies, waits for them, and re-layouts  2.94 us (2%)
    all_to_all x4, blocking collectives, exchange(): return lax.all_to_all(x, axis, split_axis=0, concat_axis=0, tiled=True)  80.5 us
    all_to_all x1, waiting for transfers between devices, exchange(): return lax.all_to_all(x, axis, split_axis=0, concat_axis=0, tiled=True)  23.8 us
    pallas_call x8, Pallas kernels, call(): pl.pallas_call(body, out_shape=tuple(outs), in_specs=[smem] * smem_count...  16.3 us
    all_to_all x1, starting transfers between devices, exchange(): return lax.all_to_all(x, axis, split_axis=0, concat_axis=0, tiled=True)  15 us
    ppermute x1, starting transfers between devices, local(): other = lax.ppermute(mine, 'core', swap)  5.95 us
    ppermute x1, starting transfers between devices, local(): taken = lax.ppermute(give, 'core', swap)  3.41 us
  transfers between devices with their start and end apart: 3, of which 3 were waited for; matrix products, arithmetic and copies ran while one was open for 0% of the time, Pallas kernels for 2%

profile of v8, /device:TPU:1, one launch (start us, length us, event | category | flops | bytes accessed | tf_op | source)
XLA Modules:
  0.0 150.4 jit_solution(14233446719055694412)
XLA Ops:
  0.6 3.1 %shard_map.120 = bf16[4224,128]{1,0:T(8,128)(2,1)} custom-call(s32[8,6]{1,0:T(8,128)} %mined_hbm.1, s32[512]{0:T(512)} %home_hbm.1, s32[8]{0:T(128)} %positive_hbm.1, bf16[256,512]{1,0:T(8,128)(2,1)} %bitcast.25, bf16[512,384]{1,0:T(8,128)(2,1)} %w_in.1, f32[384]{0:T(512)} %bias.1, bf16[384,128]{1,0:T(8,128)(2,1)} %refs_9_.1), custom_call_target="tpu_custom_call" | custom-call | flops 125829120 | bytes 1838816 | tf_op jit(solution)/shard_map/pallas_call | solution.py:48
  3.8 0.0 copy-start
  3.8 0.0 copy-start.1
  3.8 0.0 copy-start.2
  3.8 0.0 copy-start.3
  3.8 15.0 %all-to-all-start = ((bf16[64,33,2,128]{3,2,1,0:T(2,128)(2,1)}), bf16[64,33,2,128]{3,2,1,0:T(2,128)(2,1)S(1)}, u32[]{:S(2)}, u32[]{:S(2)}) async-start(bf16[64,33,2,128]{3,2,1,0:T(2,128)(2,1)} %bitcast.30), calls=%async_computation | async-start | bytes 2162688 | tf_op jit(solution)/shard_map/all_to_all | solution.py:448
  18.9 2.4 %shard_map.121 = (bf16[8,128,128]{2,1,0:T(8,128)(2,1)S(1)}, bf16[8,128,128]{2,1,0:T(8,128)(2,1)S(1)}, bf16[1280,384]{1,0:T(8,128)(2,1)S(1)}, f32[384,1280]{1,0:T(8,128)S(1)}, f32[8,384]{1,0:T(8,128)S(1)}) custom-call(bf16[1024,512]{1,0:T(8,128)(2,1)S(1)} %bitcast.28, bf16[256,512]{1,0:T(8,128)(2,1)S(1)} %bitcast.26, bf16[512,384]{1,0:T(8,128)(2,1)S(1)} %copy-done, ...), custom_call_target="tpu_custom_call" | custom-call | flops 629145600 | bytes 5289472 | tf_op jit(solution)/shard_map/pallas_call | solution.py:48
  21.3 1.3 copy-done.6
  22.6 1.0 copy-done.8
  23.6 0.1 pad_add_fusion.place.refs_0_
  23.7 23.8 %all-to-all-done = bf16[64,33,2,128]{3,2,1,0:T(2,128)(2,1)S(1)} async-done(((bf16[64,33,2,128]{3,2,1,0:T(2,128)(2,1)}), bf16[64,33,2,128]{3,2,1,0:T(2,128)(2,1)S(1)}, u32[]{:S(2)}, u32[]{:S(2)}) %all-to-all-start) | async-done | bytes 1081376 | tf_op jit(solution)/shard_map/all_to_all | solution.py:448
  47.4 3.9 %shard_map.122 = (bf16[4352,128]{1,0:T(8,128)(2,1)S(1)}, bf16[64,64,128]{2,1,0:T(8,128)(2,1)S(1)}, f32[8,128]{1,0:T(8,128)S(1)}) custom-call(s32[2]{0:T(128)S(1)} %pad_add_fusion.place.refs_0_, s32[512]{0:T(512)S(1)} %copy-done.5, bf16[4224,128]{1,0:T(8,128)(2,1)S(1)} %bitcast.16, bf16[8,128,128]{2,1,0:T(8,128)(2,1)S(1)} %get-tuple-element.19.line_vec, ...), custom_call_target="tpu_custom_call" | custom-call | flops 2147483648 | bytes 3786760 | tf_op jit(solution)/shard_map/pallas_call | solution.py:48
  51.3 35.7 %all_to_all.25 = bf16[64,17,4,128]{3,2,1,0:T(4,128)(2,1)S(1)} all-to-all(bf16[64,17,4,128]{3,2,1,0:T(4,128)(2,1)S(1)} %bitcast.15), channel_id=1, replica_groups=mesh['chip'=32,'core'=2,'dp'=8] {'chip','core'}, dimensions={0} | all-to-all | bytes 2228224 | tf_op jit(solution)/shard_map/all_to_all | solution.py:448
  87.0 4.5 %shard_map.123 = (f32[8,128]{1,0:T(8,128)S(1)}, f32[1024,128]{1,0:T(8,128)S(1)}, bf16[1024,128]{1,0:T(8,128)(2,1)S(1)}, f32[8,384]{1,0:T(8,128)S(1)}) custom-call(s32[2]{0:T(128)S(1)} %pad_add_fusion.place.refs_0_, bf16[4352,128]{1,0:T(8,128)(2,1)S(1)} %bitcast.14, bf16[4224,128]{1,0:T(8,128)(2,1)S(1)} %bitcast.17, ...), custom_call_target="tpu_custom_call" | custom-call | flops 3590324224 | bytes 8409096 | tf_op jit(solution)/shard_map/pallas_call | solution.py:48
  91.5 3.4 %collective-permute-start = (bf16[1024,128]{1,0:T(8,128)(2,1)S(1)}, bf16[1024,128]{1,0:T(8,128)(2,1)S(1)}, u32[]{:S(2)}, u32[]{:S(2)}) collective-permute-start(bf16[1024,128]{1,0:T(8,128)(2,1)S(1)} %get-tuple-element.29), channel_id=1, source_target_pairs={{0,8},{8,0},{1,9},{9,1},{2,10},{10,2},{3,11},{11,3},{4,12},{12,4},... | collective-permute-start | bytes 786440 | tf_op jit(solution)/shard_map/ppermute | solution.py:568
  94.9 1.1 collective-permute-done.refs_2_
  96.1 0.6 shard_map.124
  96.7 16.0 %all_to_all.26 = bf16[32,8,4,128]{3,2,1,0:T(4,128)(2,1)S(1)} all-to-all(bf16[32,8,4,128]{3,2,1,0:T(4,128)(2,1)S(1)} %bitcast.22), channel_id=1, replica_groups=mesh['chip'=32,'core'=2,'dp'=8] {'chip'}, dimensions={0} | all-to-all | bytes 524288 | tf_op jit(solution)/shard_map/all_to_all | solution.py:448
  112.7 13.8 %all_to_all.27 = bf16[8,8,4,128]{3,2,1,0:T(4,128)(2,1)S(1)} all-to-all(bf16[8,8,4,128]{3,2,1,0:T(4,128)(2,1)S(1)} %bitcast.23), channel_id=1, replica_groups=mesh['chip'=32,'core'=2,'dp'=8] {'dp'}, dimensions={0} | all-to-all | bytes 131072 | tf_op jit(solution)/shard_map/all_to_all | solution.py:448
  126.6 15.0 %all_to_all.28 = bf16[32,8,4,128]{3,2,1,0:T(4,128)(2,1)S(1)} all-to-all(bf16[32,8,4,128]{3,2,1,0:T(4,128)(2,1)S(1)} %bitcast.21), channel_id=1, replica_groups=mesh['chip'=32,'core'=2,'dp'=8] {'chip'}, dimensions={0} | all-to-all | bytes 524288 | tf_op jit(solution)/shard_map/all_to_all | solution.py:448
  141.5 6.0 %collective-permute-start.1 = (bf16[1024,128]{1,0:T(8,128)(2,1)S(1)}, bf16[1024,128]{1,0:T(8,128)(2,1)S(1)}, u32[]{:S(2)}, u32[]{:S(2)}) collective-permute-start(bf16[1024,128]{1,0:T(8,128)(2,1)S(1)} %bitcast.18), channel_id=1, source_target_pairs={{0,8},{8,0},{1,9},{9,1},{2,10},{10,2},{3,11},{11,3},{4,12},{12,4},... | collective-permute-start | bytes 786440 | tf_op jit(solution)/shard_map/ppermute | solution.py:581
  147.5 0.6 slice_reduce_fusion
  148.1 0.5 collective-permute-done.1.other
  148.6 1.7 %shard_map.127 = (f32[512,384]{1,0:T(8,128)}, f32[384]{0:T(512)}, f32[384,128]{1,0:T(8,128)}) custom-call(s32[2]{0:T(128)S(1)} %pad_add_fusion.place.refs_0_, bf16[1024,128]{1,0:T(8,128)(2,1)S(1)} %bitcast.19, bf16[1024,128]{1,0:T(8,128)(2,1)S(1)} %collective-permute-done.1.other, f32[8,384]{1,0:T(8,128)S(1)} %get-tuple-element.30.base_row), custom_call_target="tpu_custom_call" | custom-call | bytes 1521160 | tf_op jit(solution)/shard_map/pallas_call | solution.py:48
  (16 shorter events, 0.1 us)
Async XLA Ops:
  3.8 15.1 %copy-start = (bf16[512,384]{1,0:T(8,128)(2,1)S(1)}, bf16[512,384]{1,0:T(8,128)(2,1)}, u32[]{:S(2)}) copy-start(bf16[512,384]{1,0:T(8,128)(2,1)} %w_in.1) | copy-start | bytes 1179652
  3.8 15.1 %copy-start.1 = (bf16[8,32,512]{2,1,0:T(8,128)(2,1)S(1)}, bf16[8,32,512]{2,1,0:T(8,128)(2,1)}, u32[]{:S(2)}) copy-start(bf16[8,32,512]{2,1,0:T(8,128)(2,1)} %param.9) | copy-start | bytes 786436
  3.8 15.1 %copy-start.2 = (bf16[384,128]{1,0:T(8,128)(2,1)S(1)}, bf16[384,128]{1,0:T(8,128)(2,1)}, u32[]{:S(2)}) copy-start(bf16[384,128]{1,0:T(8,128)(2,1)} %refs_9_.1) | copy-start | bytes 294916
  3.8 15.0 %copy-start.3 = (f32[384]{0:T(512)S(1)}, f32[384]{0:T(512)}, u32[]{:S(2)}) copy-start(f32[384]{0:T(512)} %bias.1) | copy-start | bytes 4612
  3.8 15.0 %copy-start.4 = (bf16[8,128,512]{2,1,0:T(8,128)(2,1)S(1)}, bf16[8,128,512]{2,1,0:T(8,128)(2,1)}, u32[]{:S(2)}) copy-start(bf16[8,128,512]{2,1,0:T(8,128)(2,1)} %param.10) | copy-start | bytes 3145732
  3.8 43.6 %all-to-all-start = ((bf16[64,33,2,128]{3,2,1,0:T(2,128)(2,1)}), bf16[64,33,2,128]{3,2,1,0:T(2,128)(2,1)S(1)}, u32[]{:S(2)}, u32[]{:S(2)}) async-start(bf16[64,33,2,128]{3,2,1,0:T(2,128)(2,1)} %bitcast.30), calls=%async_computation | async-start | bytes 2162688 | tf_op jit(solution)/shard_map/all_to_all | solution.py:448
  18.9 28.6 %copy-start.5 = (s32[512]{0:T(512)S(1)}, s32[512]{0:T(512)}, u32[]{:S(2)}) copy-start(s32[512]{0:T(512)} %counts.1) | copy-start | bytes 6148
  21.3 1.3 copy-start.6
  22.6 1.0 copy-start.8
  47.4 39.6 %copy-start.9 = (bf16[1280,384]{1,0:T(8,128)(2,1)S(1)}, bf16[1280,384]{1,0:T(8,128)(2,1)}, u32[]{:S(2)}) copy-start(bf16[1280,384]{1,0:T(8,128)(2,1)} %copy-done.8) | copy-start | bytes 2949124
  51.3 35.7 %copy-start.7 = (f32[384,1280]{1,0:T(8,128)S(1)}, f32[384,1280]{1,0:T(8,128)}, u32[]{:S(2)}) copy-start(f32[384,1280]{1,0:T(8,128)} %copy-done.6) | copy-start | bytes 5898244
  91.5 4.6 %collective-permute-start = (bf16[1024,128]{1,0:T(8,128)(2,1)S(1)}, bf16[1024,128]{1,0:T(8,128)(2,1)S(1)}, u32[]{:S(2)}, u32[]{:S(2)}) collective-permute-start(bf16[1024,128]{1,0:T(8,128)(2,1)S(1)} %get-tuple-element.29), channel_id=1, source_target_pairs={{0,8},{8,0},{1,9},{9,1},{2,10},{10,2},{3,11},{11,3},{4,12},{12,4},... | collective-permute-start | bytes 786440 | tf_op jit(solution)/shard_map/ppermute | solution.py:568
  141.5 7.1 %collective-permute-start.1 = (bf16[1024,128]{1,0:T(8,128)(2,1)S(1)}, bf16[1024,128]{1,0:T(8,128)(2,1)S(1)}, u32[]{:S(2)}, u32[]{:S(2)}) collective-permute-start(bf16[1024,128]{1,0:T(8,128)(2,1)S(1)} %bitcast.18), channel_id=1, source_target_pairs={{0,8},{8,0},{1,9},{9,1},{2,10},{10,2},{3,11},{11,3},{4,12},{12,4},... | collective-permute-start | bytes 786440 | tf_op jit(solution)/shard_map/ppermute | solution.py:581
